TPU v7x, 128 devices: a whole 4x4x4 slice. The times are simulated.
128 devices in a mesh: fsdp: 16 (over x_hi, z, core), seq: 8 (over y, x_lo).
Axes of the slice: x: 4 (x_hi: 2, x_lo: 2; x = x_hi * 2 + x_lo), y: 4, z: 4, core: 2. Of those that a mesh axis runs over, the one named last changes fastest.
Arguments:
- tokens: bfloat16 [16, 1024, 768], P('fsdp', 'seq'), may hold values from -6 to 6
- doc_lengths: int32 [16, 4], P('fsdp'), may hold values from 1 to 896, as said below
- attn_gain: bfloat16 [768], P(('fsdp', 'seq')), may hold values from 0.5 to 1.5
- w_query: bfloat16 [768, 768], P(('fsdp', 'seq')), may hold values from -0.21875 to 0.21875
- w_key: bfloat16 [768, 768], P(('fsdp', 'seq')), may hold values from -0.21875 to 0.21875
- w_value: bfloat16 [768, 768], P(('fsdp', 'seq')), may hold values from -0.21875 to 0.21875
- w_out: bfloat16 [768, 768], P(('fsdp', 'seq')), may hold values from -1.75 to 1.75
- mlp_gain: bfloat16 [768], P(('fsdp', 'seq')), may hold values from 0.5 to 1.5
- w_gate: bfloat16 [768, 3072], P(('fsdp', 'seq')), may hold values from -0.21875 to 0.21875
- w_up: bfloat16 [768, 3072], P(('fsdp', 'seq')), may hold values from -0.21875 to 0.21875
- w_down: bfloat16 [3072, 768], P(('fsdp', 'seq')), may hold values from -0.109375 to 0.109375
- cotangent: bfloat16 [16, 1024, 768], P('fsdp', 'seq'), may hold values from -6 to 6
Outputs:
- layer_out: bfloat16 [16, 1024, 768], P('fsdp', 'seq')
- input_grad: float32 [16, 1024, 768], P('fsdp', 'seq')
- grad_attn_gain: float32 [768], P(('fsdp', 'seq'))
- grad_w_query: float32 [768, 768], P(('fsdp', 'seq'))
- grad_w_key: float32 [768, 768], P(('fsdp', 'seq'))
- grad_w_value: float32 [768, 768], P(('fsdp', 'seq'))
- grad_w_out: float32 [768, 768], P(('fsdp', 'seq'))
- grad_mlp_gain: float32 [768], P(('fsdp', 'seq'))
- grad_w_gate: float32 [768, 3072], P(('fsdp', 'seq'))
- grad_w_up: float32 [768, 3072], P(('fsdp', 'seq'))
- grad_w_down: float32 [3072, 768], P(('fsdp', 'seq'))
Inputs may be any that keep to these rules, and one draw needn't show every extreme that they name: `doc_lengths`: in each pack the lengths sum to 1024; exactly one document has 896 positions, and it is neither the first nor the last; the others together have 128.
All inputs are finite; a program needn't handle non-finite values.
Results may differ from a plain program's by a relative error of at most 0.019.
Values may be sent and summed in bfloat16 or wider, within the bound.
A program may use at most 192 MiB of HBM per device.

v0:
```python
import math

import jax
import jax.numpy as jnp
from jax import lax
from jax.sharding import PartitionSpec as P

HEADS = 12
KV_HEADS = 12
HEAD_DIM = 64


EPSILON = 1e-05
ROPE_BASE = 10000.0
MASKED_SCORE = -1e30


def rms_norm(values, gain):
    factor = lax.rsqrt(jnp.mean(values * values, axis=-1, keepdims=True) + EPSILON)
    return values * factor * gain


def rotate(values, position, head_count):
    half_dim = HEAD_DIM // 2
    freqs = ROPE_BASE ** (-(2.0 * jnp.arange(half_dim, dtype=jnp.float32)) / HEAD_DIM)
    angles = position.astype(jnp.float32)[:, None] * freqs[None, :]
    cosine = jnp.cos(angles)[:, None, :]
    sine = jnp.sin(angles)[:, None, :]
    shaped = values.reshape(values.shape[0], head_count, HEAD_DIM)
    first_half = shaped[..., :half_dim]
    second_half = shaped[..., half_dim:]
    turned = jnp.concatenate(
        [first_half * cosine - second_half * sine, second_half * cosine + first_half * sine],
        axis=-1,
    )
    return turned.reshape(values.shape[0], head_count * HEAD_DIM)


def rotate_back(gradient, position, head_count):

    def turn(values):
        return rotate(values, position, head_count)

    pullback = jax.vjp(turn, gradient)[1]
    return pullback(gradient)[0]


def doc_layout(lengths, pack_len):
    ends = jnp.cumsum(lengths)
    where_pos = jnp.arange(pack_len, dtype=jnp.int32)
    passed = where_pos[:, None] >= ends[None, :]
    segment = jnp.sum(passed.astype(jnp.int32), axis=1)
    start_pos = jnp.sum(jnp.where(passed, lengths[None, :], 0), axis=1)
    return (segment, where_pos - start_pos)


def product(form, left, right):
    return jnp.einsum(form, left, right, preferred_element_type=jnp.float32)


def probabilities(query_heads, key_heads, segment_mine, segment_all, query_index):
    scores = product("qhgd,khd->hgqk", query_heads, key_heads) * (1.0 / math.sqrt(HEAD_DIM))
    key_index = jnp.arange(key_heads.shape[0], dtype=jnp.int32)
    allowed = (segment_mine[:, None] == segment_all[None, :]) & (
        key_index[None, :] <= query_index[:, None]
    )
    scores = jnp.where(allowed[None, None], scores, MASKED_SCORE)
    return jax.nn.softmax(scores, axis=-1)


def per_device(
    tokens,
    doc_lengths,
    attn_gain,
    w_query,
    w_key,
    w_value,
    w_out,
    mlp_gain,
    w_gate,
    w_up,
    w_down,
    cotangent,
):
    tok_rows = tokens.shape[1]
    seq_count = lax.axis_size("seq")
    seq_place = lax.axis_index("seq")
    pack_len = tok_rows * seq_count
    group_size = HEADS // KV_HEADS
    scale_value = 1.0 / math.sqrt(HEAD_DIM)
    first_row = seq_place * tok_rows
    segment_all, position_all = doc_layout(doc_lengths[0], pack_len)
    segment_mine = lax.dynamic_slice_in_dim(segment_all, first_row, tok_rows)
    position_mine = lax.dynamic_slice_in_dim(position_all, first_row, tok_rows)
    query_index = first_row + jnp.arange(tok_rows, dtype=jnp.int32)
    inputs = tokens[0].astype(jnp.float32)
    attn_set = (
        lax.all_gather(attn_gain, ("fsdp", "seq"), axis=0, tiled=True),
        lax.all_gather(w_query, ("fsdp", "seq"), axis=0, tiled=True),
        lax.all_gather(w_key, ("fsdp", "seq"), axis=0, tiled=True),
        lax.all_gather(w_value, ("fsdp", "seq"), axis=0, tiled=True),
        lax.all_gather(w_out, ("fsdp", "seq"), axis=0, tiled=True),
    )
    gain_one, full_query, full_key, full_value, full_out = attn_set
    gain_one = gain_one.astype(jnp.float32)
    normed = rms_norm(inputs, gain_one).astype(jnp.bfloat16)
    query_raw = product("td,de->te", normed, full_query)
    key_raw = product("td,de->te", normed, full_key)
    value_raw = product("td,de->te", normed, full_value)
    queries = rotate(query_raw, position_mine, HEADS).astype(jnp.bfloat16)
    key_rows = rotate(key_raw, position_mine, KV_HEADS).astype(jnp.bfloat16)
    value_rows = value_raw.astype(jnp.bfloat16)
    keys_all, values_all = (
        lax.all_gather(key_rows, "seq", axis=0, tiled=True),
        lax.all_gather(value_rows, "seq", axis=0, tiled=True),
    )
    query_heads = queries.reshape(tok_rows, KV_HEADS, group_size, HEAD_DIM)
    key_heads = keys_all.reshape(pack_len, KV_HEADS, HEAD_DIM)
    value_heads = values_all.reshape(pack_len, KV_HEADS, HEAD_DIM)
    probs_low = probabilities(
        query_heads, key_heads, segment_mine, segment_all, query_index
    ).astype(jnp.bfloat16)
    attended = (
        product("hgqk,khd->qhgd", probs_low, value_heads)
        .reshape(tok_rows, HEADS * HEAD_DIM)
        .astype(jnp.bfloat16)
    )
    hidden = inputs + product("td,de->te", attended, full_out)
    mlp_set = (
        lax.all_gather(mlp_gain, ("fsdp", "seq"), axis=0, tiled=True),
        lax.all_gather(w_gate, ("fsdp", "seq"), axis=0, tiled=True),
        lax.all_gather(w_up, ("fsdp", "seq"), axis=0, tiled=True),
        lax.all_gather(w_down, ("fsdp", "seq"), axis=0, tiled=True),
    )
    gain_two, full_gate, full_up, full_down = mlp_set
    gain_two = gain_two.astype(jnp.float32)
    normed_two = rms_norm(hidden, gain_two).astype(jnp.bfloat16)
    gate_raw = product("td,df->tf", normed_two, full_gate)
    up_raw = product("td,df->tf", normed_two, full_up)

    def gated(gate_values, up_values):
        return jax.nn.silu(gate_values) * up_values

    mixed = gated(gate_raw, up_raw).astype(jnp.bfloat16)
    layer_out = (hidden + product("tf,fd->td", mixed, full_down)).astype(jnp.bfloat16)
    attn_set = (
        lax.all_gather(attn_gain, ("fsdp", "seq"), axis=0, tiled=True),
        lax.all_gather(w_query, ("fsdp", "seq"), axis=0, tiled=True),
        lax.all_gather(w_key, ("fsdp", "seq"), axis=0, tiled=True),
        lax.all_gather(w_value, ("fsdp", "seq"), axis=0, tiled=True),
        lax.all_gather(w_out, ("fsdp", "seq"), axis=0, tiled=True),
    )
    mlp_set = (
        lax.all_gather(mlp_gain, ("fsdp", "seq"), axis=0, tiled=True),
        lax.all_gather(w_gate, ("fsdp", "seq"), axis=0, tiled=True),
        lax.all_gather(w_up, ("fsdp", "seq"), axis=0, tiled=True),
        lax.all_gather(w_down, ("fsdp", "seq"), axis=0, tiled=True),
    )
    gain_one, full_query, full_key, full_value, full_out = attn_set
    gain_two, full_gate, full_up, full_down = mlp_set
    gain_one = gain_one.astype(jnp.float32)
    gain_two = gain_two.astype(jnp.float32)
    upstream = cotangent[0]
    d_mixed = product("td,fd->tf", upstream, full_down)
    d_gate, d_up = jax.vjp(gated, gate_raw, up_raw)[1](d_mixed)
    d_gate = d_gate.astype(jnp.bfloat16)
    d_up = d_up.astype(jnp.bfloat16)
    d_normed_two = product("tf,df->td", d_gate, full_gate) + product("tf,df->td", d_up, full_up)
    d_hidden_norm, grad_gain_two = jax.vjp(rms_norm, hidden, gain_two)[1](d_normed_two)
    grad_down = product("tf,td->fd", mixed, upstream)
    grad_gate = product("td,tf->df", normed_two, d_gate)
    grad_up = product("td,tf->df", normed_two, d_up)
    mlp_grads = (
        lax.psum_scatter(grad_gain_two, ("fsdp", "seq"), scatter_dimension=0, tiled=True),
        lax.psum_scatter(grad_gate, ("fsdp", "seq"), scatter_dimension=0, tiled=True),
        lax.psum_scatter(grad_up, ("fsdp", "seq"), scatter_dimension=0, tiled=True),
        lax.psum_scatter(grad_down, ("fsdp", "seq"), scatter_dimension=0, tiled=True),
    )
    owned_gain_two = mlp_grads[0]
    mlp_weight_grads = (mlp_grads[1], mlp_grads[2], mlp_grads[3])
    d_hidden = upstream.astype(jnp.float32) + d_hidden_norm
    d_hidden_low = d_hidden.astype(jnp.bfloat16)
    d_attended = product("te,de->td", d_hidden_low, full_out).astype(jnp.bfloat16)
    d_attended_heads = d_attended.reshape(tok_rows, KV_HEADS, group_size, HEAD_DIM)
    probs_again = probabilities(query_heads, key_heads, segment_mine, segment_all, query_index)
    d_probs = product("qhgd,khd->hgqk", d_attended_heads, value_heads)
    d_scores = (
        probs_again * (d_probs - jnp.sum(probs_again * d_probs, axis=-1, keepdims=True))
    ).astype(jnp.bfloat16)
    again_low = probs_again.astype(jnp.bfloat16)
    d_queries = (product("hgqk,khd->qhgd", d_scores, key_heads) * scale_value).reshape(
        tok_rows, HEADS * HEAD_DIM
    )
    d_keys_part = (product("hgqk,qhgd->khd", d_scores, query_heads) * scale_value).reshape(
        pack_len, KV_HEADS * HEAD_DIM
    )
    d_values_part = product("hgqk,qhgd->khd", again_low, d_attended_heads).reshape(
        pack_len, KV_HEADS * HEAD_DIM
    )
    d_keys, d_values = (
        lax.psum_scatter(
            d_keys_part.astype(jnp.bfloat16), "seq", scatter_dimension=0, tiled=True
        ).astype(jnp.float32),
        lax.psum_scatter(
            d_values_part.astype(jnp.bfloat16), "seq", scatter_dimension=0, tiled=True
        ).astype(jnp.float32),
    )
    d_query_raw = rotate_back(d_queries, position_mine, HEADS).astype(jnp.bfloat16)
    d_key_raw = rotate_back(d_keys, position_mine, KV_HEADS).astype(jnp.bfloat16)
    d_value_raw = d_values.astype(jnp.bfloat16)
    d_normed = (
        product("te,de->td", d_query_raw, full_query)
        + product("te,de->td", d_key_raw, full_key)
        + product("te,de->td", d_value_raw, full_value)
    )
    d_inputs_norm, grad_gain_one = jax.vjp(rms_norm, inputs, gain_one)[1](d_normed)
    input_grad = d_hidden + d_inputs_norm
    grad_out = product("td,te->de", attended, d_hidden_low)
    grad_query = product("td,te->de", normed, d_query_raw)
    grad_key = product("td,te->de", normed, d_key_raw)
    grad_value = product("td,te->de", normed, d_value_raw)
    attn_grads = (
        lax.psum_scatter(grad_gain_one, ("fsdp", "seq"), scatter_dimension=0, tiled=True),
        lax.psum_scatter(grad_query, ("fsdp", "seq"), scatter_dimension=0, tiled=True),
        lax.psum_scatter(grad_key, ("fsdp", "seq"), scatter_dimension=0, tiled=True),
        lax.psum_scatter(grad_value, ("fsdp", "seq"), scatter_dimension=0, tiled=True),
        lax.psum_scatter(grad_out, ("fsdp", "seq"), scatter_dimension=0, tiled=True),
    )
    return (
        layer_out[None],
        input_grad[None],
        attn_grads[0],
        attn_grads[1],
        attn_grads[2],
        attn_grads[3],
        attn_grads[4],
        owned_gain_two,
        mlp_weight_grads[0],
        mlp_weight_grads[1],
        mlp_weight_grads[2],
    )


def solution(mesh):
    placed = (
        P("fsdp", "seq", None),
        P("fsdp", None),
        P(("fsdp", "seq")),
        P(("fsdp", "seq"), None),
        P(("fsdp", "seq"), None),
        P(("fsdp", "seq"), None),
        P(("fsdp", "seq"), None),
        P(("fsdp", "seq")),
        P(("fsdp", "seq"), None),
        P(("fsdp", "seq"), None),
        P(("fsdp", "seq"), None),
        P("fsdp", "seq", None),
    )
    return jax.shard_map(
        per_device,
        mesh=mesh,
        in_specs=placed,
        out_specs=(
            P("fsdp", "seq", None),
            P("fsdp", "seq", None),
            P(("fsdp", "seq")),
            P(("fsdp", "seq"), None),
            P(("fsdp", "seq"), None),
            P(("fsdp", "seq"), None),
            P(("fsdp", "seq"), None),
            P(("fsdp", "seq")),
            P(("fsdp", "seq"), None),
            P(("fsdp", "seq"), None),
            P(("fsdp", "seq"), None),
        ),
        check_vma=False,
    )
```

profile of v0, /device:TPU:1, one launch (start us, length us, event | category | flops | bytes accessed | tf_op | source)
XLA Modules:
  0.0 4159.3 jit_solution(5772659999769229417)
XLA Ops:
  11.7 68.7 %all-reduce.21 = (bf16[768]{0:T(1024)(128)(2,1)S(1)}, bf16[768]{0:T(1024)(128)(2,1)S(1)}) all-reduce(bf16[768]{0:T(1024)(128)(2,1)S(1)} %dynamic-update-slice, bf16[768]{0:T(1024)(128)(2,1)S(1)} %dynamic-update-slice.1), channel_id=1, replica_groups=mesh['fsdp'=16,'seq'=8] {'fsdp','seq'}, use_global_device_ids=true, to_apply=%add.4 | all-reduce | flops 1536 | bytes 6144
  81.6 230.7 %all-gather.22.cloned.1.call-done = bf16[128,6,768]{2,1,0:T(8,128)(2,1)} async-done(((bf16[1,6,768]{2,1,0:T(8,128)(2,1)}), bf16[128,6,768]{2,1,0:T(8,128)(2,1)}) %all-gather.22.cloned.1.call-update) | async-done | bytes 1179664 | tf_op jit(solution)/shard_map/all_gather | solution.py:101
  316.3 296.3 %all-gather.26.cloned.1.call-done = bf16[128,6,768]{2,1,0:T(8,128)(2,1)} async-done(((bf16[1,6,768]{2,1,0:T(8,128)(2,1)}), bf16[128,6,768]{2,1,0:T(8,128)(2,1)}) %all-gather.26.cloned.1.call-update) | async-done | bytes 1179664 | tf_op jit(solution)/shard_map/all_gather | solution.py:99
  616.5 296.6 %all-gather.24.cloned.1.call-done = bf16[128,6,768]{2,1,0:T(8,128)(2,1)} async-done(((bf16[1,6,768]{2,1,0:T(8,128)(2,1)}), bf16[128,6,768]{2,1,0:T(8,128)(2,1)}) %all-gather.24.cloned.1.call-update) | async-done | bytes 1179664 | tf_op jit(solution)/shard_map/all_gather | solution.py:100
  924.1 288.6 %all-gather.28.cloned.1.call-done = bf16[128,6,768]{2,1,0:T(8,128)(2,1)} async-done(((bf16[1,6,768]{2,1,0:T(8,128)(2,1)}), bf16[128,6,768]{2,1,0:T(8,128)(2,1)}) %all-gather.28.cloned.1.call-update) | async-done | bytes 1179664 | tf_op jit(solution)/shard_map/all_gather | solution.py:102
  1215.0 41.1 all-gather.16.cloned.1.call-done
  1257.8 43.4 %all-gather.18.cloned.1.call-done = bf16[1024,768]{0,1:T(8,128)(2,1)} async-done(((bf16[128,768]{0,1:T(8,128)(2,1)}), bf16[1024,768]{0,1:T(8,128)(2,1)}) %all-gather.18.cloned.1.call-update) | async-done | bytes 1572880 | tf_op jit(solution)/shard_map/all_gather | solution.py:114
  1309.5 309.8 %all-gather.30.cloned.1.call-done = bf16[128,6,3072]{2,1,0:T(8,128)(2,1)} async-done(((bf16[1,6,3072]{2,1,0:T(8,128)(2,1)}), bf16[128,6,3072]{2,1,0:T(8,128)(2,1)}) %all-gather.30.cloned.1.call-update) | async-done | bytes 4718608 | tf_op jit(solution)/shard_map/all_gather | solution.py:131
  1619.3 7.8 reshape.344
  1627.1 306.4 %all-gather.32.cloned.1.call-done = bf16[128,6,3072]{2,1,0:T(8,128)(2,1)} async-done(((bf16[1,6,3072]{2,1,0:T(8,128)(2,1)}), bf16[128,6,3072]{2,1,0:T(8,128)(2,1)}) %all-gather.32.cloned.1.call-update) | async-done | bytes 4718608 | tf_op jit(solution)/shard_map/all_gather | solution.py:132
  1933.4 8.2 reshape.346
  1948.1 296.0 %all-gather.20.cloned.1.call-done = bf16[3072,768]{1,0:T(8,128)(2,1)} async-done(((bf16[24,768]{1,0:T(8,128)(2,1)}), bf16[3072,768]{1,0:T(8,128)(2,1)}) %all-gather.20.cloned.1.call-update) | async-done | bytes 4718608 | tf_op jit(solution)/shard_map/all_gather | solution.py:133
  2303.3 12.2 reduce-scatter.22.cloned.1.call-done
  2320.8 40.4 reduce-scatter.24.cloned.1.call-done
  2364.2 1011.2 %fusion.76 = (f32[8,768]{1,0:T(8,128)S(1)}, f32[8,768]{1,0:T(8,128)S(1)}, f32[8,768]{1,0:T(8,128)S(1)}, f32[8,768]{1,0:T(8,128)S(1)}, f32[8,3072]{1,0:T(8,128)S(1)}, /*index=5*/f32[8,3072]{1,0:T(8,128)S(1)}) fusion(f32[768,768]{1,0:T(8,128)} %fusion.57, f32[768,768]{1,0:T(8,128)} %fusion.55, f32[768,768]{1,0:T(8,128)} %fusion.63, f32[768,768]{1,0:T(8,128)} %fusion.60, ...), kind=kCustom, calls=%all-reduce-scatter.6 | all-reduce-scatter fusion | flops 9437185 | bytes 28606464
  3375.5 7.2 collective-permute-start.31
  3399.5 7.2 collective-permute-start.27
  3845.0 63.6 %all-reduce.20 = (f32[768]{0:T(1024)S(1)}, f32[768]{0:T(1024)S(1)}) all-reduce(f32[768]{0:T(1024)S(1)} %get-tuple-element.13, f32[768]{0:T(1024)} %get-tuple-element.11), channel_id=4, replica_groups=mesh['fsdp'=16,'seq'=8] {'fsdp','seq'}, use_global_device_ids=true, to_apply=%region_13.14.clone | all-reduce | flops 1536 | bytes 12288
  3914.3 25.7 concatenate.11
  3940.1 26.5 concatenate.12
  3966.5 27.9 concatenate.13
  4012.6 7.3 collective-permute-start.174
  4061.4 33.3 concatenate.14
  4094.7 55.1 %concatenate.15 = f32[262,3072]{1,0:T(8,128)} concatenate(f32[6,3072]{1,0:T(8,128)S(1)} %copy-done.44, f32[8,3072]{1,0:T(8,128)} %copy-done.70, f32[8,3072]{1,0:T(8,128)} %copy-done.73, f32[8,3072]{1,0:T(8,128)} %copy-done.74, f32[8,3072]{1,0:T(8,128)} %copy-done.75, f32[8,3072]{1,0:T(8,128)} %copy-done.76, f32[8,3072]{1,0:T(8,128)} %copy-done.77, ...), dimensions={0} | concatenate | bytes 6438912
  (850 shorter events, 628.8 us)
Async XLA Ops:
  7.2 305.1 %all-gather.22.cloned.1.call-start = ((), (), s32[]{:S(2)}) async-start(), calls=%async_computation.7 | async-start | bytes 1585152 | tf_op jit(solution)/shard_map/all_gather | solution.py:101
  7.9 604.8 %all-gather.26.cloned.1.call-start = ((), (), s32[]{:S(2)}) async-start(), calls=%async_computation.9 | async-start | bytes 1585152 | tf_op jit(solution)/shard_map/all_gather | solution.py:99
  8.7 904.4 %all-gather.24.cloned.1.call-start = ((), (), s32[]{:S(2)}) async-start(), calls=%async_computation.8 | async-start | bytes 1585152 | tf_op jit(solution)/shard_map/all_gather | solution.py:100
  9.4 1203.2 %all-gather.28.cloned.1.call-start = ((), (), s32[]{:S(2)}) async-start(), calls=%async_computation.10 | async-start | bytes 1585152 | tf_op jit(solution)/shard_map/all_gather | solution.py:102
  10.0 1246.1 %all-gather.16.cloned.1.call-start = ((), (), s32[]{:S(2)}) async-start(), calls=%async_computation.3 | async-start | bytes 1769472 | tf_op jit(solution)/shard_map/all_gather | solution.py:115
  315.7 985.5 %all-gather.18.cloned.1.call-start = ((), (), s32[]{:S(2)}) async-start(), calls=%async_computation.4 | async-start | bytes 1769472 | tf_op jit(solution)/shard_map/all_gather | solution.py:114
  921.5 697.8 %all-gather.30.cloned.1.call-start = ((), (), s32[]{:S(2)}) async-start(), calls=%async_computation.11 | async-start | bytes 6340608 | tf_op jit(solution)/shard_map/all_gather | solution.py:131
  922.2 1011.2 %all-gather.32.cloned.1.call-start = ((), (), s32[]{:S(2)}) async-start(), calls=%async_computation.12 | async-start | bytes 6340608 | tf_op jit(solution)/shard_map/all_gather | solution.py:132
  923.0 1321.1 %all-gather.20.cloned.1.call-start = ((), (), s32[]{:S(2)}) async-start(), calls=%async_computation.5 | async-start | bytes 4755456 | tf_op jit(solution)/shard_map/all_gather | solution.py:133
  923.7 1391.8 %reduce-scatter.22.cloned.1.call-start = ((), (), s32[]{:S(2)}) async-start(), calls=%async_computation.13 | async-start | bytes 1769472
  2273.6 87.6 %reduce-scatter.24.cloned.1.call-start = ((), (), s32[]{:S(2)}) async-start(), calls=%async_computation.14 | async-start | bytes 1769472
  2282.5 1869.5 %reduce-scatter.20.cloned.1.call-start = ((), (), s32[]{:S(2)}) async-start(), calls=%async_computation.6 | async-start | bytes 9510912 | tf_op jit(solution)/shard_map/reduce_scatter | solution.py:177
  3699.3 35.7 collective-permute-start.158
  3700.9 35.4 collective-permute-start.157
  3828.7 165.8 %collective-permute-start.184 = (f32[8,3072]{1,0:T(8,128)S(1)}, f32[8,3072]{1,0:T(8,128)}, u32[]{:S(2)}, u32[]{:S(2)}) collective-permute-start(f32[8,3072]{1,0:T(8,128)S(1)} %get-tuple-element.32), channel_id=1, source_target_pairs={{0,25},{1,26},{2,27},{3,28},{4,29},{5,30},{6,31},{7,32},{8,33},{9,... | collective-permute-start | bytes 294920
  3832.0 165.0 %collective-permute-start.183 = (f32[8,3072]{1,0:T(8,128)S(1)}, f32[8,3072]{1,0:T(8,128)}, u32[]{:S(2)}, u32[]{:S(2)}) collective-permute-start(f32[8,3072]{1,0:T(8,128)S(1)} %get-tuple-element.32), channel_id=1, source_target_pairs={{0,24},{1,25},{2,26},{3,27},{4,28},{5,29},{6,30},{7,31},{8,32},{9,... | collective-permute-start | bytes 294920
  3834.0 166.5 %collective-permute-start.182 = (f32[8,3072]{1,0:T(8,128)S(1)}, f32[8,3072]{1,0:T(8,128)}, u32[]{:S(2)}, u32[]{:S(2)}) collective-permute-start(f32[8,3072]{1,0:T(8,128)S(1)} %get-tuple-element.32), channel_id=1, source_target_pairs={{0,23},{1,24},{2,25},{3,26},{4,27},{5,28},{6,29},{7,30},{8,31},{9,... | collective-permute-start | bytes 294920
  3835.9 169.8 %collective-permute-start.181 = (f32[8,3072]{1,0:T(8,128)S(1)}, f32[8,3072]{1,0:T(8,128)}, u32[]{:S(2)}, u32[]{:S(2)}) collective-permute-start(f32[8,3072]{1,0:T(8,128)S(1)} %get-tuple-element.32), channel_id=1, source_target_pairs={{0,22},{1,23},{2,24},{3,25},{4,26},{5,27},{6,28},{7,29},{8,30},{9,... | collective-permute-start | bytes 294920
  3839.1 171.5 %collective-permute-start.180 = (f32[8,3072]{1,0:T(8,128)S(1)}, f32[8,3072]{1,0:T(8,128)}, u32[]{:S(2)}, u32[]{:S(2)}) collective-permute-start(f32[8,3072]{1,0:T(8,128)S(1)} %get-tuple-element.32), channel_id=1, source_target_pairs={{0,21},{1,22},{2,23},{3,24},{4,25},{5,26},{6,27},{7,28},{8,29},{9,... | collective-permute-start | bytes 294920
  4045.8 48.9 %collective-permute-start.164 = (f32[8,3072]{1,0:T(8,128)S(1)}, f32[8,3072]{1,0:T(8,128)}, u32[]{:S(2)}, u32[]{:S(2)}) collective-permute-start(f32[8,3072]{1,0:T(8,128)S(1)} %get-tuple-element.32), channel_id=1, source_target_pairs={{0,5},{1,6},{2,7},{3,8},{4,9},{5,10},{6,11},{7,12},{8,13},{9,14},{... | collective-permute-start | bytes 294920
  4048.5 46.1 %collective-permute-start.163 = (f32[8,3072]{1,0:T(8,128)S(1)}, f32[8,3072]{1,0:T(8,128)}, u32[]{:S(2)}, u32[]{:S(2)}) collective-permute-start(f32[8,3072]{1,0:T(8,128)S(1)} %get-tuple-element.32), channel_id=1, source_target_pairs={{0,4},{1,5},{2,6},{3,7},{4,8},{5,9},{6,10},{7,11},{8,12},{9,13},{1... | collective-permute-start | bytes 294920
  4052.8 41.9 %collective-permute-start.162 = (f32[8,3072]{1,0:T(8,128)S(1)}, f32[8,3072]{1,0:T(8,128)}, u32[]{:S(2)}, u32[]{:S(2)}) collective-permute-start(f32[8,3072]{1,0:T(8,128)S(1)} %get-tuple-element.32), channel_id=1, source_target_pairs={{0,3},{1,4},{2,5},{3,6},{4,7},{5,8},{6,9},{7,10},{8,11},{9,12},{10... | collective-permute-start | bytes 294920
  4054.8 39.9 collective-permute-start.161
  4057.3 37.4 collective-permute-start.160
  (360 other events, 30315.3 us)
Sparse Core Ops, SparseCore 0:
  9.7 302.5 all-gather.21
  314.0 298.6 all-gather.25
  614.4 298.6 all-gather.23
  914.7 297.9 all-gather.27
  1214.7 41.3 all-gather.15
  1258.1 43.1 all-gather.17
  1302.9 316.2 all-gather.29
  1621.0 312.4 all-gather.31
  1935.1 308.9 all-gather.19
  2273.8 41.7 reduce-scatter.21
  2317.9 43.2 reduce-scatter.23
  2364.1 654.0 reduce-scatter.19
where the time goes:
time: 4180 us; the launch traced here: 4160 us
  waiting for transfers between devices  2180 us (52%)
  blocking collectives  1140 us (27%)
  starting transfers between devices  510 us (12%)
  local copies, waits for them, and re-layouts  219 us (5%)
  matrix products  80 us (2%)
    unnamed x3, blocking collectives  1140 us
    unnamed x194, starting transfers between devices  510 us
    all_gather x1, waiting for transfers between devices, per_device(): lax.all_gather(w_gate, ('fsdp', 'seq'), axis=0, tiled=True)  310 us
    all_gather x1, waiting for transfers between devices, per_device(): lax.all_gather(w_up, ('fsdp', 'seq'), axis=0, tiled=True)  306 us
    all_gather x1, waiting for transfers between devices, per_device(): lax.all_gather(w_key, ('fsdp', 'seq'), axis=0, tiled=True)  297 us
    all_gather x1, waiting for transfers between devices, per_device(): lax.all_gather(w_query, ('fsdp', 'seq'), axis=0, tiled=True)  296 us
    all_gather x1, waiting for transfers between devices, per_device(): lax.all_gather(w_down, ('fsdp', 'seq'), axis=0, tiled=True)  296 us
    all_gather x1, waiting for transfers between devices, per_device(): lax.all_gather(w_out, ('fsdp', 'seq'), axis=0, tiled=True)  289 us
  transfers between devices with their start and end apart: 204, of which 14 were waited for; matrix products, arithmetic and copies ran while one was open for 31% of the time, Pallas kernels for 0%

commit v1 on v0

v1 whole, which is shorter than its diff:
```python
import functools
import math

import jax
import jax.numpy as jnp
from jax import lax
from jax.experimental import pallas as pl
from jax.experimental.pallas import tpu as pltpu
from jax.sharding import PartitionSpec as P

HEADS = 12
HEAD_DIM = 64
EPSILON = 1e-05
ROPE_BASE = 10000.0
MASKED_SCORE = -1e30
MESH = pl.DeviceIdType.MESH
BF16 = jnp.bfloat16
F32 = jnp.float32

WIDE = ("y", "xl", "xh", "z", "c")
TALL = ("xl", "xh", "z", "c", "y")
SIZES = {"y": 4, "xl": 2, "xh": 2, "z": 4, "c": 2}
ORDERS = (("y", "z", "x"), ("z", "x", "y"), ("x", "y", "z"))
ITEMS = (
    (0, 0, ORDERS[0], WIDE, 128),
    (0, 1, ORDERS[1], WIDE, 128),
    (0, 2, ORDERS[2], WIDE, 128),
    (1, None, ORDERS[0], WIDE, 384),
    (2, None, ORDERS[1], WIDE, 384),
    (3, None, ORDERS[2], TALL, 384),
)
W_SHAPES = (
    (3,) + tuple(SIZES[n] for n in WIDE) + (48, 128),
    tuple(SIZES[n] for n in WIDE) + (48, 384),
    tuple(SIZES[n] for n in WIDE) + (48, 384),
    tuple(SIZES[n] for n in TALL) + (48, 384),
)


def place():
    f = lax.axis_index("fsdp")
    s = lax.axis_index("seq")
    return {"x": (f // 8) * 2 + s % 2, "y": s // 2, "z": (f // 2) % 4, "c": f % 2}


def device(at):
    return ((at["x"] // 2) * 8 + at["z"] * 2 + at["c"], at["y"] * 2 + at["x"] % 2)


def shifted(at, axis, k):
    return {**at, axis: (at[axis] + k) % SIZES.get(axis, 4)}


def select(names, fixed):
    index = []
    for n in names:
        if n in ("xl", "xh"):
            v = fixed.get("x")
            index.append(pl.ds(0, 2) if v is None else (v % 2 if n == "xl" else v // 2))
        else:
            v = fixed.get(n)
            index.append(pl.ds(0, SIZES[n]) if v is None else v)
    return tuple(index)


def expand(axes):
    return [n for a in axes for n in (("xl", "xh") if a == "x" else (a,))]


def kept(names, axes):
    some = expand(axes)
    return tuple(n for n in names if n in some)


def remote(src, dst, send, recv, to):
    return pltpu.make_async_remote_copy(
        src_ref=src, dst_ref=dst, send_sem=send, recv_sem=recv, device_id=to, device_id_type=MESH
    )


def greet(at):
    f = lax.axis_index("fsdp")
    s = lax.axis_index("seq")
    bar = pltpu.get_barrier_semaphore()
    peers = [(f, (s + k) % 8) for k in range(1, 8)]
    peers += [device(shifted(at, "z", k)) for k in (1, 2, 3)]
    peers += [device(shifted(at, "c", 1))]
    peers += [device({**at, "x": (at["x"] + 2) % 4})]
    peers += [device({**at, "x": (at["x"] // 2 * 2 + 2) % 4 + (1 - at["x"] % 2)})]
    for p in peers:
        pl.semaphore_signal(bar, inc=1, device_id=p, device_id_type=MESH)
    pl.semaphore_wait(bar, len(peers))


def pick_rows(rows, slots, per, offset):
    i = lax.broadcasted_iota(jnp.int32, (rows, slots), 0)
    j = lax.broadcasted_iota(jnp.int32, (rows, slots), 1)
    return (j == (i // per) * 32 + offset + i % per).astype(BF16)


def gather_kernel(
    s0, d0, vh, wa, wg, wu, wd, xa, r0, rd0, sem0s, sem0r, semds, semdr, semxs, semxr, sems, semr, semcs, semcr
):
    at = place()
    f = lax.axis_index("fsdp")
    s = lax.axis_index("seq")
    arrays = (wa, wg, wu, wd)
    greet(at)

    def first(k):
        to, frm = (s + k) % 8, (s - k + 8) % 8
        out = remote(s0.at[to], r0.at[s], sem0s.at[k - 1], sem0r.at[k - 1], (f, to))
        inn = remote(s0.at[to], r0.at[frm], sem0s.at[k - 1], sem0r.at[k - 1], (f, to))
        return out, inn

    firsts = [first(k) for k in range(1, 8)]
    xl = at["x"] % 2
    beside = (f, at["y"] * 2 + 1 - xl)
    down_out = remote(d0.at[1 - xl], rd0.at[xl], semds, semdr, beside)
    down_in = remote(d0.at[1 - xl], rd0.at[1 - xl], semds, semdr, beside)
    for out, _ in firsts:
        out.start()
    down_out.start()

    def token_copy(to):
        return remote(vh, xa.at[s], semxs.at[to], semxr.at[s], (f, to))

    def token_in(frm):
        return remote(vh, xa.at[frm], semxs.at[frm], semxr.at[frm], (f, frm))

    for to in range(1, 8):
        pl.when(to > s)(lambda to=to: token_copy(to).start())

    r0[s] = s0[s]
    rd0[xl] = d0[xl]
    xa[s] = vh[...]
    for _, inn in firsts:
        inn.wait_recv()
    down_in.wait_recv()

    def block(item, fixed):
        array, third, _, names, _ = item
        ref = arrays[array]
        lead = () if third is None else (third,)
        return ref.at[lead + select(names, fixed)]

    def put(item, value):
        array, third, _, names, _ = item
        lead = () if third is None else (third,)
        arrays[array][lead + select(names, at)] = value

    flat = r0[...].reshape(256, 384)
    attn = jnp.dot(pick_rows(48, 256, 6, 12), flat, preferred_element_type=F32).astype(BF16)
    for t in range(3):
        put(ITEMS[t], attn[:, t * 128 : (t + 1) * 128])

    def ring(i, phase, k):
        item = ITEMS[i]
        order = item[2]
        axis = order[phase]
        gone = order[:phase]
        fixed = {n: at[n] for n in ("x", "y", "z", "c") if n not in gone}
        theirs = {**fixed, axis: (at[axis] - k + 4) % 4}
        to = device(shifted(at, axis, k))
        out = remote(block(item, fixed), block(item, fixed), sems.at[i, phase, k - 1], semr.at[i, phase, k - 1], to)
        inn = remote(block(item, theirs), block(item, theirs), sems.at[i, phase, k - 1], semr.at[i, phase, k - 1], to)
        return out, inn

    sibling = device(shifted(at, "c", 1))

    def across(i, k):
        item = ITEMS[i]
        axis = item[2][2]
        mine = {axis: (at[axis] - k + 4) % 4, "c": at["c"]}
        theirs = {axis: (at[axis] - k + 4) % 4, "c": 1 - at["c"]}
        out = remote(block(item, mine), block(item, mine), semcs.at[i, k], semcr.at[i, k], sibling)
        inn = remote(block(item, theirs), block(item, theirs), semcs.at[i, k], semcr.at[i, k], sibling)
        return out, inn

    def start(items, phase):
        for k in (1, 3, 2):
            for i in items:
                ring(i, phase, k)[0].start()

    def arrive(items, phase):
        for k in (1, 3, 2):
            for i in items:
                ring(i, phase, k)[1].wait_recv()

    small, large = (0, 1, 2), (3, 4, 5)
    start(small, 0)
    put(ITEMS[3], jnp.dot(pick_rows(48, 256, 6, 0), flat, preferred_element_type=F32).astype(BF16))
    put(ITEMS[4], jnp.dot(pick_rows(48, 256, 6, 6), flat, preferred_element_type=F32).astype(BF16))
    down = jnp.dot(pick_rows(48, 64, 24, 0), rd0[...].reshape(64, 384), preferred_element_type=F32)
    put(ITEMS[5], down.astype(BF16))
    start(large, 0)
    arrive(small, 0)
    start(small, 1)
    arrive(large, 0)
    start(large, 1)
    arrive(small, 1)
    start(small, 2)
    for i in small:
        across(i, 0)[0].start()
    arrive(large, 1)
    start(large, 2)
    for i in large:
        across(i, 0)[0].start()
    for items in (small, large):
        for k in (1, 3, 2):
            for i in items:
                ring(i, 2, k)[1].wait_recv()
                across(i, k)[0].start()
    for frm in range(0, 7):
        pl.when(frm < s)(lambda frm=frm: token_in(frm).wait_recv())
    for i in range(6):
        for k in range(4):
            across(i, k)[1].wait_recv()
    for out, _ in firsts:
        out.wait_send()
    down_out.wait_send()
    for to in range(1, 8):
        pl.when(to > s)(lambda to=to: token_copy(to).wait_send())
    for i in range(6):
        for phase in range(3):
            for k in (1, 2, 3):
                ring(i, phase, k)[0].wait_send()
        for k in range(4):
            across(i, k)[0].wait_send()


VMEM_SPEC = pl.BlockSpec(memory_space=pltpu.VMEM)
DMA = pltpu.SemaphoreType.DMA


def gather(s0, d0, vh):
    return pl.pallas_call(
        gather_kernel,
        out_shape=[jax.ShapeDtypeStruct(w, BF16) for w in W_SHAPES] + [jax.ShapeDtypeStruct((8, 128, 768), BF16)],
        in_specs=[VMEM_SPEC] * 3,
        out_specs=[VMEM_SPEC] * 5,
        scratch_shapes=[
            pltpu.VMEM((8, 32, 384), BF16),
            pltpu.VMEM((2, 32, 384), BF16),
            DMA((7,)), DMA((7,)), DMA, DMA, DMA((8,)), DMA((8,)),
            DMA((6, 3, 3)), DMA((6, 3, 3)), DMA((6, 4)), DMA((6, 4)),
        ],
        compiler_params=pltpu.CompilerParams(
            collective_id=0, has_side_effects=True, vmem_limit_bytes=60 * 2**20
        ),
        name="gather_weights",
    )(s0, d0, vh)


def scatter_kernel(
    ga, gg, gu, gd, dn, fo, fd, dno,
    ra, rg, ru, rd,
    t3a0, t3a1, t3a2, t3g, t3u, t3d,
    t2a0, t2a1, t2a2, t2g, t2u, t2d,
    t1a, t1m, s3s, f0, fd0, rdn,
    semcs, semcr, sems, semr, sem0s, sem0r, semds, semdr, semxs, semxr,
):
    at = place()
    f = lax.axis_index("fsdp")
    s = lax.axis_index("seq")
    grads = (ga, gg, gu, gd)
    sums = (ra, rg, ru, rd)
    t3 = (t3a0, t3a1, t3a2, t3g, t3u, t3d)
    t2 = (t2a0, t2a1, t2a2, t2g, t2u, t2d)
    greet(at)
    sibling = device(shifted(at, "c", 1))

    def token_out(to):
        return remote(dn.at[to], rdn.at[s], semxs.at[to], semxr.at[s], (f, to))

    def token_in(frm):
        return remote(dn.at[frm], rdn.at[frm], semxs.at[frm], semxr.at[frm], (f, frm))

    def grad_ref(i):
        array, third = ITEMS[i][:2]
        return grads[array] if third is None else grads[array].at[third]

    def sum_ref(i):
        array, third = ITEMS[i][:2]
        return sums[array] if third is None else sums[array].at[third]

    def names_of(i, left):
        return kept(ITEMS[i][3], ITEMS[i][2][:left])

    def across(i):
        return remote(
            grad_ref(i).at[select(ITEMS[i][3], {"c": 1 - at["c"]})], sum_ref(i), semcs.at[i], semcr.at[i], sibling
        )

    large, small = (5, 3, 4), (0, 1, 2)
    for i in large + small:
        across(i).start()
    for to in range(0, 7):
        pl.when(to < s)(lambda to=to: token_out(to).start())

    def digits(names, n):
        out = {}
        for name in reversed(names):
            out[name] = n % SIZES[name]
            n = n // SIZES[name]
        return out

    def full_index(names, fixed, free, n):
        got = digits(free, n)
        index = []
        for name in names:
            if name in free:
                index.append(got[name])
            elif name in ("xl", "xh"):
                index.append(fixed["x"] % 2 if name == "xl" else fixed["x"] // 2)
            else:
                index.append(fixed[name])
        return tuple(index)

    def count(names):
        return math.prod(SIZES[n] for n in names)

    def add_core(i):
        names = ITEMS[i][3]
        free = tuple(n for n in names if n != "c")
        g, r = grad_ref(i), sum_ref(i)

        def body(n, carry):
            gi = full_index(names, {"c": at["c"]}, free, n)
            ri = full_index(free, {}, free, n)
            r[ri] = (r[ri].astype(F32) + g[gi].astype(F32)).astype(BF16)
            return carry

        lax.fori_loop(0, count(free), body, 0)

    def hop(i, left, k):
        axis = ITEMS[i][2][left - 1]
        names = names_of(i, left)
        if left == 3:
            src = sum_ref(i).at[select(names, {axis: (at[axis] + k) % 4})]
            dst = t3[i].at[k - 1]
        else:
            base = stage_ref(i, left)
            src = base.at[select(names, {axis: (at[axis] + k) % 4})]
            dst = t2[i].at[k - 1] if left == 2 else (t1a.at[i, k - 1] if i < 3 else t1m.at[i - 3, k - 1])
        return remote(src, dst, sems.at[i, left - 1, k - 1], semr.at[i, left - 1, k - 1], device(shifted(at, axis, k)))

    def stage_ref(i, left):
        return t3[i].at[0] if left == 2 else t2[i].at[0]

    def add_ring(i, left):
        axis = ITEMS[i][2][left - 1]
        names = names_of(i, left)
        free = names_of(i, left - 1)
        own = sum_ref(i) if left == 3 else stage_ref(i, left)
        inn = t3[i] if left == 3 else t2[i]
        fixed = {axis: at[axis]}

        def body(n, carry):
            oi = full_index(names, fixed, free, n)
            fi = full_index(free, {}, free, n)
            total = own[oi].astype(F32)
            for k in range(3):
                total = total + inn[(k,) + fi].astype(F32)
            inn[(0,) + fi] = total.astype(BF16)
            return carry

        lax.fori_loop(0, count(free), body, 0)

    def start(items, left):
        for k in (1, 3, 2):
            for i in items:
                hop(i, left, k).start()

    def arrive(i, left):
        for k in (1, 3, 2):
            hop(i, left, k).wait_recv()

    for i in large + small:
        across(i).wait_recv()
        add_core(i)
        for k in (1, 3, 2):
            hop(i, 3, k).start()
    for left in (3, 2):
        for i in large + small:
            arrive(i, left)
            add_ring(i, left)
            for k in (1, 3, 2):
                hop(i, left - 1, k).start()

    def last(i):
        arrive(i, 1)
        axis = ITEMS[i][2][0]
        names = names_of(i, 1)
        own = stage_ref(i, 1)
        total = own[select(names, {axis: at[axis]})].astype(F32)
        inn = t1a if i < 3 else t1m
        for k in range(3):
            total = total + inn[i if i < 3 else i - 3, k].astype(F32)
        return total.astype(BF16)

    down = last(5)
    gate = last(3)
    up = last(4)
    attn = jnp.concatenate([last(0), last(1), last(2)], axis=1)

    def unpick(rows, slots, per, offset):
        j = lax.broadcasted_iota(jnp.int32, (slots, rows), 0)
        i = lax.broadcasted_iota(jnp.int32, (slots, rows), 1)
        return (j == (i // per) * 32 + offset + i % per).astype(BF16)

    mixed = jnp.dot(unpick(48, 256, 6, 0), gate, preferred_element_type=F32)
    mixed += jnp.dot(unpick(48, 256, 6, 6), up, preferred_element_type=F32)
    mixed += jnp.dot(unpick(48, 256, 6, 12), attn, preferred_element_type=F32)
    f0[...] = mixed.astype(BF16).reshape(8, 32, 384)
    fd0[...] = jnp.dot(unpick(48, 64, 24, 0), down, preferred_element_type=F32).astype(BF16).reshape(2, 32, 384)

    xl = at["x"] % 2
    beside = (f, at["y"] * 2 + 1 - xl)

    def final(k):
        to, frm = (s + k) % 8, (s - k + 8) % 8
        out = remote(f0.at[to], fo.at[s], sem0s.at[k - 1], sem0r.at[k - 1], (f, to))
        inn = remote(f0.at[to], fo.at[frm], sem0s.at[k - 1], sem0r.at[k - 1], (f, to))
        return out, inn

    down_out = remote(fd0.at[1 - xl], fd.at[xl], semds, semdr, beside)
    down_in = remote(fd0.at[1 - xl], fd.at[1 - xl], semds, semdr, beside)
    for k in range(1, 8):
        final(k)[0].start()
    down_out.start()
    fo[s] = f0[s]
    fd[xl] = fd0[xl]

    dno[...] = dn[s].astype(F32)
    for frm in range(1, 8):

        def add(frm=frm):
            token_in(frm).wait_recv()
            dno[...] += rdn[frm].astype(F32)

        pl.when(frm > s)(add)
    for k in range(1, 8):
        final(k)[1].wait_recv()
    down_in.wait_recv()
    for k in range(1, 8):
        final(k)[0].wait_send()
    down_out.wait_send()
    for to in range(0, 7):
        pl.when(to < s)(lambda to=to: token_out(to).wait_send())
    for i in range(6):
        across(i).wait_send()
        for left in (3, 2, 1):
            for k in (1, 2, 3):
                hop(i, left, k).wait_send()


def dims(i, left):
    return tuple(SIZES[n] for n in kept(ITEMS[i][3], ITEMS[i][2][:left]))


def scatter(ga, gg, gu, gd, dn):
    no_core = lambda shape, names, lead: shape[: names.index("c") + lead] + shape[names.index("c") + lead + 1 :]
    sums = [
        no_core(W_SHAPES[0], WIDE, 1),
        no_core(W_SHAPES[1], WIDE, 0),
        no_core(W_SHAPES[2], WIDE, 0),
        no_core(W_SHAPES[3], TALL, 0),
    ]
    scratch = [pltpu.VMEM(x, BF16) for x in sums]
    for left in (2, 1):
        for i in range(6):
            scratch.append(pltpu.VMEM((3,) + dims(i, left) + (48, ITEMS[i][4]), BF16))
    scratch += [
        pltpu.VMEM((3, 3, 48, 128), BF16),
        pltpu.VMEM((3, 3, 48, 384), BF16),
        pltpu.VMEM((8, 128), F32),
        pltpu.VMEM((8, 32, 384), BF16),
        pltpu.VMEM((2, 32, 384), BF16),
        pltpu.VMEM((8, 128, 768), BF16),
    ]
    return pl.pallas_call(
        scatter_kernel,
        out_shape=[
            jax.ShapeDtypeStruct((8, 32, 384), BF16),
            jax.ShapeDtypeStruct((2, 32, 384), BF16),
            jax.ShapeDtypeStruct((128, 768), F32),
        ],
        in_specs=[VMEM_SPEC] * 5,
        out_specs=[VMEM_SPEC] * 3,
        scratch_shapes=scratch
        + [
            DMA((6,)), DMA((6,)), DMA((6, 3, 3)), DMA((6, 3, 3)),
            DMA((7,)), DMA((7,)), DMA, DMA, DMA((8,)), DMA((8,)),
        ],
        compiler_params=pltpu.CompilerParams(
            collective_id=1, has_side_effects=True, vmem_limit_bytes=60 * 2**20
        ),
        name="scatter_grads",
    )(ga, gg, gu, gd, dn)


def rotate(values, position, sign):
    half_dim = HEAD_DIM // 2
    freqs = ROPE_BASE ** (-(2.0 * jnp.arange(half_dim, dtype=F32)) / HEAD_DIM)
    angles = position.astype(F32)[:, None] * freqs[None, :]
    cosine = jnp.cos(angles)[:, None, :]
    sine = sign * jnp.sin(angles)[:, None, :]
    shaped = values.reshape(values.shape[0], HEADS, HEAD_DIM)
    a = shaped[..., :half_dim]
    b = shaped[..., half_dim:]
    turned = jnp.concatenate([a * cosine - b * sine, b * cosine + a * sine], axis=-1)
    return turned.reshape(values.shape[0], HEADS * HEAD_DIM)


def doc_layout(lengths, pack_len):
    ends = jnp.cumsum(lengths)
    where_pos = jnp.arange(pack_len, dtype=jnp.int32)
    passed = where_pos[:, None] >= ends[None, :]
    segment = jnp.sum(passed.astype(jnp.int32), axis=1)
    start_pos = jnp.sum(jnp.where(passed, lengths[None, :], 0), axis=1)
    return (segment, where_pos - start_pos)


def product(form, left, right):
    return jnp.einsum(form, left, right, preferred_element_type=F32)


def norm_factor(values):
    return lax.rsqrt(jnp.mean(values * values, axis=-1, keepdims=True) + EPSILON)


def norm_back(values, factor, e):
    return factor * e - values * factor**3 * jnp.mean(e * values, axis=-1, keepdims=True)


def pieces(w):
    return w.reshape(6, 8, 384).transpose(1, 0, 2)


def per_device(tokens, doc_lengths, attn_gain, w_query, w_key, w_value, w_out, mlp_gain, w_gate, w_up, w_down, cotangent):
    tok_rows = tokens.shape[1]
    s = lax.axis_index("seq")
    pack_len = tok_rows * 8
    scale_value = 1.0 / math.sqrt(HEAD_DIM)
    gain_one = attn_gain.astype(F32)[:, None]
    gain_two = mlp_gain.astype(F32)[:, None]
    fold = lambda w, g: (w.astype(F32) * g).astype(BF16)

    inputs = tokens[0].astype(F32)
    factor_one = norm_factor(inputs)
    vhat = (inputs * factor_one).astype(BF16)

    attn = jnp.concatenate([fold(w_query, gain_one), fold(w_key, gain_one), fold(w_value, gain_one), w_out], axis=1)
    s0 = jnp.concatenate(
        [pieces(fold(w_gate, gain_two)), pieces(fold(w_up, gain_two)), pieces(attn), jnp.zeros((8, 14, 384), BF16)], axis=1
    )
    d0 = jnp.pad(w_down.reshape(24, 2, 384).transpose(1, 0, 2), ((0, 0), (0, 8), (0, 0)))
    wa, wg, wu, wd, xa = gather(s0, d0, vhat)
    full = wa.reshape(3, 8, 768, 128).transpose(2, 1, 0, 3).reshape(768, 3072)
    full_query, full_key, full_value, full_out = (full[:, i * 768 : (i + 1) * 768] for i in range(4))
    full_gate = wg.reshape(8, 768, 384)
    full_up = wu.reshape(8, 768, 384)
    full_down = wd.reshape(2, 3072, 384)
    before = jnp.arange(8) <= s
    vhat_all = jnp.where(before[:, None, None], xa, 0).reshape(pack_len, 768)

    first_row = s * tok_rows
    segment_all, position_all = doc_layout(doc_lengths[0], pack_len)
    segment_mine = lax.dynamic_slice_in_dim(segment_all, first_row, tok_rows)
    position_mine = lax.dynamic_slice_in_dim(position_all, first_row, tok_rows)
    query_index = first_row + jnp.arange(tok_rows, dtype=jnp.int32)

    queries = rotate(product("td,de->te", vhat, full_query), position_mine, 1.0).astype(BF16)
    key_rows = rotate(product("td,de->te", vhat_all, full_key), position_all, 1.0).astype(BF16)
    value_rows = product("td,de->te", vhat_all, full_value).astype(BF16)
    q = queries.reshape(tok_rows, HEADS, HEAD_DIM)
    k = key_rows.reshape(pack_len, HEADS, HEAD_DIM)
    v = value_rows.reshape(pack_len, HEADS, HEAD_DIM)
    scores = product("qhd,khd->hqk", q, k) * scale_value
    key_index = jnp.arange(pack_len, dtype=jnp.int32)
    allowed = (segment_mine[:, None] == segment_all[None, :]) & (key_index[None, :] <= query_index[:, None])
    probs = jax.nn.softmax(jnp.where(allowed[None], scores, MASKED_SCORE), axis=-1)
    probs_low = probs.astype(BF16)
    attended = product("hqk,khd->qhd", probs_low, v).reshape(tok_rows, 768).astype(BF16)
    hidden = inputs + product("td,de->te", attended, full_out)

    factor_two = norm_factor(hidden)
    vhat_two = (hidden * factor_two).astype(BF16)
    gate_raw = product("td,cdf->tcf", vhat_two, full_gate)
    up_raw = product("td,cdf->tcf", vhat_two, full_up)
    sig = 1.0 / (1.0 + jnp.exp(-gate_raw))
    silu = gate_raw * sig
    mixed = (silu * up_raw).astype(BF16).reshape(tok_rows, 3072)
    mlp_out = product("tf,cfd->tcd", mixed, full_down).reshape(tok_rows, 768)
    layer_out = (hidden + mlp_out).astype(BF16)

    upstream = cotangent[0]
    up_c = upstream.reshape(tok_rows, 2, 384)
    d_mixed = product("tcd,cfd->tf", up_c, full_down).reshape(tok_rows, 8, 384)
    d_gate = (d_mixed * up_raw * sig * (1.0 + gate_raw * (1.0 - sig))).astype(BF16)
    d_up = (d_mixed * silu).astype(BF16)
    e_two = product("tcf,cdf->td", d_gate, full_gate) + product("tcf,cdf->td", d_up, full_up)
    d_hidden = upstream.astype(F32) + norm_back(hidden, factor_two, e_two)
    grad_down = product("tf,tcd->cfd", mixed, up_c).astype(BF16).reshape(W_SHAPES[3])
    grad_gate = product("td,tcf->cdf", vhat_two, d_gate).astype(BF16).reshape(W_SHAPES[1])
    grad_up = product("td,tcf->cdf", vhat_two, d_up).astype(BF16).reshape(W_SHAPES[2])

    d_hidden_low = d_hidden.astype(BF16)
    d_attended = product("te,de->td", d_hidden_low, full_out).astype(BF16)
    da = d_attended.reshape(tok_rows, HEADS, HEAD_DIM)
    d_probs = product("qhd,khd->hqk", da, v)
    d_scores = (probs * (d_probs - jnp.sum(probs * d_probs, axis=-1, keepdims=True))).astype(BF16)
    d_queries = (product("hqk,khd->qhd", d_scores, k) * scale_value).reshape(tok_rows, 768)
    d_keys = (product("hqk,qhd->khd", d_scores, q) * scale_value).reshape(pack_len, 768)
    d_values = product("hqk,qhd->khd", probs_low, da).reshape(pack_len, 768)
    d_query_raw = rotate(d_queries, position_mine, -1.0).astype(BF16)
    d_key_raw = rotate(d_keys, position_all, -1.0).astype(BF16)
    d_value_raw = d_values.astype(BF16)
    e_part = product("te,de->td", d_key_raw, full_key) + product("te,de->td", d_value_raw, full_value)
    e_mine = product("te,de->td", d_query_raw, full_query)
    g_attn = jnp.concatenate(
        [
            product("td,te->de", vhat, d_query_raw),
            product("td,te->de", vhat_all, d_key_raw),
            product("td,te->de", vhat_all, d_value_raw),
            product("td,te->de", attended, d_hidden_low),
        ],
        axis=1,
    ).astype(BF16)
    g_attn = g_attn.reshape(768, 8, 3, 128).transpose(2, 1, 0, 3).reshape(W_SHAPES[0])
    fo, fd, dno = scatter(g_attn, grad_gate, grad_up, grad_down, e_part.astype(BF16).reshape(8, tok_rows, 768))
    e_one = dno + e_mine
    input_grad = d_hidden + norm_back(inputs, factor_one, e_one)

    whole = lambda i: fo[:, i * 6 : i * 6 + 6].astype(F32).transpose(1, 0, 2).reshape(6, 3072)
    h_gate, h_up, h_attn = whole(0), whole(1), whole(2)
    own = lambda h, w: jnp.sum(h * w.astype(F32), axis=1)
    hq, hk, hv, ho = (h_attn[:, i * 768 : (i + 1) * 768] for i in range(4))
    grad_gain_one = own(hq, w_query) + own(hk, w_key) + own(hv, w_value)
    grad_gain_two = own(h_gate, w_gate) + own(h_up, w_up)
    g_down = fd[:, :24].astype(F32).transpose(1, 0, 2).reshape(24, 768)
    return (
        layer_out[None],
        input_grad[None],
        grad_gain_one,
        hq * gain_one,
        hk * gain_one,
        hv * gain_one,
        ho,
        grad_gain_two,
        h_gate * gain_two,
        h_up * gain_two,
        g_down,
    )


def solution(mesh):
    rows = P(("fsdp", "seq"), None)
    gain = P(("fsdp", "seq"))
    toks = P("fsdp", "seq", None)
    return jax.shard_map(
        per_device,
        mesh=mesh,
        in_specs=(toks, P("fsdp", None), gain, rows, rows, rows, rows, gain, rows, rows, rows, toks),
        out_specs=(toks, toks, gain, rows, rows, rows, rows, gain, rows, rows, rows),
        check_vma=False,
    )
```

time: 4180 us -> 311 us (0.07)
  waiting for transfers between devices: 2180 us -> 0 us
  blocking collectives: 1140 us -> 0 us
  starting transfers between devices: 510 us -> 0 us
  local copies, waits for them, and re-layouts: 219 us -> 41.4 us
  Pallas kernels: 0 us -> 177 us
    all_gather x9 -> x0, waiting for transfers between devices: 2110 us -> none  [the longest x1 310 us: per_device(): lax.all_gather(w_gate, ('fsdp', 'seq'), axis=0, tiled=True)]
    unnamed x3 -> x0, blocking collectives: 1140 us -> none
    unnamed x194 -> x0, starting transfers between devices: 510 us -> none
    unnamed x393 -> x126, local copies, waits for them, and re-layouts: 214 us -> 5.57 us
    pallas_call x0 -> x2, Pallas kernels: none -> 177 us  [the longest x1 92 us: gather(): pl.pallas_call(gather_kernel, out_shape=[jax.ShapeDtypeStruct(w, BF16) fo...]
    unnamed x206 -> x0, waiting for transfers between devices: 70.6 us -> none
  transfers between devices with their start and end apart: 204 -> 0, of which waited for: 14 -> 0; matrix products, arithmetic and copies ran while one was open for 31% -> 0% of each run, Pallas kernels for 0% -> 0%
where the time goes in v1:
time: 311 us; the launch traced here: 307 us
  Pallas kernels  177 us (57%)
  matrix products  62.7 us (20%)
  local copies, waits for them, and re-layouts  41.4 us (13%)
  other arithmetic  23.8 us (8%)
    pallas_call x1, Pallas kernels, gather(): pl.pallas_call(gather_kernel, out_shape=[jax.ShapeDtypeStruct(w, BF16) fo...  92 us
    pallas_call x1, Pallas kernels, scatter(): pl.pallas_call(scatter_kernel, out_shape=[jax.ShapeDtypeStruct((8, 32, 38...  84.6 us
    dot_general x27, matrix products, product(): return jnp.einsum(form, left, right, preferred_element_type=F32)  62.7 us
    convert_element_type x1, local copies, waits for them, and re-layouts, per_device(): product('td,tcf->cdf', vhat_two, d_up).astype(BF16).reshape(W_SHAPES[2])  6.88 us
    reshape x1, local copies, waits for them, and re-layouts, per_device(): full = wa.reshape(3, 8, 768, 128).transpose(2, 1, 0, 3).reshape(768, 3072)  6.8 us
    reshape x1, local copies, waits for them, and re-layouts, per_device(): full_down = wd.reshape(2, 3072, 384)  6.68 us
    convert_element_type x1, local copies, waits for them, and re-layouts, per_device(): product('td,tcf->cdf', vhat_two, d_gate).astype(BF16).reshape(W_SHAPES[1])  6.63 us

profile of v1, /device:TPU:1, one launch (start us, length us, event | category | flops | bytes accessed | tf_op | source)
XLA Modules:
  0.0 306.6 jit_solution(2335043454959451277)
XLA Ops:
  10.0 92.0 %gather_weights.1 = (bf16[3,4,2,2,4,2,48,128]{7,6,5,4,3,2,1,0:T(8,128)(2,1)}, bf16[4,2,2,4,2,48,384]{6,5,4,3,2,1,0:T(8,128)(2,1)}, bf16[4,2,2,4,2,48,384]{6,5,4,...) custom-call(bf16[8,32,384]{2,1,0:T(8,128)(2,1)} %maximum_maximum_fusion.s0, ...), custom_call_target="tpu_custom_call" | custom-call | tf_op jit(solution)/shard_map/gather_weights/pallas_call | solution.py:237
  102.0 6.8 %copy.56 = bf16[3,8,768,128]{2,3,0,1:T(8,128)(2,1)} copy(bf16[3,8,768,128]{3,2,1,0:T(8,128)(2,1)} %bitcast.224) | data formatting | bytes 9437184 | tf_op jit(solution)/shard_map/reshape | solution.py:560
  108.9 1.8 fusion.63
  117.4 2.8 fusion.64
  125.5 2.0 fusion.66
  127.6 3.8 %fusion.39 = f32[3072,128,1]{1,0,2:T(8,128)S(1)} fusion(bf16[2,3072,384]{2,1,0:T(8,128)(2,1)} %bitcast.195, bf16[128,2,384]{2,1,0:T(2,128)(2,1)S(1)} %reshape_squeeze.3), kind=kOutput, calls=%fused_computation.88 | convolution fusion | flops 603979776 | bytes 6488064 | tf_op jit(solution)/shard_map/tcd,cfd->tf/dot_general | solution.py:526
  133.0 5.8 %multiply_convert_fusion.2 = (bf16[128,8,384]{2,0,1:T(8,128)(2,1)S(1)}, bf16[128,8,384]{2,0,1:T(8,128)(2,1)S(1)}, bf16[128,8,384]{2,0,1:T(8,128)(2,1)}) fusion(f32[128,8,384]{2,0,1:T(8,128)} %copy.60, f32[128,8,384]{2,0,1:T(8,128)} %fusion.66, bf16[128,768,1]{1,0,2:T(8,128)(2,1)S(1)} %fusion.34, bf16[8,768,384]{2,1,0:T(8,128)(2,1)} %bitcast.225), kind=kOutput, calls=%fused_computation.23 | convolution fusion | flops 609878016 | bytes 10420224 | tf_op jit(solution)/shard_map/td,cdf->tcf/dot_general | solution.py:526
  140.5 4.1 %multiply_reduce_fusion.1 = (f32[128]{0:T(128)S(1)}, f32[128,768]{1,0:T(8,128)S(1)}) fusion(f32[128,768]{1,0:T(8,128)S(1)} %get-tuple-element.83, f32[128,768]{1,0:T(8,128)S(1)} %convolution_bitcast_fusion, bf16[128,8,384]{2,0,1:T(8,128)(2,1)S(1)} %get-tuple-element.40, bf16[8,768,384]{2,1,0:T(8,128)(2,1)} %bitcast.226), kind=kOutput, calls=%fused_computation.71 | convolution fusion | flops 604274560 | bytes 6685184 | tf_op jit(solution)/shard_map/tcf,cdf->td/dot_general | solution.py:526
  147.4 4.7 %multiply_reduce_fusion = (f32[12,128]{1,0:T(8,128)S(1)}, f32[12,128,1024]{2,1,0:T(8,128)S(1)}) fusion(f32[12,128,1024]{2,1,0:T(8,128)} %copy-done.1, f32[12,128]{1,0:T(8,128)S(1)} %get-tuple-element.80, bf16[128,12,64]{0,2,1:T(8,128)(2,1)S(1)} %bitcast.244, bf16[1024,12,64]{0,2,1:T(8,128)(2,1)} %bitcast.256), kind=kOutput, calls=%fused_computation.2 | convolution fusion | flops 206043648 | bytes 14364672 | tf_op jit(solution)/shard_map/qhd,khd->hqk/dot_general | solution.py:526
  152.5 1.7 multiply_convert_fusion
  159.5 2.7 add_convert_fusion
  162.2 3.5 %convert_bitcast_fusion = bf16[8,768,384]{1,2,0:T(8,128)(2,1)} fusion(bf16[128,8,384]{2,0,1:T(8,128)(2,1)S(1)} %copy-done.10, bf16[128,768,1]{1,0,2:T(8,128)(2,1)S(1)} %fusion.34), kind=kOutput, calls=%fused_computation.8 | convolution fusion | flops 606339072 | bytes 5701632 | tf_op jit(solution)/shard_map/td,tcf->cdf/dot_general | solution.py:526
  165.7 6.9 %copy.71 = bf16[8,768,384]{2,1,0:T(8,128)(2,1)} copy(bf16[8,768,384]{1,2,0:T(8,128)(2,1)} %convert_bitcast_fusion) | data formatting | bytes 9437184 | tf_op jit(solution)/shard_map/convert_element_type | solution.py:607
  172.6 4.7 %convert_bitcast_fusion.1 = bf16[8,768,384]{1,2,0:T(8,128)(2,1)} fusion(bf16[128,8,384]{2,0,1:T(8,128)(2,1)} %copy-done.8, bf16[128,768,1]{1,0,2:T(8,128)(2,1)S(1)} %fusion.34), kind=kOutput, calls=%fused_computation.9 | convolution fusion | flops 606339072 | bytes 5701632 | tf_op jit(solution)/shard_map/td,tcf->cdf/dot_general | solution.py:526
  177.3 6.6 %copy.69 = bf16[8,768,384]{2,1,0:T(8,128)(2,1)} copy(bf16[8,768,384]{1,2,0:T(8,128)(2,1)} %convert_bitcast_fusion.1) | data formatting | bytes 9437184 | tf_op jit(solution)/shard_map/convert_element_type | solution.py:606
  184.0 2.7 fusion.9
  188.1 2.5 convolution_convert_fusion.5
  190.6 2.5 convolution_convert_fusion.4
  196.2 2.5 copy.67
  199.1 3.6 %convolution_convert_fusion = bf16[3072,2,384]{2,0,1:T(8,128)(2,1)} fusion(bf16[128,3072,1]{0,1,2:T(8,128)(2,1)S(1)} %bitcast.220, bf16[128,2,384]{2,1,0:T(2,128)(2,1)S(1)} %copy-done.12), kind=kOutput, calls=%fused_computation.5 | convolution fusion | flops 606339072 | bytes 5701632 | tf_op jit(solution)/shard_map/tf,tcd->cfd/dot_general | solution.py:526
  202.8 84.6 %scatter_grads.1 = (bf16[8,32,384]{2,1,0:T(8,128)(2,1)}, bf16[2,32,384]{2,1,0:T(8,128)(2,1)}, f32[128,768]{1,0:T(8,128)}) custom-call(bf16[3,4,2,2,4,2,48,128]{7,6,5,4,3,2,1,0:T(8,128)(2,1)} %bitcast.199, bf16[4,2,2,4,2,48,384]{6,5,4,3,2,1,0:T(8,128)(2,1)} %bitcast.198, bf16[4,2,2,4,2,48,384]{6,5,4,3,2,1,0:T(8,128)(2,1)} %bitcast.197, ...), custom_call_target="tpu_custom_call" | custom-call | tf_op jit(solution)/shard_map/scatter_grads/pallas_call | solution.py:482
  291.4 1.8 fusion.32
  294.8 6.7 %copy.58 = bf16[2,3072,384]{1,2,0:T(8,128)(2,1)} copy(bf16[2,3072,384]{2,1,0:T(8,128)(2,1)} %bitcast.196) | data formatting | bytes 9437184 | tf_op jit(solution)/shard_map/reshape | solution.py:564
  301.5 4.7 %fusion.15 = bf16[1,128,768]{2,1,0:T(8,128)(2,1)} fusion(f32[128,768]{1,0:T(8,128)S(1)} %copy-done.3, bf16[128,3072]{0,1:T(8,128)(2,1)S(1)} %bitcast.221, bf16[768,3072]{1,0:T(8,128)(2,1)} %bitcast.218), kind=kOutput, calls=%fused_computation.48 | convolution fusion | flops 604176384 | bytes 6094848 | tf_op jit(solution)/shard_map/tf,cfd->tcd/dot_general | solution.py:526
  (194 shorter events, 43.0 us)
Async XLA Ops:
  3.5 5.1 %copy-start.46 = (f32[6]{0:T(128)}, f32[6]{0:T(128)S(1)}, u32[]{:S(2)}) copy-start(f32[6]{0:T(128)S(1)} %convert_element_type.181) | copy-start | bytes 76
  6.9 103.8 %copy-start.42 = (f32[128]{0:T(128)}, f32[128]{0:T(128)S(1)}, u32[]{:S(2)}) copy-start(f32[128]{0:T(128)S(1)} %get-tuple-element.72) | copy-start | bytes 1540
  112.7 7.5 %copy-start.15 = (bf16[8,128,768]{2,1,0:T(8,128)(2,1)}, bf16[8,128,768]{2,1,0:T(8,128)(2,1)S(1)}, u32[]{:S(2)}) copy-start(bf16[8,128,768]{2,1,0:T(8,128)(2,1)S(1)} %broadcast_select_fusion) | copy-start | bytes 4718596
  116.0 4.3 %slice-start = ((s8[4718592]{0:T(1024)(128)(4,1)}), s8[4194304]{0:T(1024)(128)(4,1)S(1)}, s32[]{:S(2)}) async-start(s8[4718592]{0:T(1024)(128)(4,1)} %bitcast.204), calls=%async_computation | async-start | bytes 8388608
  120.2 27.1 %copy-start.40 = (f32[12,128]{1,0:T(8,128)}, f32[12,128]{1,0:T(8,128)S(1)}, u32[]{:S(2)}) copy-start(f32[12,128]{1,0:T(8,128)S(1)} %get-tuple-element.80) | copy-start | bytes 18436
  125.3 19.2 %copy-start.2 = (f32[128,768]{1,0:T(8,128)}, f32[128,768]{1,0:T(8,128)S(1)}, u32[]{:S(2)}) copy-start(f32[128,768]{1,0:T(8,128)S(1)} %get-tuple-element.83) | copy-start | bytes 1179652
  127.6 3.8 %copy-start.11 = (bf16[128,2,384]{2,1,0:T(2,128)(2,1)}, bf16[128,2,384]{2,1,0:T(2,128)(2,1)S(1)}, u32[]{:S(2)}) copy-start(bf16[128,2,384]{2,1,0:T(2,128)(2,1)S(1)} %reshape_squeeze.3) | copy-start | bytes 589828
  131.4 7.4 %slice-start.6 = ((s8[4718592]{0:T(1024)(128)(4,1)}), s8[524288]{0:T(1024)(128)(4,1)S(1)}, s32[]{:S(2)}) async-start(s8[4718592]{0:T(1024)(128)(4,1)} %bitcast.215), calls=%async_computation.6 | async-start | bytes 1048576
  133.0 5.8 %slice-start.7 = ((s8[4718592]{0:T(1024)(128)(4,1)}), s8[4194304]{0:T(1024)(128)(4,1)S(1)}, s32[]{:S(2)}) async-start(s8[4718592]{0:T(1024)(128)(4,1)} %bitcast.215), calls=%async_computation.7 | async-start | bytes 8388608
  145.4 6.7 %copy-start.4 = (f32[128,768]{1,0:T(8,128)}, f32[128,768]{1,0:T(8,128)S(1)}, u32[]{:S(2)}) copy-start(f32[128,768]{1,0:T(8,128)S(1)} %get-tuple-element.33) | copy-start | bytes 1179652
  147.3 4.8 %copy-start.31 = (bf16[128,768]{0,1:T(8,128)(2,1)}, bf16[128,768]{0,1:T(8,128)(2,1)S(1)}, u32[]{:S(2)}) copy-start(bf16[128,768]{0,1:T(8,128)(2,1)S(1)} %copy.62) | copy-start | bytes 589828
  147.3 4.8 %slice-start.8 = ((s8[6291456]{0:T(1024)(128)(4,1)}), s8[4194304]{0:T(1024)(128)(4,1)S(1)}, s32[]{:S(2)}) async-start(s8[6291456]{0:T(1024)(128)(4,1)} %bitcast.222), calls=%async_computation.8 | async-start | bytes 8388608
  147.3 5.2 %slice-start.9 = ((s8[6291456]{0:T(1024)(128)(4,1)}), s8[2097152]{0:T(1024)(128)(4,1)S(1)}, s32[]{:S(2)}) async-start(s8[6291456]{0:T(1024)(128)(4,1)} %bitcast.222), calls=%async_computation.9 | async-start | bytes 4194304
  202.8 85.8 %copy-start.33 = (bf16[6,3072]{1,0:T(8,128)(2,1)S(1)}, bf16[6,3072]{1,0:T(8,128)(2,1)}, u32[]{:S(2)}) copy-start(bf16[6,3072]{1,0:T(8,128)(2,1)} %param.20) | copy-start | bytes 110596
  202.8 85.8 %copy-start.34 = (bf16[6,3072]{1,0:T(8,128)(2,1)S(1)}, bf16[6,3072]{1,0:T(8,128)(2,1)}, u32[]{:S(2)}) copy-start(bf16[6,3072]{1,0:T(8,128)(2,1)} %param.21) | copy-start | bytes 110596
  202.8 85.8 %copy-start.47 = (f32[6]{0:T(128)S(1)}, f32[6]{0:T(128)}, u32[]{:S(2)}) copy-start(f32[6]{0:T(128)} %copy-done.46) | copy-start | bytes 76
  202.8 87.2 %copy-start.36 = (bf16[6,768]{1,0:T(8,128)(2,1)S(1)}, bf16[6,768]{1,0:T(8,128)(2,1)}, u32[]{:S(2)}) copy-start(bf16[6,768]{1,0:T(8,128)(2,1)} %param.15) | copy-start | bytes 27652
  202.8 87.2 %copy-start.37 = (bf16[6,768]{1,0:T(8,128)(2,1)S(1)}, bf16[6,768]{1,0:T(8,128)(2,1)}, u32[]{:S(2)}) copy-start(bf16[6,768]{1,0:T(8,128)(2,1)} %param.16) | copy-start | bytes 27652
  202.8 87.2 %copy-start.38 = (bf16[6,768]{1,0:T(8,128)(2,1)S(1)}, bf16[6,768]{1,0:T(8,128)(2,1)}, u32[]{:S(2)}) copy-start(bf16[6,768]{1,0:T(8,128)(2,1)} %param.17) | copy-start | bytes 27652
  202.8 87.2 %copy-start.45 = (f32[6]{0:T(128)S(1)}, f32[6]{0:T(128)}, u32[]{:S(2)}) copy-start(f32[6]{0:T(128)} %copy-done.44) | copy-start | bytes 76
  287.5 5.7 %copy-start.5 = (f32[128,768]{1,0:T(8,128)S(1)}, f32[128,768]{1,0:T(8,128)}, u32[]{:S(2)}) copy-start(f32[128,768]{1,0:T(8,128)} %copy-done.4) | copy-start | bytes 1179652
  287.5 5.7 %copy-start.48 = (f32[128]{0:T(128)S(1)}, f32[128]{0:T(128)}, u32[]{:S(2)}) copy-start(f32[128]{0:T(128)} %get-tuple-element.71) | copy-start | bytes 1540
  288.5 5.6 %copy-start.39 = (bf16[2,32,384]{2,1,0:T(8,128)(2,1)S(1)}, bf16[2,32,384]{2,1,0:T(8,128)(2,1)}, u32[]{:S(2)}) copy-start(bf16[2,32,384]{2,1,0:T(8,128)(2,1)} %get-tuple-element.26) | copy-start | bytes 147460
  294.8 6.7 %copy-start.3 = (f32[128,768]{1,0:T(8,128)S(1)}, f32[128,768]{1,0:T(8,128)}, u32[]{:S(2)}) copy-start(f32[128,768]{1,0:T(8,128)} %copy-done.2) | copy-start | bytes 1179652
  (39 other events, 84.5 us)

commit v2 on v0

v2 whole, which is shorter than its diff:
```python
import math

import jax
import jax.numpy as jnp
from jax import lax
from jax.experimental import pallas as pl
from jax.experimental.pallas import tpu as pltpu
from jax.sharding import PartitionSpec as P

HEADS = 12
HEAD_DIM = 64
EPSILON = 1e-05
ROPE_BASE = 10000.0
MASKED_SCORE = -1e30
VMEM_LIMIT = 62 * 2**20
MESH = pl.DeviceIdType.MESH
BF16 = jnp.bfloat16
F32 = jnp.float32

WIDE = ("y", "xl", "xh", "z", "c")
TALL = ("xl", "xh", "z", "c", "y")
SIZES = {"y": 4, "xl": 2, "xh": 2, "z": 4, "c": 2}
ORDERS = (("y", "z", "x"), ("z", "x", "y"), ("x", "y", "z"))
ITEMS = (
    (0, 0, ORDERS[0], WIDE, 128),
    (0, 1, ORDERS[1], WIDE, 128),
    (0, 2, ORDERS[2], WIDE, 128),
    (1, None, ORDERS[0], WIDE, 384),
    (2, None, ORDERS[1], WIDE, 384),
    (3, None, ORDERS[2], TALL, 384),
)
W_SHAPES = (
    (3,) + tuple(SIZES[n] for n in WIDE) + (48, 128),
    tuple(SIZES[n] for n in WIDE) + (48, 384),
    tuple(SIZES[n] for n in WIDE) + (48, 384),
    tuple(SIZES[n] for n in TALL) + (48, 384),
)


def place():
    f = lax.axis_index("fsdp")
    s = lax.axis_index("seq")
    return {"x": (f // 8) * 2 + s % 2, "y": s // 2, "z": (f // 2) % 4, "c": f % 2}


def device(at):
    return ((at["x"] // 2) * 8 + at["z"] * 2 + at["c"], at["y"] * 2 + at["x"] % 2)


def shifted(at, axis, k):
    return {**at, axis: (at[axis] + k) % SIZES.get(axis, 4)}


def select(names, fixed):
    index = []
    for n in names:
        if n in ("xl", "xh"):
            v = fixed.get("x")
            index.append(pl.ds(0, 2) if v is None else (v % 2 if n == "xl" else v // 2))
        else:
            v = fixed.get(n)
            index.append(pl.ds(0, SIZES[n]) if v is None else v)
    return tuple(index)


def expand(axes):
    return [n for a in axes for n in (("xl", "xh") if a == "x" else (a,))]


def kept(names, axes):
    some = expand(axes)
    return tuple(n for n in names if n in some)


def remote(src, dst, send, recv, to):
    return pltpu.make_async_remote_copy(
        src_ref=src, dst_ref=dst, send_sem=send, recv_sem=recv, device_id=to, device_id_type=MESH
    )


def greet(at):
    f = lax.axis_index("fsdp")
    s = lax.axis_index("seq")
    bar = pltpu.get_barrier_semaphore()
    peers = [(f, (s + k) % 8) for k in range(1, 8)]
    peers += [device(shifted(at, "z", k)) for k in (1, 2, 3)]
    peers += [device(shifted(at, "c", 1))]
    peers += [device({**at, "x": (at["x"] + 2) % 4})]
    peers += [device({**at, "x": (at["x"] // 2 * 2 + 2) % 4 + (1 - at["x"] % 2)})]
    for p in peers:
        pl.semaphore_signal(bar, inc=1, device_id=p, device_id_type=MESH)
    pl.semaphore_wait(bar, len(peers))


def one_hot(rows, slots, per, offset, flip=False):
    shape = (slots, rows) if flip else (rows, slots)
    i = lax.broadcasted_iota(jnp.int32, shape, 1 if flip else 0)
    j = lax.broadcasted_iota(jnp.int32, shape, 0 if flip else 1)
    return (j == (i // per) * 32 + offset + i % per).astype(BF16)


def nn(a, b):
    return jnp.dot(a, b, preferred_element_type=F32)


def nt(a, b):
    return lax.dot_general(a, b, (((1,), (1,)), ((), ())), preferred_element_type=F32)


def tn(a, b):
    return lax.dot_general(a, b, (((0,), (0,)), ((), ())), preferred_element_type=F32)


def norm_factor(values):
    return lax.rsqrt(jnp.mean(values * values, axis=-1, keepdims=True) + EPSILON)


def norm_back(values, factor, e):
    return factor * e - values * (factor * factor * factor * jnp.mean(e * values, axis=-1, keepdims=True))


def swap_halves(v):
    lane = lax.broadcasted_iota(jnp.int32, v.shape, 1)
    return jnp.where(lane % 64 < 32, pltpu.roll(v, 96, 1), pltpu.roll(v, 32, 1))


def digits(names, n):
    out = {}
    for name in reversed(names):
        out[name] = n % SIZES[name]
        n = n // SIZES[name]
    return out


def full_index(names, fixed, free, n):
    got = digits(free, n)
    index = []
    for name in names:
        if name in free:
            index.append(got[name])
        elif name in ("xl", "xh"):
            index.append(fixed["x"] % 2 if name == "xl" else fixed["x"] // 2)
        else:
            index.append(fixed[name])
    return tuple(index)


def count(names):
    return math.prod(SIZES[n] for n in names)


def layer_kernel(
    lens, gains, tok, cot, w_query, w_key, w_value, w_out, w_gate, w_up, w_down,
    out_o, in_o, ga1_o, gq_o, gk_o, gv_o, go_o, ga2_o, gg_o, gu_o, gd_o,
    wa, wg, wu, wd, ga, gg, gu, gd, xa, xat, r0, rd0, s0, d0,
    ks, vs, qs, ps, att, hid, oacc, eacc, dhid, dqs, cosine, sine, bias, rdn, fo, fd0,
    t2a0, t2a1, t2a2, t2g, t2u, t2d, t1a, t1m,
    sem0s, sem0r, semds, semdr, semxs, semxr, sems, semr, semcs, semcr,
    bem0s, bem0r, bemds, bemdr, bemxs, bemxr, bems, bemr, bemcs, bemcr, free_large, free_small,
):
    at = place()
    f = lax.axis_index("fsdp")
    s = lax.axis_index("seq")
    weights = (wa, wg, wu, wd)
    grads = (ga, gg, gu, gd)
    t2 = (t2a0, t2a1, t2a2, t2g, t2u, t2d)
    sibling = device(shifted(at, "c", 1))
    xl = at["x"] % 2
    beside = (f, at["y"] * 2 + 1 - xl)
    small, large = (0, 1, 2), (5, 3, 4)

    row = lax.broadcasted_iota(jnp.int32, (6, 1), 0)

    def gain_column(which):
        col = jnp.zeros((6, 1), F32)
        for r in range(6):
            col = jnp.where(row == r, gains[which, r], col)
        return col

    gain_one, gain_two = gain_column(0), gain_column(1)
    inputs = tok[...].astype(F32)
    factor_one = norm_factor(inputs)
    xa[s] = (inputs * factor_one).astype(BF16)
    s0[...] = jnp.zeros_like(s0)
    d0[...] = jnp.zeros_like(d0)
    for b in range(8):
        lanes = pl.ds(b * 384, 384)
        half = pl.ds((b % 2) * 384, 384)
        s0[b, 0:6] = w_gate[:, lanes].astype(F32) * gain_two
        s0[b, 8:14] = w_up[:, lanes].astype(F32) * gain_two
        if b < 6:
            s0[b, 16:22] = (w_query, w_key, w_value)[b // 2][:, half].astype(F32) * gain_one
        else:
            s0[b, 16:22] = w_out[:, half].astype(F32)
    for b in range(2):
        d0[b, 0:24] = w_down[:, b * 384 : (b + 1) * 384].astype(F32)
    s0b, d0b = fo, fd0
    s0b[...] = s0[...].astype(BF16)
    d0b[...] = d0[...].astype(BF16)

    greet(at)

    def first(k):
        to, frm = (s + k) % 8, (s - k + 8) % 8
        out = remote(s0b.at[to], r0.at[s], sem0s.at[k - 1], sem0r.at[k - 1], (f, to))
        inn = remote(s0b.at[to], r0.at[frm], sem0s.at[k - 1], sem0r.at[k - 1], (f, to))
        return out, inn

    def down_copy(slot):
        return remote(d0b.at[1 - xl], rd0.at[slot], semds, semdr, beside)

    def token_out(to):
        return remote(xa.at[s], xa.at[s], semxs.at[to], semxr.at[s], (f, to))

    def token_in(frm):
        return remote(xa.at[frm], xa.at[frm], semxs.at[frm], semxr.at[frm], (f, frm))

    for k in range(1, 8):
        first(k)[0].start()
    down_copy(xl).start()
    for to in range(1, 8):
        pl.when(to > s)(lambda to=to: token_out(to).start())
    r0[s] = s0b[s]
    rd0[xl] = d0b[xl]

    def item_ref(arrays, i):
        array, third = ITEMS[i][:2]
        return arrays[array] if third is None else arrays[array].at[third]

    def block(i, fixed):
        return item_ref(weights, i).at[select(ITEMS[i][3], fixed)]

    def put(i, value):
        array, third, _, names, _ = ITEMS[i]
        lead = () if third is None else (third,)
        weights[array][lead + select(names, at)] = value

    def ring(i, phase, k):
        order = ITEMS[i][2]
        axis = order[phase]
        fixed = {n: at[n] for n in ("x", "y", "z", "c") if n not in order[:phase]}
        theirs = {**fixed, axis: (at[axis] - k + 4) % 4}
        to = device(shifted(at, axis, k))
        send, recv = sems.at[i, phase, k - 1], semr.at[i, phase, k - 1]
        return remote(block(i, fixed), block(i, fixed), send, recv, to), remote(
            block(i, theirs), block(i, theirs), send, recv, to
        )

    def across(i, k):
        axis = ITEMS[i][2][2]
        mine = {axis: (at[axis] - k + 4) % 4, "c": at["c"]}
        theirs = {**mine, "c": 1 - at["c"]}
        send, recv = semcs.at[i, k], semcr.at[i, k]
        return remote(block(i, mine), block(i, mine), send, recv, sibling), remote(
            block(i, theirs), block(i, theirs), send, recv, sibling
        )

    def start(items, phase):
        for k in (1, 3, 2):
            for i in items:
                ring(i, phase, k)[0].start()

    def arrive(items, phase):
        for k in (1, 3, 2):
            for i in items:
                ring(i, phase, k)[1].wait_recv()

    for k in range(1, 8):
        first(k)[1].wait_recv()
    flat = r0[...].reshape(256, 384)
    piece = nn(one_hot(48, 256, 6, 16), flat).astype(BF16)
    for t in range(3):
        put(t, piece[:, t * 128 : (t + 1) * 128])
    start(small, 0)
    put(3, nn(one_hot(48, 256, 6, 0), flat).astype(BF16))
    put(4, nn(one_hot(48, 256, 6, 8), flat).astype(BF16))
    down_copy(1 - xl).wait_recv()
    put(5, nn(one_hot(48, 64, 24, 0), rd0[...].reshape(64, 384)).astype(BF16))
    start(large, 0)
    arrive(small, 0)
    start(small, 1)
    arrive(large, 0)
    start(large, 1)

    ends = [lens[0, 0], lens[0, 0] + lens[0, 1], lens[0, 0] + lens[0, 1] + lens[0, 2]]
    freq_lane = (lax.broadcasted_iota(jnp.int32, (1, 128), 1) % 32).astype(F32)
    freqs = jnp.exp(freq_lane * (-2.0 * math.log(ROPE_BASE) / HEAD_DIM))
    lane = lax.broadcasted_iota(jnp.int32, (128, 128), 1)

    def segment_of(index):
        return sum((index >= e).astype(jnp.int32) for e in ends)

    def table(u, carry):
        index = u * 128 + lax.broadcasted_iota(jnp.int32, (128, 1), 0)
        begin = jnp.zeros_like(index)
        for e in ends:
            begin = jnp.where(index >= e, e, begin)
        angle = (index - begin).astype(F32) * freqs
        rows = pl.ds(pl.multiple_of(u * 128, 128), 128)
        cosine[rows, :] = jnp.cos(angle)
        sine[rows, :] = jnp.where(lane % 64 < 32, -1.0, 1.0) * jnp.sin(angle)
        mine = s * 128 + lax.broadcasted_iota(jnp.int32, (1, 128), 1)
        allowed = (segment_of(index) == segment_of(mine)) & (index <= mine)
        bias[rows, :] = jnp.where(allowed, 0.0, MASKED_SCORE)
        return carry

    lax.fori_loop(0, 8, table, 0)

    arrive(small, 1)
    start(small, 2)
    for i in small:
        across(i, 0)[0].start()
    arrive(large, 1)
    start(large, 2)
    for i in large:
        across(i, 0)[0].start()
    for u in range(1, 8):

        def clear(u=u):
            xa[u] = jnp.zeros((128, 768), BF16)

        pl.when(u > s)(clear)
    for frm in range(0, 7):
        pl.when(frm < s)(lambda frm=frm: token_in(frm).wait_recv())

    def transpose_tokens(u, carry):
        xat[:, pl.ds(pl.multiple_of(u * 128, 128), 128)] = xa[u].T
        return carry

    lax.fori_loop(0, 8, transpose_tokens, 0)
    for k in (1, 3, 2):
        for i in small:
            ring(i, 2, k)[1].wait_recv()
            across(i, k)[0].start()
    for k in range(4):
        for i in small:
            across(i, k)[1].wait_recv()

    for k in range(1, 8):
        first(k)[0].wait_send()
    down_copy(xl).wait_send()
    for to in range(1, 8):
        pl.when(to > s)(lambda to=to: token_out(to).wait_send())

    mine = pl.ds(pl.multiple_of(s * 128, 128), 128)
    cos_mine, sin_mine = cosine[mine, :], sine[mine, :]
    left = lax.broadcasted_iota(jnp.int32, (128, 128), 1) < 64

    def attn_weight(kind, p):
        return wa[p % 3, kind, p // 3].reshape(768, 128)

    def attn_full(kind):
        return jnp.concatenate([attn_weight(kind, p) for p in range(6)], axis=1)

    def stacked(v):
        zero = jnp.zeros_like(v)
        return jnp.concatenate([jnp.where(left, v, zero), jnp.where(left, zero, v)], axis=0)

    def unstacked(v):
        return jnp.concatenate([v[:64, :128], v[64:, 128:]], axis=0).T

    def pair_lanes(p):
        return pl.ds(pl.multiple_of(p * 128, 128), 128)

    def attend(p, carry):
        tokens_all = xa[...].reshape(1024, 768)
        w_kv = jnp.concatenate([attn_weight(1, p), attn_weight(2, p)], axis=1)
        kv = nn(tokens_all, w_kv)
        k_raw = kv[:, :128]
        k = (k_raw * cosine[...] + swap_halves(k_raw) * sine[...]).astype(BF16)
        v = kv[:, 128:].astype(BF16)
        q_raw = nn(xa[s], attn_weight(0, p))
        q = ((q_raw * cos_mine + swap_halves(q_raw) * sin_mine).astype(BF16) * (1.0 / math.sqrt(HEAD_DIM))).astype(BF16)
        qq = stacked(q)
        ks[p] = k
        vs[p] = v
        qs[p] = qq
        masks = bias[...]
        scores = nt(k, qq) + jnp.concatenate([masks, masks], axis=1)
        top = jnp.max(scores, axis=0, keepdims=True)
        e = jnp.exp(scores - top)
        total = jnp.sum(e, axis=0, keepdims=True)
        probs = (e * (1.0 / total)).astype(BF16)
        ps[p] = probs
        att[:, pair_lanes(p)] = unstacked(tn(v, probs)).astype(BF16)
        return carry

    lax.fori_loop(0, 6, attend, 0)

    hidden = tok[...].astype(F32) + nn(att[...], attn_full(3))
    hid[...] = hidden
    factor_two = norm_factor(hidden)
    v2 = (hidden * factor_two).astype(BF16)
    v2t = v2.T
    oacc[...] = jnp.zeros_like(oacc)
    eacc[...] = jnp.zeros_like(eacc)

    for k in (1, 3, 2):
        for i in large:
            ring(i, 2, k)[1].wait_recv()
            across(i, k)[0].start()
    for k in range(4):
        for i in large:
            across(i, k)[1].wait_recv()

    def feed(b, carry):
        y, h = b // 2, b % 2
        g_w = wg[y, h].reshape(768, 384)
        u_w = wu[y, h].reshape(768, 384)
        d_w = jnp.concatenate([wd[0, b // 4, b % 4].reshape(384, 384), wd[1, b // 4, b % 4].reshape(384, 384)], axis=1)
        c = cot[...]
        gate = nn(v2, g_w)
        up = nn(v2, u_w)
        sig = 1.0 / (1.0 + jnp.exp(-gate))
        silu = gate * sig
        mixed = (silu * up).astype(BF16)
        oacc[...] += nn(mixed, d_w)
        d_mixed = nt(c, d_w)
        d_gate = (d_mixed * up * sig * (1.0 + gate * (1.0 - sig))).astype(BF16)
        d_up = (d_mixed * silu).astype(BF16)
        eacc[...] += nt(d_gate, g_w) + nt(d_up, u_w)
        gg[y, h] = nn(v2t, d_gate).astype(BF16).reshape(2, 4, 2, 48, 384)
        gu[y, h] = nn(v2t, d_up).astype(BF16).reshape(2, 4, 2, 48, 384)
        g_d = tn(mixed, c).astype(BF16)
        gd[0, b // 4, b % 4] = g_d[:, :384].reshape(2, 4, 48, 384)
        gd[1, b // 4, b % 4] = g_d[:, 384:].reshape(2, 4, 48, 384)
        return carry

    lax.fori_loop(0, 8, feed, 0)

    def give(sem):
        peers = [sibling] + [device(shifted(at, a, k)) for a in ("x", "y", "z") for k in (1, 2, 3)]
        for p in peers:
            pl.semaphore_signal(sem, inc=1, device_id=p, device_id_type=MESH)
        pl.semaphore_wait(sem, len(peers))

    def sent(items):
        for i in items:
            for phase in range(3):
                for k in (1, 2, 3):
                    ring(i, phase, k)[0].wait_send()
            for k in range(4):
                across(i, k)[0].wait_send()

    def chunk(i, l, core):
        return item_ref(grads, i).at[select(ITEMS[i][3], {ITEMS[i][2][2]: l, "c": core})]

    def store(i, l, core):
        return item_ref(weights, i).at[select(ITEMS[i][3], {ITEMS[i][2][2]: l, "c": core})]

    def share(i, k):
        l = (at[ITEMS[i][2][2]] + k) % 4
        return remote(chunk(i, l, 1 - at["c"]), store(i, l, 0), bemcs.at[i, k], bemcr.at[i, k], sibling)

    def hop(i, left, k):
        order = ITEMS[i][2]
        axis = order[left - 1]
        there = (at[axis] + k) % 4
        if left == 3:
            src, dst = store(i, there, 0), store(i, k - 1, 1)
        else:
            fixed = {order[2]: at[order[2]], "c": 0, axis: there}
            if left == 1:
                fixed[order[1]] = at[order[1]]
            src = item_ref(weights, i).at[select(ITEMS[i][3], fixed)]
            dst = t2[i].at[k - 1] if left == 2 else (t1a.at[i, k - 1] if i < 3 else t1m.at[i - 3, k - 1])
        send, recv = bems.at[i, left - 1, k - 1], bemr.at[i, left - 1, k - 1]
        return remote(src, dst, send, recv, device(shifted(at, axis, k)))

    def add_core(i, k):
        names, order = ITEMS[i][3], ITEMS[i][2]
        free = kept(names, order[:2])
        axis = order[2]
        l = (at[axis] + k) % 4
        g, r = item_ref(grads, i), item_ref(weights, i)

        def body(n, carry):
            gi = full_index(names, {axis: l, "c": at["c"]}, free, n)
            ri = full_index(names, {axis: l, "c": 0}, free, n)
            r[ri] = (r[ri].astype(F32) + g[gi].astype(F32)).astype(BF16)
            return carry

        lax.fori_loop(0, count(free), body, 0)

    def add_ring(i, left):
        names, order = ITEMS[i][3], ITEMS[i][2]
        axis = order[left - 1]
        free = kept(names, order[: left - 1])
        r = item_ref(weights, i)
        fixed = {order[2]: at[order[2]], "c": 0, axis: at[axis]}

        def body(n, carry):
            oi = full_index(names, fixed, free, n)
            total = r[oi].astype(F32)
            for k in range(3):
                if left == 3:
                    total = total + r[full_index(names, {axis: k, "c": 1}, free, n)].astype(F32)
                else:
                    total = total + t2[i][(k,) + full_index(free, {}, free, n)].astype(F32)
            r[oi] = total.astype(BF16)
            return carry

        lax.fori_loop(0, count(free), body, 0)

    def hop_arrive(i, left):
        for k in (1, 3, 2):
            hop(i, left, k).wait_recv()

    def last(i):
        hop_arrive(i, 1)
        fixed = {**at, "c": 0}
        total = item_ref(weights, i)[select(ITEMS[i][3], fixed)].astype(F32)
        for k in range(3):
            total = total + (t1a[i, k] if i < 3 else t1m[i - 3, k]).astype(F32)
        return total.astype(BF16)

    sent(large)
    give(free_large)
    for k in (1, 3, 2, 0):
        for i in large:
            share(i, k).start()

    hidden = hid[...]
    factor_two = norm_factor(hidden)
    out_o[...] = (hidden + oacc[...]).astype(BF16)
    d_hidden = cot[...].astype(F32) + norm_back(hidden, factor_two, eacc[...])
    dhid[...] = d_hidden
    dh = d_hidden.astype(BF16)
    d_att = nt(dh, attn_full(3)).astype(BF16)
    att_t = att[...].T
    for j in range(2):
        g_o = nn(att_t, dh[:, j * 384 : (j + 1) * 384]).astype(BF16)
        for t in range(3):
            ga[t, 3, j] = g_o[:, t * 128 : (t + 1) * 128].reshape(2, 4, 2, 48, 128)
    att[...] = d_att

    def attend_back(p, carry):
        da = stacked(att[:, pair_lanes(p)])
        k, v, qq, probs = ks[p], vs[p], qs[p], ps[p]
        d_probs = nt(v, da)
        probs_f = probs.astype(F32)
        d_sum = jnp.sum(probs_f * d_probs, axis=0, keepdims=True)
        d_scores = (probs_f * (d_probs - d_sum)).astype(BF16)
        d_v = nn(probs, da).astype(BF16)
        d_k = nn(d_scores, qq)
        d_k = (d_k * cosine[...] - swap_halves(d_k) * sine[...]).astype(BF16)
        d_q = unstacked(tn(k, d_scores)) * (1.0 / math.sqrt(HEAD_DIM))
        d_q = (d_q * cos_mine - swap_halves(d_q) * sin_mine).astype(BF16)
        ks[p] = d_k
        vs[p] = d_v
        dqs[:, pair_lanes(p)] = d_q
        g_kv = nn(xat[...], jnp.concatenate([d_k, d_v], axis=1)).astype(BF16)
        g_q = nn(xat[:, mine], d_q).astype(BF16)
        t, h = p % 3, p // 3
        ga[t, 0, h] = g_q.reshape(2, 4, 2, 48, 128)
        ga[t, 1, h] = g_kv[:, :128].reshape(2, 4, 2, 48, 128)
        ga[t, 2, h] = g_kv[:, 128:].reshape(2, 4, 2, 48, 128)
        return carry

    for j, k in enumerate((1, 3, 2)):
        lax.fori_loop(2 * j, 2 * j + 2, attend_back, 0)
        for i in large:
            share(i, k).wait_recv()
            add_core(i, k)
            hop(i, 3, k).start()

    w_kv = jnp.concatenate([attn_full(1), attn_full(2)], axis=1)

    def tokens_back(u, carry):
        rows = pl.ds(pl.multiple_of(u * 128, 128), 128)
        d_kv = jnp.concatenate([ks[p, rows, :] for p in range(6)] + [vs[p, rows, :] for p in range(6)], axis=1)
        xa[u] = nt(d_kv, w_kv).astype(BF16)
        return carry

    lax.fori_loop(0, 8, tokens_back, 0)

    def grad_out(to):
        return remote(xa.at[to], rdn.at[s], bemxs.at[to], bemxr.at[s], (f, to))

    def grad_in(frm):
        return remote(xa.at[frm], rdn.at[frm], bemxs.at[frm], bemxr.at[frm], (f, frm))

    for to in range(0, 7):
        pl.when(to < s)(lambda to=to: grad_out(to).start())
    eacc[...] = nt(dqs[...], attn_full(0))

    sent(small)
    give(free_small)
    for k in (1, 3, 2, 0):
        for i in small:
            share(i, k).start()

    for i in large:
        share(i, 0).wait_recv()
        add_core(i, 0)
    for k in (1, 3, 2):
        for i in small:
            share(i, k).wait_recv()
            add_core(i, k)
            hop(i, 3, k).start()
    for i in small:
        share(i, 0).wait_recv()
        add_core(i, 0)
    for i in large:
        hop_arrive(i, 3)
        add_ring(i, 3)
        for k in (1, 3, 2):
            hop(i, 2, k).start()
    for i in small:
        hop_arrive(i, 3)
        add_ring(i, 3)
        for k in (1, 3, 2):
            hop(i, 2, k).start()
    for i in large + small:
        hop_arrive(i, 2)
        add_ring(i, 2)
        for k in (1, 3, 2):
            hop(i, 1, k).start()

    eacc[...] += xa[s].astype(F32)
    for frm in range(1, 8):

        def add(frm=frm):
            grad_in(frm).wait_recv()
            eacc[...] += rdn[frm].astype(F32)

        pl.when(frm > s)(add)
    inputs = tok[...].astype(F32)
    in_o[...] = dhid[...] + norm_back(inputs, norm_factor(inputs), eacc[...])

    down, gate, up = last(5), last(3), last(4)
    attn = jnp.concatenate([last(0), last(1), last(2)], axis=1)
    rows = nn(one_hot(48, 256, 6, 0, True), gate)
    rows += nn(one_hot(48, 256, 6, 8, True), up)
    rows += nn(one_hot(48, 256, 6, 16, True), attn)
    fo[...] = rows.astype(BF16).reshape(8, 32, 384)
    fd0[...] = nn(one_hot(48, 64, 24, 0, True), down).astype(BF16).reshape(2, 32, 384)

    def final(k):
        to, frm = (s + k) % 8, (s - k + 8) % 8
        out = remote(fo.at[to], r0.at[s], bem0s.at[k - 1], bem0r.at[k - 1], (f, to))
        inn = remote(fo.at[to], r0.at[frm], bem0s.at[k - 1], bem0r.at[k - 1], (f, to))
        return out, inn

    def final_down(slot):
        return remote(fd0.at[1 - xl], rd0.at[slot], bemds, bemdr, beside)

    for k in range(1, 8):
        final(k)[0].start()
    final_down(xl).start()
    r0[s] = fo[s]
    rd0[xl] = fd0[xl]
    for k in range(1, 8):
        final(k)[1].wait_recv()
    final_down(1 - xl).wait_recv()

    s0[...] = r0[...].astype(F32)
    d0[...] = rd0[...].astype(F32)
    gain_sum_one = jnp.zeros((6, 1), F32)
    gain_sum_two = jnp.zeros((6, 1), F32)
    for b in range(8):
        lanes = pl.ds(b * 384, 384)
        half = pl.ds((b % 2) * 384, 384)
        h_gate, h_up, h_attn = s0[b, 0:6], s0[b, 8:14], s0[b, 16:22]
        gg_o[:, lanes] = h_gate * gain_two
        gu_o[:, lanes] = h_up * gain_two
        gain_sum_two += jnp.sum(h_gate * w_gate[:, lanes].astype(F32), axis=1, keepdims=True)
        gain_sum_two += jnp.sum(h_up * w_up[:, lanes].astype(F32), axis=1, keepdims=True)
        if b < 6:
            (gq_o, gk_o, gv_o)[b // 2][:, half] = h_attn * gain_one
            raw = (w_query, w_key, w_value)[b // 2][:, half].astype(F32)
            gain_sum_one += jnp.sum(h_attn * raw, axis=1, keepdims=True)
        else:
            go_o[:, half] = h_attn
    for b in range(2):
        gd_o[:, b * 384 : (b + 1) * 384] = d0[b, 0:24]
    ga1_o[...] = gain_sum_one
    ga2_o[...] = gain_sum_two

    for k in range(1, 8):
        final(k)[0].wait_send()
    final_down(xl).wait_send()
    for to in range(0, 7):
        pl.when(to < s)(lambda to=to: grad_out(to).wait_send())
    for i in range(6):
        for k in range(4):
            share(i, k).wait_send()
        for left in (3, 2, 1):
            for k in (1, 2, 3):
                hop(i, left, k).wait_send()


VMEM_SPEC = pl.BlockSpec(memory_space=pltpu.VMEM)
SMEM_SPEC = pl.BlockSpec(memory_space=pltpu.SMEM)
DMA = pltpu.SemaphoreType.DMA
REGULAR = pltpu.SemaphoreType.REGULAR


def layer(lens, gains, *arrays):
    outs = [
        ((128, 768), BF16), ((128, 768), F32), ((6, 1), F32),
        ((6, 768), F32), ((6, 768), F32), ((6, 768), F32), ((6, 768), F32),
        ((6, 1), F32), ((6, 3072), F32), ((6, 3072), F32), ((24, 768), F32),
    ]
    scratch = [(w, BF16) for w in W_SHAPES] * 2
    scratch += [
        ((8, 128, 768), BF16), ((768, 1024), BF16), ((8, 32, 384), BF16), ((2, 32, 384), BF16),
        ((8, 32, 384), F32), ((2, 32, 384), F32),
        ((6, 1024, 128), BF16), ((6, 1024, 128), BF16), ((6, 256, 128), BF16), ((6, 1024, 256), BF16),
        ((128, 768), BF16), ((128, 768), F32), ((128, 768), F32), ((128, 768), F32), ((128, 768), F32), ((128, 768), BF16),
        ((1024, 128), F32), ((1024, 128), F32), ((1024, 128), F32), ((8, 128, 768), BF16),
        ((8, 32, 384), BF16), ((2, 32, 384), BF16),
    ]
    for i in range(6):
        kept_dims = tuple(SIZES[n] for n in kept(ITEMS[i][3], ITEMS[i][2][:1]))
        scratch.append(((3,) + kept_dims + (48, ITEMS[i][4]), BF16))
    scratch += [((3, 3, 48, 128), BF16), ((3, 3, 48, 384), BF16)]
    copies = [
        DMA((7,)), DMA((7,)), DMA, DMA, DMA((8,)), DMA((8,)),
        DMA((6, 3, 3)), DMA((6, 3, 3)), DMA((6, 4)), DMA((6, 4)),
    ]
    return pl.pallas_call(
        layer_kernel,
        out_shape=[jax.ShapeDtypeStruct(shape, kind) for shape, kind in outs],
        in_specs=[SMEM_SPEC] * 2 + [VMEM_SPEC] * 9,
        out_specs=[VMEM_SPEC] * len(outs),
        scratch_shapes=[pltpu.VMEM(shape, kind) for shape, kind in scratch] + copies + copies + [REGULAR, REGULAR],
        compiler_params=pltpu.CompilerParams(collective_id=0, has_side_effects=True, vmem_limit_bytes=VMEM_LIMIT),
        name="layer",
    )(lens, gains, *arrays)


def per_device(tokens, doc_lengths, attn_gain, w_query, w_key, w_value, w_out, mlp_gain, w_gate, w_up, w_down, cotangent):
    gains = jnp.stack([attn_gain, mlp_gain]).astype(F32)
    out = layer(
        doc_lengths, gains, tokens[0], cotangent[0], w_query, w_key, w_value, w_out, w_gate, w_up, w_down
    )
    return (out[0][None], out[1][None], out[2][:, 0]) + tuple(out[3:7]) + (out[7][:, 0],) + tuple(out[8:])


def solution(mesh):
    rows = P(("fsdp", "seq"), None)
    gain = P(("fsdp", "seq"))
    toks = P("fsdp", "seq", None)
    return jax.shard_map(
        per_device,
        mesh=mesh,
        in_specs=(toks, P("fsdp", None), gain, rows, rows, rows, rows, gain, rows, rows, rows, toks),
        out_specs=(toks, toks, gain, rows, rows, rows, rows, gain, rows, rows, rows),
        check_vma=False,
    )
```

time: 4180 us -> 198 us (0.05)
  waiting for transfers between devices: 2180 us -> 0 us
  blocking collectives: 1140 us -> 0 us
  starting transfers between devices: 510 us -> 0 us
  local copies, waits for them, and re-layouts: 219 us -> 8.09 us
  Pallas kernels: 0 us -> 185 us
  matrix products: 80 us -> 0 us
    all_gather x9 -> x0, waiting for transfers between devices: 2110 us -> none  [the longest x1 310 us: per_device(): lax.all_gather(w_gate, ('fsdp', 'seq'), axis=0, tiled=True)]
    unnamed x3 -> x0, blocking collectives: 1140 us -> none
    unnamed x194 -> x0, starting transfers between devices: 510 us -> none
    unnamed x393 -> x29, local copies, waits for them, and re-layouts: 214 us -> 8.09 us
    pallas_call x0 -> x1, Pallas kernels: none -> 185 us  [layer(): pl.pallas_call(layer_kernel, out_shape=[jax.ShapeDtypeStruct(shape, kind)...]
    dot_general x27 -> x0, matrix products: 80 us -> none  [product(): return jnp.einsum(form, left, right, preferred_element_type=jnp.float32)]
    unnamed x206 -> x0, waiting for transfers between devices: 70.6 us -> none
  transfers between devices with their start and end apart: 204 -> 0, of which waited for: 14 -> 0; matrix products, arithmetic and copies ran while one was open for 31% -> 0% of each run, Pallas kernels for 0% -> 0%
where the time goes in v2:
time: 198 us; the launch traced here: 197 us
  Pallas kernels  185 us (93%)
  local copies, waits for them, and re-layouts  8.09 us (4%)
  other arithmetic  3.22 us (2%)
    pallas_call x1, Pallas kernels, layer(): pl.pallas_call(layer_kernel, out_shape=[jax.ShapeDtypeStruct(shape, kind)...  185 us
    unnamed x29, local copies, waits for them, and re-layouts  8.09 us

profile of v2, /device:TPU:1, one launch (start us, length us, event | category | flops | bytes accessed | tf_op | source)
XLA Modules:
  0.0 197.4 jit_solution(12206820653376123751)
XLA Ops:
  0.6 0.0 copy-start.8
  0.7 0.0 copy-start.9
  0.7 0.6 copy-done.8
  1.3 0.0 copy-done.9
  1.3 0.6 maximum_convert_fusion.gains
  1.9 185.4 %layer.1 = (bf16[128,768]{1,0:T(8,128)(2,1)}, f32[128,768]{1,0:T(8,128)}, f32[6,1]{1,0:T(8,128)}, f32[6,768]{1,0:T(8,128)}, f32[6,768]{1,0:T(8,128)}, /*index=5*...) custom-call(s32[1,4]{1,0:T(1,128)} %lens.1, ...), custom_call_target="tpu_custom_call" | custom-call | tf_op jit(solution)/shard_map/layer/pallas_call | solution.py:722
  187.3 0.0 copy-start
  187.3 1.4 reduce
  188.7 1.3 reduce.1
  190.0 1.6 copy.32
  191.6 0.7 copy.33
  192.3 0.0 copy-done.7
  192.3 0.6 copy.34
  193.0 0.0 copy-done.6
  193.0 0.6 copy.35
  193.6 0.6 copy.36
  194.2 0.1 copy-done.4
  194.3 0.6 copy.37
  194.9 0.0 copy-done.2
  194.9 0.6 copy.38
  195.6 0.3 copy-done.1
  195.9 0.6 copy.39
  196.5 0.3 copy-done.3
  196.8 0.6 copy.40
  (9 shorter events, 0.0 us)
Async XLA Ops:
  0.6 0.7 copy-start.8
  0.7 0.7 copy-start.9
  187.3 4.3 %copy-start = (f32[128,768]{1,0:T(8,128)S(1)}, f32[128,768]{1,0:T(8,128)}, u32[]{:S(2)}) copy-start(f32[128,768]{1,0:T(8,128)} %get-tuple-element.23) | copy-start | bytes 1179652
  191.6 0.8 copy-start.7
  191.6 1.4 copy-start.6
  191.6 2.0 %copy-start.5 = (f32[6,768]{1,0:T(8,128)S(1)}, f32[6,768]{1,0:T(8,128)}, u32[]{:S(2)}) copy-start(f32[6,768]{1,0:T(8,128)} %get-tuple-element.49) | copy-start | bytes 55300
  192.3 2.6 %copy-start.2 = (f32[6,3072]{1,0:T(8,128)S(1)}, f32[6,3072]{1,0:T(8,128)}, u32[]{:S(2)}) copy-start(f32[6,3072]{1,0:T(8,128)} %get-tuple-element.52) | copy-start | bytes 221188
  193.6 0.7 copy-start.4
  194.9 0.9 copy-start.1
  195.9 0.9 copy-start.3

commit v3 on v2

v3 whole, which is shorter than its diff:
```python
import math

import jax
import jax.numpy as jnp
from jax import lax
from jax.experimental import pallas as pl
from jax.experimental.pallas import tpu as pltpu
from jax.sharding import PartitionSpec as P

HEADS = 12
HEAD_DIM = 64
EPSILON = 1e-05
ROPE_BASE = 10000.0
MASKED_SCORE = -1e30
VMEM_LIMIT = 62 * 2**20
MESH = pl.DeviceIdType.MESH
BF16 = jnp.bfloat16
F32 = jnp.float32

WIDE = ("y", "xl", "xh", "z")
TALL = ("xl", "xh", "z", "y")
SIZES = {"y": 4, "xl": 2, "xh": 2, "z": 4, "c": 2}
ORDERS = (("y", "z", "x"), ("z", "x", "y"), ("x", "y", "z"))
ITEMS = (
    (0, (0,), (), ORDERS[0], WIDE, (48, 128)),
    (0, (1,), (), ORDERS[1], WIDE, (48, 128)),
    (0, (2,), (), ORDERS[2], WIDE, (48, 128)),
    (1, (), (), ORDERS[0], WIDE, (96, 128)),
    (2, (), (), ORDERS[1], WIDE, (96, 128)),
    (3, (), (), ORDERS[2], TALL, (32, 384)),
    (4, (), (0,), ORDERS[0], WIDE, (48, 128)),
    (4, (), (1,), ORDERS[1], WIDE, (48, 128)),
    (5, (), (), ORDERS[2], TALL, (16, 384)),
)
W_SHAPES = (
    (3, 4, 2, 2, 4, 2, 48, 128),
    (4, 2, 2, 4, 96, 128),
    (4, 2, 2, 4, 96, 128),
    (2, 2, 4, 4, 32, 384),
    (4, 2, 2, 4, 2, 48, 128),
    (2, 2, 4, 4, 16, 384),
)


def place():
    f = lax.axis_index("fsdp")
    s = lax.axis_index("seq")
    return {"x": (f // 8) * 2 + s % 2, "y": s // 2, "z": (f // 2) % 4, "c": f % 2}


def device(at):
    return ((at["x"] // 2) * 8 + at["z"] * 2 + at["c"], at["y"] * 2 + at["x"] % 2)


def shifted(at, axis, k):
    return {**at, axis: (at[axis] + k) % SIZES.get(axis, 4)}


def select(names, fixed):
    index = []
    for n in names:
        if n in ("xl", "xh"):
            v = fixed.get("x")
            index.append(pl.ds(0, 2) if v is None else (v % 2 if n == "xl" else v // 2))
        else:
            v = fixed.get(n)
            index.append(pl.ds(0, SIZES[n]) if v is None else v)
    return tuple(index)


def expand(axes):
    return [n for a in axes for n in (("xl", "xh") if a == "x" else (a,))]


def kept(names, axes):
    some = expand(axes)
    return tuple(n for n in names if n in some)


def remote(src, dst, send, recv, to):
    return pltpu.make_async_remote_copy(
        src_ref=src, dst_ref=dst, send_sem=send, recv_sem=recv, device_id=to, device_id_type=MESH
    )


def greet(at):
    f = lax.axis_index("fsdp")
    s = lax.axis_index("seq")
    bar = pltpu.get_barrier_semaphore()
    peers = [(f, (s + k) % 8) for k in range(1, 8)]
    peers += [(f + 1 - 2 * (f % 2), (s + k) % 8) for k in range(8)]
    peers += [device(shifted(at, "z", k)) for k in (1, 2, 3)]
    peers += [device({**at, "x": (at["x"] + 2) % 4})]
    peers += [device({**at, "x": (at["x"] // 2 * 2 + 2) % 4 + (1 - at["x"] % 2)})]
    for p in peers:
        pl.semaphore_signal(bar, inc=1, device_id=p, device_id_type=MESH)
    pl.semaphore_wait(bar, len(peers))


def one_hot(rows, slots, per, size, offset, flip=False):
    shape = (slots * size, rows) if flip else (rows, slots * size)
    i = lax.broadcasted_iota(jnp.int32, shape, 1 if flip else 0)
    j = lax.broadcasted_iota(jnp.int32, shape, 0 if flip else 1)
    return (j == (i // per) * size + offset + i % per).astype(BF16)


def units(core, up, flip=False):
    i = lax.broadcasted_iota(jnp.int32, (384, 384), 1 if flip else 0)
    j = lax.broadcasted_iota(jnp.int32, (384, 384), 0 if flip else 1)
    y, r = (i % 192) // 48, i % 48
    early = y * 32 + r + (128 if up else 0)
    late = y * 16 + r - 32 + (320 if up else 256)
    return ((i // 192 == core) & (j == jnp.where(r < 32, early, late))).astype(BF16)


def nn(a, b):
    return jnp.dot(a, b, preferred_element_type=F32)


def nt(a, b):
    return lax.dot_general(a, b, (((1,), (1,)), ((), ())), preferred_element_type=F32)


def tn(a, b):
    return lax.dot_general(a, b, (((0,), (0,)), ((), ())), preferred_element_type=F32)


def norm_factor(values):
    return lax.rsqrt(jnp.mean(values * values, axis=-1, keepdims=True) + EPSILON)


def norm_back(values, factor, e):
    return factor * e - values * (factor * factor * factor * jnp.mean(e * values, axis=-1, keepdims=True))


def swap_halves(v):
    lane = lax.broadcasted_iota(jnp.int32, v.shape, 1)
    return jnp.where(lane % 64 < 32, pltpu.roll(v, 96, 1), pltpu.roll(v, 32, 1))


def digits(names, n):
    out = {}
    for name in reversed(names):
        out[name] = n % SIZES[name]
        n = n // SIZES[name]
    return out


def full_index(names, fixed, free, n):
    got = digits(free, n)
    index = []
    for name in names:
        if name in free:
            index.append(got[name])
        elif name in ("xl", "xh"):
            index.append(fixed["x"] % 2 if name == "xl" else fixed["x"] // 2)
        else:
            index.append(fixed[name])
    return tuple(index)


def count(names):
    return math.prod(SIZES[n] for n in names)


def layer_kernel(
    lens, gains, tok, cot, w_query, w_key, w_value, w_out, w_gate, w_up, w_down,
    out_o, in_o, ga1_o, gq_o, gk_o, gv_o, go_o, ga2_o, gg_o, gu_o, gd_o,
    wa, wg, wu, wd, wm, we, ga, gg, gu, gd, gm, ge,
    xa, xat, r0, rd0, s0, d0, s0b, d0b, ks, vs, qs, ps, att, hid, dhid, dqs, cosine, sine, bias, rdn,
    v2s, cs, oacc, eacc, osum, esum, ra, *rest
):
    at = place()
    f = lax.axis_index("fsdp")
    s = lax.axis_index("seq")
    t3, t2, t1 = rest[:9], rest[9:18], rest[18:27]
    sem0s, sem0r, semds, semdr, semxs, semxr, sems, semr, semcs, semcr, semps, sempr = rest[27:39]
    bem0s, bem0r, bemds, bemdr, bems, bemr, bemcs, bemcr = rest[39:]
    weights = (wa, wg, wu, wd, wm, we)
    grads = (ga, gg, gu, gd, gm, ge)
    sibling = device(shifted(at, "c", 1))
    xl = at["x"] % 2
    beside = (f, at["y"] * 2 + 1 - xl)
    small, early, late = (0, 1, 2), (5, 3, 4), (8, 6, 7)
    large = early + late

    row = lax.broadcasted_iota(jnp.int32, (6, 1), 0)

    def gain_column(which):
        col = jnp.zeros((6, 1), F32)
        for r in range(6):
            col = jnp.where(row == r, gains[which, r], col)
        return col

    gain_one, gain_two = gain_column(0), gain_column(1)
    inputs = tok[...].astype(F32)
    factor_one = norm_factor(inputs)
    xa[s] = (inputs * factor_one).astype(BF16)
    cs[at["c"]] = cot[...]
    s0[...] = jnp.zeros_like(s0)
    d0[...] = jnp.zeros_like(d0)
    for b in range(8):
        lanes = pl.ds(b * 384, 384)
        half = pl.ds((b % 2) * 384, 384)
        s0[0, b, 0:6] = w_gate[:, lanes].astype(F32) * gain_two
        s0[1, b, 0:6] = w_up[:, lanes].astype(F32) * gain_two
        if b < 6:
            s0[2, b, 0:6] = (w_query, w_key, w_value)[b // 2][:, half].astype(F32) * gain_one
        else:
            s0[2, b, 0:6] = w_out[:, half].astype(F32)
    for b in range(2):
        d0[b, 0:24] = w_down[:, b * 384 : (b + 1) * 384].astype(F32)
    d0b[...] = d0[...].astype(BF16)
    gate_rows = s0[0].reshape(64, 384).astype(BF16)
    up_rows = s0[1].reshape(64, 384).astype(BF16)
    for core in range(2):
        rows = nn(gate_rows, units(core, False)) + nn(up_rows, units(core, True))
        s0b[core] = jnp.concatenate([rows.reshape(8, 8, 384), s0[2]], axis=1).astype(BF16)

    greet(at)

    def group(k, src, dst, sends, recvs):
        me = at["c"] * 8 + s
        to, frm = (me + k) % 16, (me - k + 16) % 16
        peer = (f - at["c"] + to // 8, to % 8)
        send, recv = sends.at[k - 1], recvs.at[k - 1]
        out = remote(src.at[to // 8, to % 8], dst.at[me], send, recv, peer)
        inn = remote(src.at[to // 8, to % 8], dst.at[frm], send, recv, peer)
        return out, inn

    def first(k):
        return group(k, s0b, r0, sem0s, sem0r)

    def swap(buf, n):
        c = at["c"]
        return remote(buf.at[c], buf.at[c], semps.at[n], sempr.at[n], sibling)

    def swapped(buf, n):
        c = at["c"]
        return remote(buf.at[c], buf.at[1 - c], semps.at[n], sempr.at[n], sibling)

    def down_copy(slot):
        return remote(d0b.at[1 - xl], rd0.at[slot], semds, semdr, beside)

    def token_out(to):
        return remote(xa.at[s], xa.at[s], semxs.at[to], semxr.at[s], (f, to))

    def token_in(frm):
        return remote(xa.at[frm], xa.at[frm], semxs.at[frm], semxr.at[frm], (f, frm))

    for k in range(1, 16):
        first(k)[0].start()
    down_copy(xl).start()
    swap(cs, 0).start()
    r0[at["c"] * 8 + s] = s0b[at["c"], s]
    rd0[xl] = d0b[xl]

    def cored(i, core):
        return (core,) if i < 3 else ()

    def block(i, fixed, core):
        array, lead, tail, _, names, _ = ITEMS[i]
        return weights[array].at[lead + select(names, fixed) + cored(i, core) + tail]

    def put(i, value):
        array, lead, tail, _, names, _ = ITEMS[i]
        weights[array][lead + select(names, at) + cored(i, at["c"]) + tail] = value

    def ring(i, phase, k):
        order = ITEMS[i][3]
        axis = order[phase]
        fixed = {n: at[n] for n in ("x", "y", "z") if n not in order[:phase]}
        theirs = {**fixed, axis: (at[axis] - k + 4) % 4}
        to = device(shifted(at, axis, k))
        mine, other = block(i, fixed, at["c"]), block(i, theirs, at["c"])
        send, recv = sems.at[i, phase, k - 1], semr.at[i, phase, k - 1]
        return remote(mine, mine, send, recv, to), remote(other, other, send, recv, to)

    def across(i, k):
        axis = ITEMS[i][3][2]
        where = {axis: (at[axis] - k + 4) % 4}
        mine, other = block(i, where, at["c"]), block(i, where, 1 - at["c"])
        send, recv = semcs.at[i, k], semcr.at[i, k]
        return remote(mine, mine, send, recv, sibling), remote(other, other, send, recv, sibling)

    def start(items, phase):
        for k in (1, 3, 2):
            for i in items:
                ring(i, phase, k)[0].start()

    def arrive(items, phase):
        for k in (1, 3, 2):
            for i in items:
                ring(i, phase, k)[1].wait_recv()

    for k in range(1, 16):
        first(k)[1].wait_recv()
    flat = r0[...].reshape(256, 384)
    piece = nn(one_hot(48, 16, 6, 16, at["c"] * 128 + 8), flat).astype(BF16)
    for j in range(3):
        put(j, piece[:, j * 128 : (j + 1) * 128])
    start(small, 0)
    piece = nn(one_hot(96, 16, 6, 16, 0), flat).astype(BF16)
    put(3, piece[:, :128])
    put(4, piece[:, 128:256])
    put(6, piece[:48, 256:])
    put(7, piece[48:, 256:])
    down_copy(1 - xl).wait_recv()
    piece = nn(one_hot(48, 2, 24, 32, 0), rd0[...].reshape(64, 384)).astype(BF16)
    put(5, piece[:32])
    put(8, piece[32:])
    start(large, 0)
    arrive(small, 0)
    start(small, 1)
    arrive(large, 0)
    start(large, 1)

    ends = [lens[0, 0], lens[0, 0] + lens[0, 1], lens[0, 0] + lens[0, 1] + lens[0, 2]]
    freq_lane = (lax.broadcasted_iota(jnp.int32, (1, 128), 1) % 32).astype(F32)
    freqs = jnp.exp(freq_lane * (-2.0 * math.log(ROPE_BASE) / HEAD_DIM))
    lane = lax.broadcasted_iota(jnp.int32, (128, 128), 1)

    def segment_of(index):
        return sum((index >= e).astype(jnp.int32) for e in ends)

    def table(u, carry):
        index = u * 128 + lax.broadcasted_iota(jnp.int32, (128, 1), 0)
        begin = jnp.zeros_like(index)
        for e in ends:
            begin = jnp.where(index >= e, e, begin)
        angle = (index - begin).astype(F32) * freqs
        rows = pl.ds(pl.multiple_of(u * 128, 128), 128)
        cosine[rows, :] = jnp.cos(angle)
        sine[rows, :] = jnp.where(lane % 64 < 32, -1.0, 1.0) * jnp.sin(angle)
        mine = s * 128 + lax.broadcasted_iota(jnp.int32, (1, 128), 1)
        allowed = (segment_of(index) == segment_of(mine)) & (index <= mine)
        bias[rows, :] = jnp.where(allowed, 0.0, MASKED_SCORE)
        return carry

    lax.fori_loop(0, 8, table, 0)

    arrive(small, 1)
    start(small, 2)
    for i in small:
        across(i, 0)[0].start()
    for to in range(1, 8):
        pl.when(to > s)(lambda to=to: token_out(to).start())
    arrive(large, 1)
    start(early, 2)
    start(late, 2)
    for u in range(1, 8):

        def clear(u=u):
            xa[u] = jnp.zeros((128, 768), BF16)

        pl.when(u > s)(clear)
    for frm in range(0, 7):
        pl.when(frm < s)(lambda frm=frm: token_in(frm).wait_recv())

    def transpose_tokens(u, carry):
        xat[:, pl.ds(pl.multiple_of(u * 128, 128), 128)] = xa[u].T
        return carry

    lax.fori_loop(0, 8, transpose_tokens, 0)
    for k in (1, 3, 2):
        for i in small:
            ring(i, 2, k)[1].wait_recv()
            across(i, k)[0].start()
    for k in range(4):
        for i in small:
            across(i, k)[1].wait_recv()

    for k in range(1, 16):
        first(k)[0].wait_send()
    down_copy(xl).wait_send()
    for to in range(1, 8):
        pl.when(to > s)(lambda to=to: token_out(to).wait_send())

    mine = pl.ds(pl.multiple_of(s * 128, 128), 128)
    cos_mine, sin_mine = cosine[mine, :], sine[mine, :]
    left = lax.broadcasted_iota(jnp.int32, (128, 128), 1) < 64

    def attn_weight(kind, p):
        return wa[p % 3, kind, p // 3].reshape(768, 128)

    def attn_full(kind):
        return jnp.concatenate([attn_weight(kind, p) for p in range(6)], axis=1)

    def stacked(v):
        zero = jnp.zeros_like(v)
        return jnp.concatenate([jnp.where(left, v, zero), jnp.where(left, zero, v)], axis=0)

    def unstacked(v):
        return jnp.concatenate([v[:64, :128], v[64:, 128:]], axis=0).T

    def pair_lanes(p):
        return pl.ds(pl.multiple_of(p * 128, 128), 128)

    def attend(p, carry):
        tokens_all = xa[...].reshape(1024, 768)
        w_kv = jnp.concatenate([attn_weight(1, p), attn_weight(2, p)], axis=1)
        kv = nn(tokens_all, w_kv)
        k_raw = kv[:, :128]
        k = (k_raw * cosine[...] + swap_halves(k_raw) * sine[...]).astype(BF16)
        v = kv[:, 128:].astype(BF16)
        q_raw = nn(xa[s], attn_weight(0, p))
        q = ((q_raw * cos_mine + swap_halves(q_raw) * sin_mine).astype(BF16) * (1.0 / math.sqrt(HEAD_DIM))).astype(BF16)
        qq = stacked(q)
        ks[p] = k
        vs[p] = v
        qs[p] = qq
        masks = bias[...]
        scores = nt(k, qq) + jnp.concatenate([masks, masks], axis=1)
        top = jnp.max(scores, axis=0, keepdims=True)
        e = jnp.exp(scores - top)
        total = jnp.sum(e, axis=0, keepdims=True)
        probs = (e * (1.0 / total)).astype(BF16)
        ps[p] = probs
        att[:, pair_lanes(p)] = unstacked(tn(v, probs)).astype(BF16)
        return carry

    lax.fori_loop(0, 6, attend, 0)

    hidden = tok[...].astype(F32) + nn(att[...], attn_full(3))
    hid[...] = hidden
    factor_two = norm_factor(hidden)
    v2s[at["c"]] = (hidden * factor_two).astype(BF16)
    swap(v2s, 1).start()
    oacc[...] = jnp.zeros_like(oacc)
    eacc[...] = jnp.zeros_like(eacc)
    swapped(cs, 0).wait()
    swapped(v2s, 1).wait()
    v2 = v2s[...].reshape(256, 768)
    v2t = v2.T

    def pair(a, b):
        return jnp.concatenate([a, b], axis=1)

    def gated(gate, up, d_w):
        c = cs[...].reshape(256, 768)
        sig = 1.0 / (1.0 + jnp.exp(-gate))
        silu = gate * sig
        mixed = (silu * up).astype(BF16)
        oacc[...] += nn(mixed, d_w).reshape(2, 128, 768)
        d_mixed = nt(c, d_w)
        d_gate = d_mixed * up * sig * (1.0 + gate * (1.0 - sig))
        d_up = d_mixed * silu
        return d_gate, d_up, tn(mixed, c).astype(BF16)

    def feed_early(y, carry):
        g_w = pair(wg[y, 0].reshape(768, 128), wg[y, 1].reshape(768, 128))
        u_w = pair(wu[y, 0].reshape(768, 128), wu[y, 1].reshape(768, 128))
        xh, z = y // 2, (y % 2) * 2
        d_w = jnp.concatenate(
            [pair(wd[0, xh, z + b].reshape(128, 384), wd[1, xh, z + b].reshape(128, 384)) for b in range(2)], axis=0
        )
        d_gate, d_up, g_d = gated(nn(v2, g_w), nn(v2, u_w), d_w)
        d_gate, d_up = d_gate.astype(BF16), d_up.astype(BF16)
        eacc[...] += (nt(d_gate, g_w) + nt(d_up, u_w)).reshape(2, 128, 768)
        g_g = nn(v2t, d_gate).astype(BF16)
        g_u = nn(v2t, d_up).astype(BF16)
        for b in range(2):
            lanes = slice(b * 128, (b + 1) * 128)
            gg[y, b] = g_g[:, lanes].reshape(2, 4, 96, 128)
            gu[y, b] = g_u[:, lanes].reshape(2, 4, 96, 128)
            for h in range(2):
                gd[h, xh, z + b] = g_d[lanes, h * 384 : (h + 1) * 384].reshape(4, 32, 384)
        return carry

    def feed_late(y, carry):
        w = pair(wm[y, 0].reshape(768, 128), wm[y, 1].reshape(768, 128))
        xh, z = y // 2, (y % 2) * 2
        d_w = jnp.concatenate(
            [pair(we[0, xh, z + b].reshape(64, 384), we[1, xh, z + b].reshape(64, 384)) for b in range(2)], axis=0
        )
        both = nn(v2, w)
        low = lax.broadcasted_iota(jnp.int32, (256, 128), 1) < 64

        def mix(a, b):
            return jnp.where(low, a, pltpu.roll(b, 64, 1)), jnp.where(low, pltpu.roll(a, 64, 1), b)

        gate, up = mix(both[:, :128], both[:, 128:])
        d_gate, d_up, g_d = gated(gate, up, d_w)
        d_both = pair(*mix(d_gate, d_up)).astype(BF16)
        eacc[...] += nt(d_both, w).reshape(2, 128, 768)
        g = nn(v2t, d_both).astype(BF16)
        for b in range(2):
            gm[y, b] = g[:, b * 128 : (b + 1) * 128].reshape(2, 4, 2, 48, 128)
            for h in range(2):
                ge[h, xh, z + b] = g_d[b * 64 : (b + 1) * 64, h * 384 : (h + 1) * 384].reshape(4, 16, 384)
        return carry

    def home(i):
        array, lead, tail = ITEMS[i][:3]
        return (ra, lead, ()) if i < 3 else (grads[array], lead, tail)

    def home_at(i, index):
        ref, lead, tail = home(i)
        return ref.at[lead + index + tail]

    def share(i, k):
        axis = ITEMS[i][3][2]
        where = select(ITEMS[i][4], {axis: (at[axis] + k) % 4})
        part = ga.at[ITEMS[i][1] + where + (1 - at["c"],)]
        return remote(part, home_at(i, where), bemcs.at[i, k], bemcr.at[i, k], sibling)

    def hop(i, left, k):
        order, names = ITEMS[i][3:5]
        axis = order[left - 1]
        fixed = {a: at[a] for a in order[left:]}
        src = home_at(i, select(names, {**fixed, axis: (at[axis] + k) % 4}))
        dst = (t1, t2, t3)[left - 1][i].at[k - 1]
        send, recv = bems.at[i, left - 1, k - 1], bemr.at[i, left - 1, k - 1]
        return remote(src, dst, send, recv, device(shifted(at, axis, k)))

    def add_core(i, k):
        order, names = ITEMS[i][3:5]
        free = kept(names, order[:2])
        axis = order[2]
        fixed = {axis: (at[axis] + k) % 4}

        def body(n, carry):
            index = ITEMS[i][1] + full_index(names, fixed, free, n)
            ra[index] = (ra[index].astype(F32) + ga[index + (at["c"],)].astype(F32)).astype(BF16)
            return carry

        lax.fori_loop(0, count(free), body, 0, unroll=4)

    def add_ring(i, left):
        order, names = ITEMS[i][3:5]
        free = kept(names, order[: left - 1])
        fixed = {a: at[a] for a in order[left - 1 :]}
        ref, lead, tail = home(i)
        came = (t1, t2, t3)[left - 1][i]

        def body(n, carry):
            index = lead + full_index(names, fixed, free, n) + tail
            total = ref[index].astype(F32)
            for k in range(3):
                total = total + came[(k,) + full_index(free, {}, free, n)].astype(F32)
            ref[index] = total.astype(BF16)
            return carry

        lax.fori_loop(0, count(free), body, 0, unroll=4)

    def hop_start(items, left):
        for k in (1, 3, 2):
            for i in items:
                hop(i, left, k).start()

    def hop_on(i, left):
        for k in (1, 3, 2):
            hop(i, left, k).wait_recv()
        add_ring(i, left)
        hop_start((i,), left - 1)

    def last(i):
        for k in (1, 3, 2):
            hop(i, 1, k).wait_recv()
        ref, lead, tail = home(i)
        total = ref[lead + select(ITEMS[i][4], at) + tail].astype(F32)
        for k in range(3):
            total = total + t1[i][k].astype(F32)
        return total.astype(BF16)

    def sent(items):
        for i in items:
            for phase in range(3):
                for k in (1, 2, 3):
                    ring(i, phase, k)[0].wait_send()
            if i < 3:
                for k in range(4):
                    across(i, k)[0].wait_send()

    arrive(early, 2)
    lax.fori_loop(0, 4, feed_early, 0)
    sent(large)
    hop_start(early, 3)
    arrive(late, 2)
    lax.fori_loop(0, 4, feed_late, 0)
    sum_o = remote(oacc.at[1 - at["c"]], osum, semps.at[2], sempr.at[2], sibling)
    sum_e = remote(eacc.at[1 - at["c"]], esum, semps.at[3], sempr.at[3], sibling)
    sum_e.start()
    sum_o.start()
    hop_start(late, 3)
    sum_e.wait()

    hidden = hid[...]
    factor_two = norm_factor(hidden)
    d_hidden = cot[...].astype(F32) + norm_back(hidden, factor_two, eacc[at["c"]] + esum[...])
    dhid[...] = d_hidden
    dh = d_hidden.astype(BF16)
    d_att = nt(dh, attn_full(3)).astype(BF16)
    att_t = att[...].T
    for j in range(2):
        g_o = nn(att_t, dh[:, j * 384 : (j + 1) * 384]).astype(BF16)
        for t in range(3):
            ga[t, 3, j] = g_o[:, t * 128 : (t + 1) * 128].reshape(2, 4, 2, 48, 128)
    att[...] = d_att

    def attend_back(p, carry):
        da = stacked(att[:, pair_lanes(p)])
        k, v, qq, probs = ks[p], vs[p], qs[p], ps[p]
        d_probs = nt(v, da)
        probs_f = probs.astype(F32)
        d_sum = jnp.sum(probs_f * d_probs, axis=0, keepdims=True)
        d_scores = (probs_f * (d_probs - d_sum)).astype(BF16)
        d_v = nn(probs, da).astype(BF16)
        d_k = nn(d_scores, qq)
        d_k = (d_k * cosine[...] - swap_halves(d_k) * sine[...]).astype(BF16)
        d_q = unstacked(tn(k, d_scores)) * (1.0 / math.sqrt(HEAD_DIM))
        d_q = (d_q * cos_mine - swap_halves(d_q) * sin_mine).astype(BF16)
        ks[p] = d_k
        vs[p] = d_v
        dqs[:, pair_lanes(p)] = d_q
        g_kv = nn(xat[...], jnp.concatenate([d_k, d_v], axis=1)).astype(BF16)
        g_q = nn(xat[:, mine], d_q).astype(BF16)
        t, h = p % 3, p // 3
        ga[t, 0, h] = g_q.reshape(2, 4, 2, 48, 128)
        ga[t, 1, h] = g_kv[:, :128].reshape(2, 4, 2, 48, 128)
        ga[t, 2, h] = g_kv[:, 128:].reshape(2, 4, 2, 48, 128)
        return carry

    def back_on(t):
        for k in (1, 3, 2, 0):
            share(t, k).wait_recv()
            add_core(t, k)
            if k:
                hop(t, 3, k).start()

    for t in range(3):

        def third_back(h, carry, t=t):
            return attend_back(t + 3 * h, carry)

        lax.fori_loop(0, 2, third_back, 0)
        for k in (1, 3, 2, 0):
            share(t, k).start()
        if t:
            back_on(t - 1)

    w_kv = jnp.concatenate([attn_full(1), attn_full(2)], axis=1)

    def tokens_back(u, carry):
        rows = pl.ds(pl.multiple_of(u * 128, 128), 128)
        d_kv = jnp.concatenate([ks[p, rows, :] for p in range(6)] + [vs[p, rows, :] for p in range(6)], axis=1)
        xa[u] = nt(d_kv, w_kv).astype(BF16)
        return carry

    lax.fori_loop(0, 8, tokens_back, 0)

    def grad_out(to):
        return remote(xa.at[to], rdn.at[s], semxs.at[to], semxr.at[s], (f, to))

    def grad_in(frm):
        return remote(xa.at[frm], rdn.at[frm], semxs.at[frm], semxr.at[frm], (f, frm))

    for to in range(0, 7):
        pl.when(to < s)(lambda to=to: grad_out(to).start())
    sum_o.wait()
    out_o[...] = (hid[...] + oacc[at["c"]] + osum[...]).astype(BF16)
    esum[...] = nt(dqs[...], attn_full(0))

    back_on(2)
    for i in early + late:
        hop_on(i, 3)
    for i in small:
        hop_on(i, 3)
    for i in early + late + small:
        hop_on(i, 2)

    esum[...] += xa[s].astype(F32)
    for frm in range(1, 8):

        def add(frm=frm):
            grad_in(frm).wait_recv()
            esum[...] += rdn[frm].astype(F32)

        pl.when(frm > s)(add)
    inputs = tok[...].astype(F32)
    in_o[...] = dhid[...] + norm_back(inputs, norm_factor(inputs), esum[...])

    down = jnp.concatenate([last(5), last(8)], axis=0)
    both = jnp.concatenate([last(3), last(4), jnp.concatenate([last(6), last(7)], axis=0)], axis=1)
    attn = jnp.concatenate([last(t) for t in small], axis=1)
    rows = nn(one_hot(96, 16, 6, 16, 0, True), both)
    rows += nn(one_hot(48, 16, 6, 16, at["c"] * 128 + 8, True), attn)
    s0b[...] = rows.astype(BF16).reshape(2, 8, 16, 384)
    d0b[...] = nn(one_hot(48, 2, 24, 32, 0, True), down).astype(BF16).reshape(2, 32, 384)

    def final(k):
        return group(k, s0b, r0, bem0s, bem0r)

    def final_down(slot):
        return remote(d0b.at[1 - xl], rd0.at[slot], bemds, bemdr, beside)

    for k in range(1, 16):
        final(k)[0].start()
    final_down(xl).start()
    r0[at["c"] * 8 + s] = s0b[at["c"], s]
    rd0[xl] = d0b[xl]
    for k in range(1, 16):
        final(k)[1].wait_recv()
    final_down(1 - xl).wait_recv()

    got = r0[...].reshape(2, 8, 16, 384)
    halves = [got[core, :, :8].reshape(64, 384) for core in range(2)]
    for which in range(2):
        natural = nn(halves[0], units(0, which == 1, True)) + nn(halves[1], units(1, which == 1, True))
        s0[which] = natural.reshape(8, 8, 384)
    s0[2] = r0[pl.ds(at["c"] * 8, 8), 8:, :].astype(F32)
    d0[...] = rd0[...].astype(F32)
    gain_sum_one = jnp.zeros((6, 1), F32)
    gain_sum_two = jnp.zeros((6, 1), F32)
    for b in range(8):
        lanes = pl.ds(b * 384, 384)
        half = pl.ds((b % 2) * 384, 384)
        h_gate, h_up, h_attn = s0[0, b, 0:6], s0[1, b, 0:6], s0[2, b, 0:6]
        gg_o[:, lanes] = h_gate * gain_two
        gu_o[:, lanes] = h_up * gain_two
        gain_sum_two += jnp.sum(h_gate * w_gate[:, lanes].astype(F32), axis=1, keepdims=True)
        gain_sum_two += jnp.sum(h_up * w_up[:, lanes].astype(F32), axis=1, keepdims=True)
        if b < 6:
            (gq_o, gk_o, gv_o)[b // 2][:, half] = h_attn * gain_one
            raw = (w_query, w_key, w_value)[b // 2][:, half].astype(F32)
            gain_sum_one += jnp.sum(h_attn * raw, axis=1, keepdims=True)
        else:
            go_o[:, half] = h_attn
    for b in range(2):
        gd_o[:, b * 384 : (b + 1) * 384] = d0[b, 0:24]
    ga1_o[...] = gain_sum_one
    ga2_o[...] = gain_sum_two

    for k in range(1, 16):
        final(k)[0].wait_send()
    final_down(xl).wait_send()
    for to in range(0, 7):
        pl.when(to < s)(lambda to=to: grad_out(to).wait_send())
    sent(small)
    for i in range(9):
        if i < 3:
            for k in range(4):
                share(i, k).wait_send()
        for left in (3, 2, 1):
            for k in (1, 2, 3):
                hop(i, left, k).wait_send()


VMEM_SPEC = pl.BlockSpec(memory_space=pltpu.VMEM)
SMEM_SPEC = pl.BlockSpec(memory_space=pltpu.SMEM)
DMA = pltpu.SemaphoreType.DMA


def layer(lens, gains, *arrays):
    outs = [
        ((128, 768), BF16), ((128, 768), F32), ((6, 1), F32),
        ((6, 768), F32), ((6, 768), F32), ((6, 768), F32), ((6, 768), F32),
        ((6, 1), F32), ((6, 3072), F32), ((6, 3072), F32), ((24, 768), F32),
    ]
    scratch = [(w, BF16) for w in W_SHAPES] * 2
    scratch += [
        ((8, 128, 768), BF16), ((768, 1024), BF16), ((16, 16, 384), BF16), ((2, 32, 384), BF16),
        ((3, 8, 8, 384), F32), ((2, 32, 384), F32), ((2, 8, 16, 384), BF16), ((2, 32, 384), BF16),
        ((6, 1024, 128), BF16), ((6, 1024, 128), BF16), ((6, 256, 128), BF16), ((6, 1024, 256), BF16),
        ((128, 768), BF16), ((128, 768), F32), ((128, 768), F32), ((128, 768), BF16),
        ((1024, 128), F32), ((1024, 128), F32), ((1024, 128), F32), ((8, 128, 768), BF16),
        ((2, 128, 768), BF16), ((2, 128, 768), BF16), ((2, 128, 768), F32), ((2, 128, 768), F32),
        ((128, 768), F32), ((128, 768), F32), ((3, 4, 2, 2, 4, 48, 128), BF16),
    ]
    for rings in (2, 1, 0):
        for item in ITEMS:
            left = tuple(SIZES[n] for n in kept(item[4], item[3][:rings]))
            scratch.append(((3,) + left + item[5], BF16))
    copies = [
        DMA((15,)), DMA((15,)), DMA, DMA, DMA((8,)), DMA((8,)),
        DMA((9, 3, 3)), DMA((9, 3, 3)), DMA((3, 4)), DMA((3, 4)), DMA((4,)), DMA((4,)),
        DMA((15,)), DMA((15,)), DMA, DMA, DMA((9, 3, 3)), DMA((9, 3, 3)), DMA((3, 4)), DMA((3, 4)),
    ]
    return pl.pallas_call(
        layer_kernel,
        out_shape=[jax.ShapeDtypeStruct(shape, kind) for shape, kind in outs],
        in_specs=[SMEM_SPEC] * 2 + [VMEM_SPEC] * 9,
        out_specs=[VMEM_SPEC] * len(outs),
        scratch_shapes=[pltpu.VMEM(shape, kind) for shape, kind in scratch] + copies,
        compiler_params=pltpu.CompilerParams(collective_id=0, has_side_effects=True, vmem_limit_bytes=VMEM_LIMIT),
        name="layer",
    )(lens, gains, *arrays)


def per_device(tokens, doc_lengths, attn_gain, w_query, w_key, w_value, w_out, mlp_gain, w_gate, w_up, w_down, cotangent):
    gains = jnp.stack([attn_gain, mlp_gain]).astype(F32)
    out = layer(
        doc_lengths, gains, tokens[0], cotangent[0], w_query, w_key, w_value, w_out, w_gate, w_up, w_down
    )
    return (out[0][None], out[1][None], out[2][:, 0]) + tuple(out[3:7]) + (out[7][:, 0],) + tuple(out[8:])


def solution(mesh):
    rows = P(("fsdp", "seq"), None)
    gain = P(("fsdp", "seq"))
    toks = P("fsdp", "seq", None)
    return jax.shard_map(
        per_device,
        mesh=mesh,
        in_specs=(toks, P("fsdp", None), gain, rows, rows, rows, rows, gain, rows, rows, rows, toks),
        out_specs=(toks, toks, gain, rows, rows, rows, rows, gain, rows, rows, rows),
        check_vma=False,
    )
```

time: 198 us -> 175 us (0.88)
  Pallas kernels: 185 us -> 162 us
    pallas_call x1, Pallas kernels: 185 us -> 162 us  [layer(): pl.pallas_call(layer_kernel, out_shape=[jax.ShapeDtypeStruct(shape, kind)...]
where the time goes in v3:
time: 175 us; the launch traced here: 174 us
  Pallas kernels  162 us (93%)
  local copies, waits for them, and re-layouts  8.09 us (5%)
  other arithmetic  3.22 us (2%)
    pallas_call x1, Pallas kernels, layer(): pl.pallas_call(layer_kernel, out_shape=[jax.ShapeDtypeStruct(shape, kind)...  162 us
    unnamed x29, local copies, waits for them, and re-layouts  8.09 us

profile of v3, /device:TPU:1, one launch (start us, length us, event | category | flops | bytes accessed | tf_op | source)
XLA Modules:
  0.0 174.1 jit_solution(4237955768234902947)
XLA Ops:
  0.6 0.0 copy-start.8
  0.7 0.0 copy-start.9
  0.7 0.6 copy-done.8
  1.3 0.0 copy-done.9
  1.3 0.6 maximum_convert_fusion.gains
  1.9 162.1 %layer.1 = (bf16[128,768]{1,0:T(8,128)(2,1)}, f32[128,768]{1,0:T(8,128)}, f32[6,1]{1,0:T(8,128)}, f32[6,768]{1,0:T(8,128)}, f32[6,768]{1,0:T(8,128)}, /*index=5*...) custom-call(s32[1,4]{1,0:T(1,128)} %lens.1, ...), custom_call_target="tpu_custom_call" | custom-call | tf_op jit(solution)/shard_map/layer/pallas_call | solution.py:779
  164.0 0.0 copy-start
  164.0 1.4 reduce
  165.4 1.3 reduce.1
  166.7 1.6 copy.32
  168.3 0.7 copy.33
  169.1 0.0 copy-done.7
  169.1 0.6 copy.34
  169.7 0.0 copy-done.6
  169.7 0.6 copy.35
  170.3 0.6 copy.36
  170.9 0.1 copy-done.4
  171.0 0.6 copy.37
  171.7 0.0 copy-done.2
  171.7 0.6 copy.38
  172.3 0.3 copy-done.1
  172.6 0.6 copy.39
  173.2 0.3 copy-done.3
  173.5 0.6 copy.40
  (9 shorter events, 0.0 us)
Async XLA Ops:
  0.6 0.7 copy-start.8
  0.7 0.7 copy-start.9
  164.0 4.3 %copy-start = (f32[128,768]{1,0:T(8,128)S(1)}, f32[128,768]{1,0:T(8,128)}, u32[]{:S(2)}) copy-start(f32[128,768]{1,0:T(8,128)} %get-tuple-element.23) | copy-start | bytes 1179652
  168.3 0.8 copy-start.7
  168.3 1.4 copy-start.6
  168.3 2.0 %copy-start.5 = (f32[6,768]{1,0:T(8,128)S(1)}, f32[6,768]{1,0:T(8,128)}, u32[]{:S(2)}) copy-start(f32[6,768]{1,0:T(8,128)} %get-tuple-element.49) | copy-start | bytes 55300
  169.1 2.6 %copy-start.2 = (f32[6,3072]{1,0:T(8,128)S(1)}, f32[6,3072]{1,0:T(8,128)}, u32[]{:S(2)}) copy-start(f32[6,3072]{1,0:T(8,128)} %get-tuple-element.52) | copy-start | bytes 221188
  170.3 0.7 copy-start.4
  171.7 0.9 copy-start.1
  172.6 0.9 copy-start.3

commit v4 on v3

v4 whole, which is shorter than its diff:
```python
import math

import jax
import jax.numpy as jnp
from jax import lax
from jax.experimental import pallas as pl
from jax.experimental.pallas import tpu as pltpu
from jax.sharding import PartitionSpec as P

HEADS = 12
HEAD_DIM = 64
EPSILON = 1e-05
ROPE_BASE = 10000.0
MASKED_SCORE = -1e30
VMEM_LIMIT = 62 * 2**20
MESH = pl.DeviceIdType.MESH
BF16 = jnp.bfloat16
F32 = jnp.float32

NAMES = ("y", "xl", "xh", "z")
SIZES = {"y": 4, "xl": 2, "xh": 2, "z": 4, "c": 2}
ORDERS = (("y", "z", "x"), ("z", "x", "y"), ("x", "y", "z"))
ROWS = (208, 144, 224)
FULL = (1, 0, 2)
ATTN = {0: (0, 48), 1: (0, 48), 2: (0, 48)}
EARLY = {0: (48, 96), 1: (48, 96), 2: (48, 96)}
LATE = {0: (144, 64), 2: (144, 80)}
PARTS = (ATTN, EARLY, LATE)


def place():
    f = lax.axis_index("fsdp")
    s = lax.axis_index("seq")
    return {"x": (f // 8) * 2 + s % 2, "y": s // 2, "z": (f // 2) % 4, "c": f % 2}


def device(at):
    return ((at["x"] // 2) * 8 + at["z"] * 2 + at["c"], at["y"] * 2 + at["x"] % 2)


def shifted(at, axis, k):
    return {**at, axis: (at[axis] + k) % SIZES.get(axis, 4)}


def select(names, fixed, half=None):
    index = []
    for n in names:
        size = SIZES[n]
        if half is not None and n == half[0]:
            index.append(pl.ds(half[1] * (size // 2), size // 2))
        elif n in ("xl", "xh"):
            v = fixed.get("x")
            index.append(pl.ds(0, 2) if v is None else (v % 2 if n == "xl" else v // 2))
        else:
            v = fixed.get(n)
            index.append(pl.ds(0, size) if v is None else v)
    return tuple(index)


def expand(axes):
    return [n for a in axes for n in (("xl", "xh") if a == "x" else (a,))]


def kept(names, axes):
    some = expand(axes)
    return tuple(n for n in names if n in some)


def remote(src, dst, send, recv, to):
    return pltpu.make_async_remote_copy(
        src_ref=src, dst_ref=dst, send_sem=send, recv_sem=recv, device_id=to, device_id_type=MESH
    )


def greeting(at):
    f = lax.axis_index("fsdp")
    s = lax.axis_index("seq")
    bar = pltpu.get_barrier_semaphore()
    peers = [(f, (s + k) % 8) for k in range(1, 8)]
    peers += [(f + 1 - 2 * (f % 2), (s + k) % 8) for k in range(8)]
    peers += [device(shifted(at, "z", k)) for k in (1, 2, 3)]
    peers += [device({**at, "x": (at["x"] + 2) % 4})]
    peers += [device({**at, "x": (at["x"] // 2 * 2 + 2) % 4 + (1 - at["x"] % 2)})]
    for p in peers:
        pl.semaphore_signal(bar, inc=1, device_id=p, device_id_type=MESH)
    return bar, len(peers)


def one_hot(rows, slots, per, size, offset, flip=False):
    shape = (slots * size, rows) if flip else (rows, slots * size)
    i = lax.broadcasted_iota(jnp.int32, shape, 1 if flip else 0)
    j = lax.broadcasted_iota(jnp.int32, shape, 0 if flip else 1)
    return (j == (i // per) * size + offset + i % per).astype(BF16)


def units(core, up, flip=False):
    i = lax.broadcasted_iota(jnp.int32, (384, 384), 1 if flip else 0)
    j = lax.broadcasted_iota(jnp.int32, (384, 384), 0 if flip else 1)
    y, r = (i % 192) // 48, i % 48
    early = y * 32 + r + (128 if up else 0)
    late = y * 16 + r - 32 + (320 if up else 256)
    return ((i // 192 == core) & (j == jnp.where(r < 32, early, late))).astype(BF16)


def nn(a, b):
    return jnp.dot(a, b, preferred_element_type=F32)


def nt(a, b):
    return lax.dot_general(a, b, (((1,), (1,)), ((), ())), preferred_element_type=F32)


def tn(a, b):
    return lax.dot_general(a, b, (((0,), (0,)), ((), ())), preferred_element_type=F32)


def norm_factor(values):
    return lax.rsqrt(jnp.mean(values * values, axis=-1, keepdims=True) + EPSILON)


def norm_back(values, factor, e):
    return factor * e - values * (factor * factor * factor * jnp.mean(e * values, axis=-1, keepdims=True))


def swap_halves(v):
    lane = lax.broadcasted_iota(jnp.int32, v.shape, 1)
    return jnp.where(lane % 64 < 32, pltpu.roll(v, 96, 1), pltpu.roll(v, 32, 1))


def digits(names, n):
    out = {}
    for name in reversed(names):
        out[name] = n % SIZES[name]
        n = n // SIZES[name]
    return out


def full_index(names, fixed, free, n):
    got = digits(free, n)
    index = []
    for name in names:
        if name in free:
            index.append(got[name])
        elif name in ("xl", "xh"):
            index.append(fixed["x"] % 2 if name == "xl" else fixed["x"] // 2)
        else:
            index.append(fixed[name])
    return tuple(index)


def count(names):
    return math.prod(SIZES[n] for n in names)


def layer_kernel(
    lens, gains, tok, cot, w_query, w_key, w_value, w_out, w_gate, w_up, w_down,
    out_o, in_o, rows_o, down_o,
    a0, a1, a2, w0, w1, w2, g0, g1, g2, h0, h1, h2,
    xa, xat, r0, rd0, s0, d0, s0b, d0b, ks, vs, qs, ps, att, hid, dhid, dqs, cosine, sine, bias, rdn,
    v2s, cs, oacc, eacc, osum, esum, rdc, toks, out_s, in_s, lens_out, lens_in, *rest
):
    at = place()
    f = lax.axis_index("fsdp")
    s = lax.axis_index("seq")
    xl = at["x"] % 2
    here = at["y"] * 2 + at["c"]
    stays = at["c"] == xl
    partner = (f - at["c"] + xl, here)
    t3, t2, t1 = rest[:3], rest[3:6], rest[6:9]
    sem0s, sem0r, semds, semdr, semxs, semxr, sems, semr, semls, semlr, semcs, semcr, semps, sempr = rest[9:23]
    bem0s, bem0r, bemds, bemdr, bems, bemr, bemls, bemlr, bemcs, bemcr = rest[23:33]
    semms, semmr, semys, semyr, semzs, semzr, semws, semwr = rest[33:]
    attn_weights = (a0, a1, a2)
    weights = (w0, w1, w2)
    own_grads = (g0, g1, g2)
    homes = (h0, h1, h2)
    sibling = device(shifted(at, "c", 1))
    xl = at["x"] % 2
    beside = (f, at["y"] * 2 + 1 - xl)
    bar, others = greeting(at)
    row = lax.broadcasted_iota(jnp.int32, (6, 1), 0)

    def gain_column(which):
        col = jnp.zeros((6, 1), F32)
        for r in range(6):
            col = jnp.where(row == r, gains[which, r], col)
        return col

    gain_one, gain_two = gain_column(0), gain_column(1)
    for r in range(4):
        lens_out[r : r + 1] = jnp.full((1, 128), lens[0, r], jnp.int32).astype(F32)
    lens_out[4:8] = jnp.zeros((4, 128), F32)
    s0[...] = jnp.zeros_like(s0)
    d0[...] = jnp.zeros_like(d0)
    for b in range(8):
        lanes = pl.ds(b * 384, 384)
        half = pl.ds((b % 2) * 384, 384)
        s0[0, b, 0:6] = w_gate[:, lanes].astype(F32) * gain_two
        s0[1, b, 0:6] = w_up[:, lanes].astype(F32) * gain_two
        if b < 6:
            s0[2, b, 0:6] = (w_query, w_key, w_value)[b // 2][:, half].astype(F32) * gain_one
        else:
            s0[2, b, 0:6] = w_out[:, half].astype(F32)
    for b in range(2):
        d0[b, 0:24] = w_down[:, b * 384 : (b + 1) * 384].astype(F32)
    d0b[...] = d0[...].astype(BF16)
    gate_rows = s0[0].reshape(64, 384).astype(BF16)
    up_rows = s0[1].reshape(64, 384).astype(BF16)
    for core in range(2):
        rows = nn(gate_rows, units(core, False)) + nn(up_rows, units(core, True))
        s0b[core] = jnp.concatenate([rows.reshape(8, 8, 384), s0[2]], axis=1).astype(BF16)

    pl.semaphore_wait(bar, others)

    def group(k, src, dst, sends, recvs):
        me = at["c"] * 8 + s
        to, frm = (me + k) % 16, (me - k + 16) % 16
        peer = (f - at["c"] + to // 8, to % 8)
        send, recv = sends.at[k - 1], recvs.at[k - 1]
        out = remote(src.at[to // 8, to % 8], dst.at[me], send, recv, peer)
        inn = remote(src.at[to // 8, to % 8], dst.at[frm], send, recv, peer)
        return out, inn

    def first(k):
        return group(k, s0b, r0, sem0s, sem0r)

    def swap(buf, n):
        c = at["c"]
        return remote(buf.at[c], buf.at[c], semps.at[n], sempr.at[n], sibling)

    def swapped(buf, n):
        c = at["c"]
        return remote(buf.at[c], buf.at[1 - c], semps.at[n], sempr.at[n], sibling)

    def down_copy(slot):
        return remote(d0b.at[1 - xl], rd0.at[slot], semds, semdr, beside)

    def moves(n):
        src = (tok, cot, lens_out)[n]
        dst = (toks, cs.at[xl], lens_in)[n]
        return remote(src, dst, semms.at[n], semmr.at[n], partner)

    def token_out(y):
        return remote(xa.at[here], xa.at[here], semxs.at[y], semxr.at[at["y"]], (f, y * 2 + xl))

    def token_in(y):
        block = xa.at[y * 2 + at["c"]]
        return remote(block, block, semxs.at[y], semxr.at[y], (f, y * 2 + xl))

    def token_across(y):
        mine, other = xa.at[y * 2 + at["c"]], xa.at[y * 2 + 1 - at["c"]]
        send, recv = semys.at[y], semyr.at[y]
        return remote(mine, mine, send, recv, sibling), remote(other, other, send, recv, sibling)

    for k in range(1, 16):
        first(k)[0].start()
    down_copy(xl).start()

    def move():
        for n in (0, 2, 1):
            moves(n).start()
        for n in range(3):
            moves(n).wait()

    def stay():
        toks[...] = tok[...]
        cs[xl] = cot[...]
        lens_in[...] = lens_out[...]

    pl.when(jnp.logical_not(stays))(move)
    pl.when(stays)(stay)
    swap(cs, 0).start()
    inputs = toks[...].astype(F32)
    xa[here] = (inputs * norm_factor(inputs)).astype(BF16)
    for y in range(1, 4):
        pl.when(y > at["y"])(lambda y=y: token_out(y).start())
    pl.when(at["c"] == 0)(lambda: token_across(at["y"])[0].start())
    r0[at["c"] * 8 + s] = s0b[at["c"], s]
    rd0[xl] = d0b[xl]

    def rest(i, part):
        return pl.ds(0, 48) if part == 0 else pl.ds(48, ROWS[i] - 48)

    def block(i, fixed, core, rows):
        where = select(NAMES, fixed)
        if rows.start < 48:
            return attn_weights[i].at[where + (core,)]
        return weights[i].at[where + (pl.ds(rows.start - 48, rows.size),)]

    def put(i, first_row, value):
        where = select(NAMES, at)
        if first_row < 48:
            attn_weights[i][where + (at["c"],)] = value
        else:
            weights[i][where + (slice(first_row - 48, first_row - 48 + value.shape[0]),)] = value

    def ring(i, part, phase, k):
        order = ORDERS[i]
        axis = order[phase]
        fixed = {n: at[n] for n in ("x", "y", "z") if n not in order[:phase]}
        theirs = {**fixed, axis: (at[axis] - k + 4) % 4}
        mine, other = block(i, fixed, at["c"], rest(i, part)), block(i, theirs, at["c"], rest(i, part))
        slot = 2 * part + phase
        send, recv = sems.at[i, slot, k - 1], semr.at[i, slot, k - 1]
        to = device(shifted(at, axis, k))
        return remote(mine, mine, send, recv, to), remote(other, other, send, recv, to)

    def direct(i, part, k):
        axis = ORDERS[i][2]
        rows = pl.ds(*PARTS[part][i])
        mine = block(i, {axis: at[axis]}, at["c"], rows)
        other = block(i, {axis: (at[axis] - k + 4) % 4}, at["c"], rows)
        send, recv = semls.at[i, part, k - 1], semlr.at[i, part, k - 1]
        to = device(shifted(at, axis, k))
        return remote(mine, mine, send, recv, to), remote(other, other, send, recv, to)

    def across(i, k):
        axis = ORDERS[i][2]
        where = {axis: (at[axis] + k) % 4}
        mine, other = block(i, where, at["c"], rest(i, 0)), block(i, where, 1 - at["c"], rest(i, 0))
        send, recv = semcs.at[i, k], semcr.at[i, k]
        return remote(mine, mine, send, recv, sibling), remote(other, other, send, recv, sibling)

    def start(part, phase):
        for k in (1, 3, 2):
            for i in FULL:
                ring(i, part, phase, k)[0].start()

    def arrive(part, phase):
        for k in (1, 3, 2):
            for i in FULL:
                ring(i, part, phase, k)[1].wait_recv()

    def start_last(part):
        for k in (1, 3, 2):
            for i in PARTS[part]:
                direct(i, part, k)[0].start()

    def arrive_last(part):
        for k in (1, 3, 2):
            for i in PARTS[part]:
                direct(i, part, k)[1].wait_recv()
                if part == 0:
                    across(i, (4 - k) % 4)[0].start()

    def sent(part):
        for i in PARTS[part]:
            for k in (1, 2, 3):
                direct(i, part, k)[0].wait_send()

    for k in range(1, 16):
        first(k)[1].wait_recv()
    flat = r0[...].reshape(256, 384)
    piece = nn(one_hot(48, 16, 6, 16, at["c"] * 128 + 8), flat).astype(BF16)
    for i in range(3):
        put(i, 0, piece[:, i * 128 : (i + 1) * 128])
    start(0, 0)
    piece = nn(one_hot(96, 16, 6, 16, 0), flat).astype(BF16)
    put(0, 48, piece[:, :128])
    put(0, 144, piece[:64, 256:])
    put(1, 48, piece[:, 128:256])
    put(2, 192, piece[64:, 256:])
    down_copy(1 - xl).wait_recv()
    piece = nn(one_hot(48, 2, 24, 32, 0), rd0[...].reshape(64, 384)).astype(BF16)
    for b in range(3):
        lanes = slice(b * 128, (b + 1) * 128)
        put(2, 48 + 32 * b, piece[:32, lanes])
        put(2, 144 + 16 * b, piece[32:, lanes])
    start(1, 0)
    arrive(0, 0)
    start(0, 1)
    arrive(0, 1)
    start_last(0)
    for i in ATTN:
        across(i, 0)[0].start()
    arrive(1, 0)
    start(1, 1)

    ends = [lens_in[0:1, :]]
    for r in (1, 2):
        ends.append(ends[-1] + lens_in[r : r + 1, :])
    freq_lane = (lax.broadcasted_iota(jnp.int32, (1, 128), 1) % 32).astype(F32)
    freqs = jnp.exp(freq_lane * (-2.0 * math.log(ROPE_BASE) / HEAD_DIM))
    lane = lax.broadcasted_iota(jnp.int32, (128, 128), 1)

    def segment_of(index):
        return sum(jnp.where(index >= e, 1.0, 0.0) for e in ends)

    def table(u, carry):
        index = (u * 128 + lax.broadcasted_iota(jnp.int32, (128, 128), 0)).astype(F32)
        begin = jnp.zeros_like(index)
        for e in ends:
            begin = jnp.where(index >= e, e, begin)
        angle = (index - begin) * freqs
        rows = pl.ds(pl.multiple_of(u * 128, 128), 128)
        cosine[rows, :] = jnp.cos(angle)
        sine[rows, :] = jnp.where(lane % 64 < 32, -1.0, 1.0) * jnp.sin(angle)
        mine = (here * 128 + lax.broadcasted_iota(jnp.int32, (1, 128), 1)).astype(F32)
        allowed = (segment_of(index) == segment_of(mine)) & (index <= mine)
        bias[rows, :] = jnp.where(allowed, 0.0, MASKED_SCORE)
        return carry

    lax.fori_loop(0, 8, table, 0)

    arrive(1, 1)
    start_last(1)
    for u in range(1, 8):

        def clear(u=u):
            xa[u] = jnp.zeros((128, 768), BF16)

        pl.when(u > here)(clear)
    for y in range(3):

        def pass_on(y=y):
            token_in(y).wait_recv()
            token_across(y)[0].start()

        pl.when(y < at["y"])(pass_on)
    for y in range(3):
        pl.when(y < at["y"])(lambda y=y: token_across(y)[1].wait_recv())
    pl.when(at["c"] == 1)(lambda: token_across(at["y"])[1].wait_recv())

    def transpose_tokens(u, carry):
        xat[:, pl.ds(pl.multiple_of(u * 128, 128), 128)] = xa[u].T
        return carry

    lax.fori_loop(0, 8, transpose_tokens, 0)
    arrive_last(0)
    for k in range(4):
        for i in ATTN:
            across(i, k)[1].wait_recv()

    for k in range(1, 16):
        first(k)[0].wait_send()
    down_copy(xl).wait_send()
    for y in range(1, 4):
        pl.when(y > at["y"])(lambda y=y: token_out(y).wait_send())
    for y in range(3):
        pl.when(y < at["y"])(lambda y=y: token_across(y)[0].wait_send())
    pl.when(at["c"] == 0)(lambda: token_across(at["y"])[0].wait_send())

    mine = pl.ds(pl.multiple_of(here * 128, 128), 128)
    cos_mine, sin_mine = cosine[mine, :], sine[mine, :]
    left = lax.broadcasted_iota(jnp.int32, (128, 128), 1) < 64

    def attn_weight(kind, t, h):
        return attn_weights[t][kind, h].reshape(768, 128)

    def put_grad(kind, t, h, value):
        own_grads[t][kind, h] = value.reshape(2, 4, 2, 48, 128)

    def attn_full(kind):
        return jnp.concatenate([attn_weight(kind, p % 3, p // 3) for p in range(6)], axis=1)

    def stacked(v):
        zero = jnp.zeros_like(v)
        return jnp.concatenate([jnp.where(left, v, zero), jnp.where(left, zero, v)], axis=0)

    def unstacked(v):
        return jnp.concatenate([v[:64, :128], v[64:, 128:]], axis=0).T

    def pair_lanes(p):
        return pl.ds(pl.multiple_of(p * 128, 128), 128)

    def attend(t, h):
        p = t + 3 * h
        tokens_all = xa[...].reshape(1024, 768)
        w_kv = jnp.concatenate([attn_weight(1, t, h), attn_weight(2, t, h)], axis=1)
        kv = nn(tokens_all, w_kv)
        k_raw = kv[:, :128]
        k = (k_raw * cosine[...] + swap_halves(k_raw) * sine[...]).astype(BF16)
        v = kv[:, 128:].astype(BF16)
        q_raw = nn(xa[here], attn_weight(0, t, h))
        q = ((q_raw * cos_mine + swap_halves(q_raw) * sin_mine).astype(BF16) * (1.0 / math.sqrt(HEAD_DIM))).astype(BF16)
        qq = stacked(q)
        ks[p] = k
        vs[p] = v
        qs[p] = qq
        masks = bias[...]
        scores = nt(k, qq) + jnp.concatenate([masks, masks], axis=1)
        top = jnp.max(scores, axis=0, keepdims=True)
        e = jnp.exp(scores - top)
        total = jnp.sum(e, axis=0, keepdims=True)
        probs = (e * (1.0 / total)).astype(BF16)
        ps[p] = probs
        att[:, pair_lanes(p)] = unstacked(tn(v, probs)).astype(BF16)

    for t in range(3):

        def attend_third(h, carry, t=t):
            attend(t, h)
            return carry

        lax.fori_loop(0, 2, attend_third, 0)
        if t == 0:
            start_last(2)


    hidden = toks[...].astype(F32) + nn(att[...], attn_full(3))
    hid[...] = hidden
    factor_two = norm_factor(hidden)
    v2s[at["c"]] = (hidden * factor_two).astype(BF16)
    swap(v2s, 1).start()
    oacc[...] = jnp.zeros_like(oacc)
    eacc[...] = jnp.zeros_like(eacc)
    swapped(cs, 0).wait()
    swapped(v2s, 1).wait()
    v2 = v2s[...].reshape(256, 768)
    v2t = v2.T

    def pair(a, b):
        return jnp.concatenate([a, b], axis=1)

    def gated(gate, up, d_w):
        c = cs[...].reshape(256, 768)
        sig = 1.0 / (1.0 + jnp.exp(-gate))
        silu = gate * sig
        mixed = (silu * up).astype(BF16)
        oacc[...] += nn(mixed, d_w).reshape(2, 128, 768)
        d_mixed = nt(c, d_w)
        d_gate = d_mixed * up * sig * (1.0 + gate * (1.0 - sig))
        d_up = d_mixed * silu
        return d_gate, d_up, tn(mixed, c).astype(BF16)

    def down_rows(xh, z, first_row, rows):
        def part(b, h, n):
            some = pl.ds(first_row - 48 + n * rows, rows)
            return w2[:, h, xh, z + b, some].reshape(4 * rows, 128)

        return jnp.concatenate(
            [jnp.concatenate([part(b, h, n) for h in range(2) for n in range(3)], axis=1) for b in range(2)], axis=0
        )

    def put_down(xh, z, first_row, rows, g):
        for b in range(2):
            for h in range(2):
                for n in range(3):
                    some = pl.ds(first_row + n * rows, rows)
                    lanes = slice(h * 384 + n * 128, h * 384 + (n + 1) * 128)
                    h2[:, h, xh, z + b, some] = g[b * 4 * rows : (b + 1) * 4 * rows, lanes].reshape(4, rows, 128)

    def feed_early(y, carry):
        g_w = pair(*(w0[y, b, :, :, 0:96].reshape(768, 128) for b in range(2)))
        u_w = pair(*(w1[y, b].reshape(768, 128) for b in range(2)))
        xh, z = y // 2, (y % 2) * 2
        d_w = down_rows(xh, z, 48, 32)
        d_gate, d_up, g_d = gated(nn(v2, g_w), nn(v2, u_w), d_w)
        d_gate, d_up = d_gate.astype(BF16), d_up.astype(BF16)
        eacc[...] += (nt(d_gate, g_w) + nt(d_up, u_w)).reshape(2, 128, 768)
        g_g = nn(v2t, d_gate).astype(BF16)
        g_u = nn(v2t, d_up).astype(BF16)
        for b in range(2):
            lanes = slice(b * 128, (b + 1) * 128)
            h0[y, b, :, :, 48:144] = g_g[:, lanes].reshape(2, 4, 96, 128)
            h1[y, b, :, :, 48:144] = g_u[:, lanes].reshape(2, 4, 96, 128)
        put_down(xh, z, 48, 32, g_d)
        return carry

    def feed_late(y, carry):
        def weight(b):
            low_rows, high_rows = w0[y, b, :, :, 96:160], w2[y, b, :, :, 144:176]
            return jnp.concatenate([low_rows, high_rows], axis=2).reshape(768, 128)

        w = pair(weight(0), weight(1))
        xh, z = y // 2, (y % 2) * 2
        d_w = down_rows(xh, z, 144, 16)
        both = nn(v2, w)
        low = lax.broadcasted_iota(jnp.int32, (256, 128), 1) < 64

        def mix(a, b):
            return jnp.where(low, a, pltpu.roll(b, 64, 1)), jnp.where(low, pltpu.roll(a, 64, 1), b)

        gate, up = mix(both[:, :128], both[:, 128:])
        d_gate, d_up, g_d = gated(gate, up, d_w)
        d_both = pair(*mix(d_gate, d_up)).astype(BF16)
        eacc[...] += nt(d_both, w).reshape(2, 128, 768)
        g = nn(v2t, d_both).astype(BF16)
        for b in range(2):
            rows = g[:, b * 128 : (b + 1) * 128].reshape(2, 4, 96, 128)
            h0[y, b, :, :, 144:208] = rows[:, :, :64]
            h2[y, b, :, :, 192:224] = rows[:, :, 64:]
        put_down(xh, z, 144, 16, g_d)
        return carry

    def home(i, fixed, part=None, half=None):
        first_row, rows = (0, ROWS[i]) if part is None else PARTS[part][i]
        return homes[i].at[select(NAMES, fixed, half) + (pl.ds(first_row, rows),)]

    def share(i, k):
        where = {ORDERS[i][2]: (at[ORDERS[i][2]] + k) % 4}
        part = own_grads[i].at[select(NAMES, where) + (1 - at["c"],)]
        return remote(part, home(i, where, 0), bemcs.at[i, k], bemcr.at[i, k], sibling)

    def add_core(i, k):
        order = ORDERS[i]
        free = kept(NAMES, order[:2])
        fixed = {order[2]: (at[order[2]] + k) % 4}
        rows = pl.ds(*ATTN[i])

        def body(n, carry):
            index = full_index(NAMES, fixed, free, n)
            total = homes[i][index + (rows,)].astype(F32) + own_grads[i][index + (at["c"],)].astype(F32)
            homes[i][index + (rows,)] = total.astype(BF16)
            return carry

        lax.fori_loop(0, count(free), body, 0, unroll=4)

    def split(i):
        return "z" if ORDERS[i][2] == "y" else "y"

    def halfway(i, part, way):
        axis = ORDERS[i][2]
        half = (split(i), way)
        src = home(i, {axis: (at[axis] + 2) % 4}, part, half)
        dst = t3[i].at[(1,) + select(kept(NAMES, ORDERS[i][:2]), {}, half) + (pl.ds(*PARTS[part][i]),)]
        send, recv = bemls.at[i, part, way], bemlr.at[i, part, way]
        return remote(src, dst, send, recv, device(shifted(at, axis, (1, 3)[way])))

    def whole(i, part, way):
        axis = ORDERS[i][2]
        src = home(i, {axis: (at[axis] + (1, 3)[way]) % 4}, part)
        dst = t3[i].at[2 * way, :, :, :, pl.ds(*PARTS[part][i])] if ORDERS[i][2] != "x" else t3[i].at[
            2 * way, :, :, pl.ds(*PARTS[part][i])
        ]
        send, recv = bemls.at[i, part, 2 + way], bemlr.at[i, part, 2 + way]
        return remote(src, dst, send, recv, device(shifted(at, axis, (1, 3)[way])))

    def add_half(i, part, way):
        order = ORDERS[i]
        where = split(i)
        free = kept(NAMES, order[:2])
        turned = (where,) + tuple(m for m in free if m != where)
        fixed = {order[2]: (at[order[2]] + (1, 3)[way]) % 4}
        rows = pl.ds(*PARTS[part][i])

        def body(n, carry):
            got = digits(turned, n)
            got[where] = got[where] + way * (SIZES[where] // 2)
            n = 0
            for m in free:
                n = n * SIZES[m] + got[m]
            index = full_index(NAMES, fixed, free, n) + (rows,)
            came = t3[i][(1,) + tuple(got[m] for m in free) + (rows,)]
            homes[i][index] = (homes[i][index].astype(F32) + came.astype(F32)).astype(BF16)
            return carry

        lax.fori_loop(0, count(free) // 2, body, 0, unroll=4)

    def add_whole(i, part):
        order = ORDERS[i]
        free = kept(NAMES, order[:2])
        fixed = {order[2]: at[order[2]]}
        rows = pl.ds(*PARTS[part][i])

        def body(n, carry):
            index = full_index(NAMES, fixed, free, n) + (rows,)
            there = full_index(free, {}, free, n) + (rows,)
            total = homes[i][index].astype(F32) + t3[i][(0,) + there].astype(F32) + t3[i][(2,) + there].astype(F32)
            homes[i][index] = total.astype(BF16)
            return carry

        lax.fori_loop(0, count(free), body, 0, unroll=4)

    def hop(i, part, left, k):
        order = ORDERS[i]
        axis = order[left - 1]
        fixed = {a: at[a] for a in order[left:]}
        rows = rest(i, part)
        src = homes[i].at[select(NAMES, {**fixed, axis: (at[axis] + k) % 4}) + (rows,)]
        if left == 1:
            dst = t1[i].at[k - 1, rows]
        else:
            dst = t2[i].at[(k - 1,) + select(kept(NAMES, order[:1]), {}) + (rows,)]
        slot = 2 * part + left - 1
        send, recv = bems.at[i, slot, k - 1], bemr.at[i, slot, k - 1]
        return remote(src, dst, send, recv, device(shifted(at, axis, k)))

    def add_ring(i, part):
        order = ORDERS[i]
        free = kept(NAMES, order[:1])
        fixed = {a: at[a] for a in order[1:]}
        rows = rest(i, part)

        def body(n, carry):
            index = full_index(NAMES, fixed, free, n) + (rows,)
            total = homes[i][index].astype(F32)
            for k in range(3):
                total = total + t2[i][(k,) + full_index(free, {}, free, n) + (rows,)].astype(F32)
            homes[i][index] = total.astype(BF16)
            return carry

        lax.fori_loop(0, count(free), body, 0)

    def hop_start(part):
        for k in (1, 3, 2):
            for i in FULL:
                hop(i, part, 2, k).start()

    def hop_on(part):
        for i in FULL:
            for k in (1, 3, 2):
                hop(i, part, 2, k).wait_recv()
            add_ring(i, part)
            for k in (1, 3, 2):
                hop(i, part, 1, k).start()

    def last(i, part):
        for k in (1, 3, 2):
            hop(i, part, 1, k).wait_recv()
        rows = rest(i, part)
        total = homes[i][select(NAMES, at) + (rows,)].astype(F32)
        for k in range(3):
            total = total + t1[i][k, rows].astype(F32)
        return total.astype(BF16)

    def half_start(part, items=FULL):
        for way in range(2):
            for i in items:
                if i in PARTS[part]:
                    halfway(i, part, way).start()

    def half_on(part, items=FULL):
        for way in range(2):
            for i in items:
                if i in PARTS[part]:
                    halfway(i, part, way).wait_recv()
                    add_half(i, part, way)
                    whole(i, part, way).start()

    def whole_on(part):
        for i in PARTS[part]:
            for way in range(2):
                whole(i, part, way).wait_recv()
            add_whole(i, part)

    for i in FULL:
        for part in range(2):
            if i in FULL:
                for phase in range(2):
                    for k in (1, 2, 3):
                        ring(i, part, phase, k)[0].wait_send()
    arrive_last(1)
    lax.fori_loop(0, 4, feed_early, 0)
    half_start(1)
    arrive_last(2)
    lax.fori_loop(0, 4, feed_late, 0)
    sum_o = remote(oacc.at[1 - at["c"]], osum, semps.at[2], sempr.at[2], sibling)
    sum_e = remote(eacc.at[1 - at["c"]], esum, semps.at[3], sempr.at[3], sibling)
    sum_e.start()
    sum_o.start()
    half_start(2)
    half_on(1)
    sum_e.wait()

    hidden = hid[...]
    factor_two = norm_factor(hidden)
    d_hidden = cs[at["c"]].astype(F32) + norm_back(hidden, factor_two, eacc[at["c"]] + esum[...])
    dhid[...] = d_hidden
    dh = d_hidden.astype(BF16)
    d_att = nt(dh, attn_full(3)).astype(BF16)
    att_t = att[...].T
    for j in range(2):
        g_o = nn(att_t, dh[:, j * 384 : (j + 1) * 384]).astype(BF16)
        for t in range(3):
            put_grad(3, t, j, g_o[:, t * 128 : (t + 1) * 128])
    att[...] = d_att

    def attend_back(t, h):
        p = t + 3 * h
        da = stacked(att[:, pair_lanes(p)])
        k, v, qq, probs = ks[p], vs[p], qs[p], ps[p]
        d_probs = nt(v, da)
        probs_f = probs.astype(F32)
        d_sum = jnp.sum(probs_f * d_probs, axis=0, keepdims=True)
        d_scores = (probs_f * (d_probs - d_sum)).astype(BF16)
        d_v = nn(probs, da).astype(BF16)
        d_k = nn(d_scores, qq)
        d_k = (d_k * cosine[...] - swap_halves(d_k) * sine[...]).astype(BF16)
        d_q = unstacked(tn(k, d_scores)) * (1.0 / math.sqrt(HEAD_DIM))
        d_q = (d_q * cos_mine - swap_halves(d_q) * sin_mine).astype(BF16)
        ks[p] = d_k
        vs[p] = d_v
        dqs[:, pair_lanes(p)] = d_q
        g_kv = nn(xat[...], jnp.concatenate([d_k, d_v], axis=1)).astype(BF16)
        g_q = nn(xat[:, mine], d_q).astype(BF16)
        put_grad(0, t, h, g_q)
        put_grad(1, t, h, g_kv[:, :128])
        put_grad(2, t, h, g_kv[:, 128:])

    def share_on(i):
        for k in (2, 1, 3, 0):
            share(i, k).wait_recv()
            add_core(i, k)
            if k == 2:
                half_start(0, (i,))

    half_on(2)
    def third_back(h, carry):
        attend_back(0, h)
        return carry

    lax.fori_loop(0, 2, third_back, 0)

    def share_start(i):
        for k in (2, 1, 3, 0):
            share(i, k).start()

    share_start(0)
    attend_back(1, 0)
    share_on(0)
    attend_back(1, 1)
    share_start(1)
    half_on(0, (0,))
    attend_back(2, 0)
    share_on(1)
    attend_back(2, 1)
    share_start(2)
    whole_on(1)
    half_on(0, (1,))
    share_on(2)
    whole_on(2)
    hop_start(1)

    w_kv = jnp.concatenate([attn_full(1), attn_full(2)], axis=1)

    def tokens_back(u, carry):
        rows = pl.ds(pl.multiple_of(u * 128, 128), 128)
        d_kv = jnp.concatenate([ks[p, rows, :] for p in range(6)] + [vs[p, rows, :] for p in range(6)], axis=1)
        xa[u] = nt(d_kv, w_kv).astype(BF16)
        return carry

    lax.fori_loop(0, 8, tokens_back, 0)

    def grad_across(y):
        mine = xa.at[y * 2 + 1 - at["c"]]
        return remote(mine, rdc.at[y], semzs.at[y], semzr.at[y], sibling)

    def grad_out(y):
        return remote(xa.at[y * 2 + at["c"]], rdn.at[at["y"]], semws.at[y], semwr.at[at["y"]], (f, y * 2 + xl))

    def grad_in(y):
        return remote(xa.at[y * 2 + at["c"]], rdn.at[y], semws.at[y], semwr.at[y], (f, y * 2 + xl))

    for y in range(3):
        pl.when(y < at["y"])(lambda y=y: grad_across(y).start())
    pl.when(at["c"] == 1)(lambda: grad_across(at["y"]).start())
    for y in range(3):

        def add_across(y=y):
            grad_across(y).wait_recv()
            block = xa[y * 2 + at["c"]].astype(F32) + rdc[y].astype(F32)
            xa[y * 2 + at["c"]] = block.astype(BF16)
            grad_out(y).start()

        pl.when(y < at["y"])(add_across)
    half_on(0, (2,))
    sum_o.wait()
    out_s[...] = (hid[...] + oacc[at["c"]] + osum[...]).astype(BF16)

    def out_move():
        return remote(out_s, out_o, semms.at[3], semmr.at[3], partner)

    def out_stay():
        out_o[...] = out_s[...]

    pl.when(jnp.logical_not(stays))(lambda: out_move().start())
    pl.when(stays)(out_stay)
    esum[...] = nt(dqs[...], attn_full(0))

    hop_on(1)
    whole_on(0)
    hop_start(0)
    sum0, sum1, sum2 = last(0, 1), last(1, 1), last(2, 1)
    down = jnp.concatenate(
        [
            jnp.concatenate([sum2[a + b * n : a + b * (n + 1)] for n in range(3)], axis=1)
            for a, b in ((0, 32), (96, 16))
        ],
        axis=0,
    )
    mixed_units = jnp.concatenate([sum0[96:160], sum2[144:176]], axis=0)
    both = jnp.concatenate([sum0[0:96], sum1[0:96], mixed_units], axis=1)
    rows_mlp = nn(one_hot(96, 16, 6, 16, 0, True), both)
    d0b[...] = nn(one_hot(48, 2, 24, 32, 0, True), down).astype(BF16).reshape(2, 32, 384)
    hop_on(0)

    esum[...] += xa[here].astype(F32)

    def add_own():
        grad_across(at["y"]).wait_recv()
        esum[...] += rdc[at["y"]].astype(F32)

    pl.when(at["c"] == 0)(add_own)
    for y in range(1, 4):

        def add(y=y):
            grad_in(y).wait_recv()
            esum[...] += rdn[y].astype(F32)

        pl.when(y > at["y"])(add)
    inputs = toks[...].astype(F32)
    in_s[...] = dhid[...] + norm_back(inputs, norm_factor(inputs), esum[...])

    def in_move():
        return remote(in_s, in_o, semms.at[4], semmr.at[4], partner)

    def in_stay():
        in_o[...] = in_s[...]

    pl.when(jnp.logical_not(stays))(lambda: in_move().start())
    pl.when(stays)(in_stay)
    attn = jnp.concatenate([last(i, 0) for i in range(3)], axis=1)
    rows = rows_mlp + nn(one_hot(48, 16, 6, 16, at["c"] * 128 + 8, True), attn)
    s0b[...] = rows.astype(BF16).reshape(2, 8, 16, 384)

    def final(k):
        return group(k, s0b, r0, bem0s, bem0r)

    def final_down(slot):
        return remote(d0b.at[1 - xl], rd0.at[slot], bemds, bemdr, beside)

    for k in range(1, 16):
        final(k)[0].start()
    final_down(xl).start()
    r0[at["c"] * 8 + s] = s0b[at["c"], s]
    rd0[xl] = d0b[xl]
    for k in range(1, 16):
        final(k)[1].wait_recv()
    final_down(1 - xl).wait_recv()

    rows_o[...] = r0[...]
    down_o[...] = rd0[...]
    for k in range(1, 16):
        final(k)[0].wait_send()
    final_down(xl).wait_send()
    for y in range(3):

        def across_sent(y=y):
            grad_across(y).wait_send()
            grad_out(y).wait_send()

        pl.when(y < at["y"])(across_sent)
    pl.when(at["c"] == 1)(lambda: grad_across(at["y"]).wait_send())

    def moved():
        out_move().wait()
        in_move().wait()

    pl.when(jnp.logical_not(stays))(moved)
    for part in range(3):
        sent(part)
    for i in ATTN:
        for k in range(4):
            across(i, k)[0].wait_send()
            share(i, k).wait_send()
    for part in range(3):
        for i in PARTS[part]:
            for way in range(2):
                halfway(i, part, way).wait_send()
                whole(i, part, way).wait_send()
    for part in range(2):
        for i in FULL:
            for left in (2, 1):
                for k in (1, 2, 3):
                    hop(i, part, left, k).wait_send()


def finish_kernel(gains, w_query, w_key, w_value, w_gate, w_up, rows_i, down_i, out_i, in_i,
                  out_o, in_o, ga1_o, gq_o, gk_o, gv_o, go_o, ga2_o, gg_o, gu_o, gd_o, s0):
    out_o[...] = out_i[...]
    in_o[...] = in_i[...]
    row = lax.broadcasted_iota(jnp.int32, (6, 1), 0)

    def gain_column(which):
        col = jnp.zeros((6, 1), F32)
        for r in range(6):
            col = jnp.where(row == r, gains[which, r], col)
        return col

    def as_row(col):
        lane = lax.broadcasted_iota(jnp.int32, (6, 6), 1)
        side = lax.broadcasted_iota(jnp.int32, (6, 6), 0)
        return jnp.sum(jnp.where(lane == side, col, 0.0), axis=0, keepdims=True)

    gain_one, gain_two = gain_column(0), gain_column(1)
    c = lax.axis_index("fsdp") % 2
    got = rows_i[...].reshape(2, 8, 16, 384)
    halves = [got[core, :, :8].reshape(64, 384) for core in range(2)]
    for which in range(2):
        natural = nn(halves[0], units(0, which == 1, True)) + nn(halves[1], units(1, which == 1, True))
        s0[which] = natural.reshape(8, 8, 384)
    s0[2] = rows_i[pl.ds(c * 8, 8), 8:, :].astype(F32)
    down = down_i[...].astype(F32)
    gain_sum_one = jnp.zeros((6, 1), F32)
    gain_sum_two = jnp.zeros((6, 1), F32)
    for b in range(8):
        lanes = pl.ds(b * 384, 384)
        half = pl.ds((b % 2) * 384, 384)
        h_gate, h_up, h_attn = s0[0, b, 0:6], s0[1, b, 0:6], s0[2, b, 0:6]
        gg_o[:, lanes] = h_gate * gain_two
        gu_o[:, lanes] = h_up * gain_two
        gain_sum_two += jnp.sum(h_gate * w_gate[:, lanes].astype(F32), axis=1, keepdims=True)
        gain_sum_two += jnp.sum(h_up * w_up[:, lanes].astype(F32), axis=1, keepdims=True)
        if b < 6:
            (gq_o, gk_o, gv_o)[b // 2][:, half] = h_attn * gain_one
            raw = (w_query, w_key, w_value)[b // 2][:, half].astype(F32)
            gain_sum_one += jnp.sum(h_attn * raw, axis=1, keepdims=True)
        else:
            go_o[:, half] = h_attn
    for b in range(2):
        gd_o[:, b * 384 : (b + 1) * 384] = down[b, 0:24]
    ga1_o[...] = as_row(gain_sum_one)
    ga2_o[...] = as_row(gain_sum_two)


VMEM_SPEC = pl.BlockSpec(memory_space=pltpu.VMEM)
SMEM_SPEC = pl.BlockSpec(memory_space=pltpu.SMEM)
DMA = pltpu.SemaphoreType.DMA


def layer(lens, gains, *arrays):
    outs = [((128, 768), BF16), ((128, 768), F32), ((16, 16, 384), BF16), ((2, 32, 384), BF16)]
    sizes = tuple(SIZES[n] for n in NAMES)
    scratch = [(sizes + (2, 48, 128), BF16) for _ in ROWS] + [(sizes + (r - 48, 128), BF16) for r in ROWS]
    scratch += [(sizes + (2, 48, 128), BF16) for _ in ROWS]
    scratch += [(sizes + (r, 128), BF16) for r in ROWS]
    scratch += [
        ((8, 128, 768), BF16), ((768, 1024), BF16), ((16, 16, 384), BF16), ((2, 32, 384), BF16),
        ((3, 8, 8, 384), F32), ((2, 32, 384), F32), ((2, 8, 16, 384), BF16), ((2, 32, 384), BF16),
        ((6, 1024, 128), BF16), ((6, 1024, 128), BF16), ((6, 256, 128), BF16), ((6, 1024, 256), BF16),
        ((128, 768), BF16), ((128, 768), F32), ((128, 768), F32), ((128, 768), BF16),
        ((1024, 128), F32), ((1024, 128), F32), ((1024, 128), F32), ((4, 128, 768), BF16),
        ((2, 128, 768), BF16), ((2, 128, 768), BF16), ((2, 128, 768), F32), ((2, 128, 768), F32),
        ((128, 768), F32), ((128, 768), F32), ((4, 128, 768), BF16), ((128, 768), BF16), ((128, 768), BF16), ((128, 768), F32),
        ((8, 128), F32), ((8, 128), F32),
    ]
    for rings in (2, 1, 0):
        for i in range(3):
            left = tuple(SIZES[n] for n in kept(NAMES, ORDERS[i][:rings]))
            scratch.append(((3,) + left + (ROWS[i], 128), BF16))
    copies = [
        DMA((15,)), DMA((15,)), DMA, DMA, DMA((4,)), DMA((4,)),
        DMA((3, 4, 3)), DMA((3, 4, 3)), DMA((3, 3, 4)), DMA((3, 3, 4)), DMA((3, 4)), DMA((3, 4)), DMA((4,)), DMA((4,)),
        DMA((15,)), DMA((15,)), DMA, DMA,
        DMA((3, 4, 3)), DMA((3, 4, 3)), DMA((3, 3, 4)), DMA((3, 3, 4)), DMA((3, 4)), DMA((3, 4)),
        DMA((5,)), DMA((5,)), DMA((4,)), DMA((4,)), DMA((4,)), DMA((4,)), DMA((4,)), DMA((4,)),
    ]
    return pl.pallas_call(
        layer_kernel,
        out_shape=[jax.ShapeDtypeStruct(shape, kind) for shape, kind in outs],
        in_specs=[SMEM_SPEC] * 2 + [VMEM_SPEC] * 9,
        out_specs=[VMEM_SPEC] * len(outs),
        scratch_shapes=[pltpu.VMEM(shape, kind) for shape, kind in scratch] + copies,
        compiler_params=pltpu.CompilerParams(collective_id=0, has_side_effects=True, vmem_limit_bytes=VMEM_LIMIT),
        name="layer",
    )(lens, gains, *arrays)


def finish(gains, *arrays):
    outs = [
        ((128, 768), BF16), ((128, 768), F32), ((1, 6), F32),
        ((6, 768), F32), ((6, 768), F32), ((6, 768), F32), ((6, 768), F32),
        ((1, 6), F32), ((6, 3072), F32), ((6, 3072), F32), ((24, 768), F32),
    ]
    return pl.pallas_call(
        finish_kernel,
        out_shape=[jax.ShapeDtypeStruct(shape, kind) for shape, kind in outs],
        in_specs=[SMEM_SPEC] + [VMEM_SPEC] * 9,
        out_specs=[VMEM_SPEC] * len(outs),
        scratch_shapes=[pltpu.VMEM((3, 8, 8, 384), F32)],
        name="finish",
    )(gains, *arrays)


def per_device(tokens, doc_lengths, attn_gain, w_query, w_key, w_value, w_out, mlp_gain, w_gate, w_up, w_down, cotangent):
    gains = jnp.stack([attn_gain, mlp_gain]).astype(F32)
    layer_out, input_grad, rows, down = layer(
        doc_lengths, gains, tokens[0], cotangent[0], w_query, w_key, w_value, w_out, w_gate, w_up, w_down
    )
    out = finish(gains, w_query, w_key, w_value, w_gate, w_up, rows, down, layer_out, input_grad)
    return (out[0][None], out[1][None], out[2][0]) + tuple(out[3:7]) + (out[7][0],) + tuple(out[8:])


def solution(mesh):
    rows = P(("fsdp", "seq"), None)
    gain = P(("fsdp", "seq"))
    toks = P("fsdp", "seq", None)
    return jax.shard_map(
        per_device,
        mesh=mesh,
        in_specs=(toks, P("fsdp", None), gain, rows, rows, rows, rows, gain, rows, rows, rows, toks),
        out_specs=(toks, toks, gain, rows, rows, rows, rows, gain, rows, rows, rows),
        check_vma=False,
    )
```

time: 175 us -> 161 us (0.920)
  local copies, waits for them, and re-layouts: 8.09 us -> 0.66 us
  Pallas kernels: 162 us -> 159 us
  other arithmetic: 3.22 us -> 0.58 us
    unnamed x29 -> x4, local copies, waits for them, and re-layouts: 8.09 us -> 0.66 us
    pallas_call x1, Pallas kernels: 162 us -> 157 us  [layer(): pl.pallas_call(layer_kernel, out_shape=[jax.ShapeDtypeStruct(shape, kind)...]
    pallas_call x2 -> x0, other arithmetic: 2.66 us -> none  [layer(): pl.pallas_call(layer_kernel, out_shape=[jax.ShapeDtypeStruct(shape, kind)...]
    pallas_call x0 -> x1, Pallas kernels: none -> 2.62 us  [finish(): pl.pallas_call(finish_kernel, out_shape=[jax.ShapeDtypeStruct(shape, kind...]
where the time goes in v4:
time: 161 us
  Pallas kernels  159 us (99%)
    pallas_call x1, Pallas kernels, layer(): pl.pallas_call(layer_kernel, out_shape=[jax.ShapeDtypeStruct(shape, kind)...  157 us

profile of v4, /device:TPU:1, one launch (start us, length us, event | category | flops | bytes accessed | tf_op | source)
XLA Modules:
  0.0 161.2 jit_solution(17190793190628091027)
XLA Ops:
  0.6 0.0 copy-start
  0.7 0.0 copy-start.1
  0.7 0.6 copy-done
  1.3 0.0 copy-done.1
  1.3 0.6 maximum_convert_fusion.gains
  1.9 156.5 %layer.1 = (bf16[128,768]{1,0:T(8,128)(2,1)}, f32[128,768]{1,0:T(8,128)}, bf16[16,16,384]{2,1,0:T(8,128)(2,1)}, bf16[2,32,384]{2,1,0:T(8,128)(2,1)}) custom-call(s32[1,4]{1,0:T(1,128)} %lens.1, f32[2,6]{1,0:T(2,128)} %maximum_convert_fusion.gains, bf16[128,768]{1,0:T(8,128)(2,1)} %bitcast.8, bf16[128,768]{1,0:T(8,128)(2,1)} %bitcast.9, ...), custom_call_target="tpu_custom_call" | custom-call | tf_op jit(solution)/shard_map/layer/pallas_call | solution.py:1049
  158.4 2.6 %finish.1 = (bf16[128,768]{1,0:T(8,128)(2,1)}, f32[128,768]{1,0:T(8,128)}, f32[1,6]{1,0:T(1,128)}, f32[6,768]{1,0:T(8,128)}, f32[6,768]{1,0:T(8,128)}, /*index=5...) custom-call(f32[2,6]{1,0:T(2,128)} %maximum_convert_fusion.gains, ...), custom_call_target="tpu_custom_call" | custom-call | tf_op jit(solution)/shard_map/finish/pallas_call | solution.py:1066
Async XLA Ops:
  0.6 0.7 copy-start
  0.7 0.7 copy-start.1

commit v5 on v4

--- a/solution.py
+++ b/solution.py
@@ -20,11 +20,11 @@
 NAMES = ("y", "xl", "xh", "z")
 SIZES = {"y": 4, "xl": 2, "xh": 2, "z": 4, "c": 2}
 ORDERS = (("y", "z", "x"), ("z", "x", "y"), ("x", "y", "z"))
-ROWS = (208, 144, 224)
+ROWS = (208, 176, 192)
 FULL = (1, 0, 2)
 ATTN = {0: (0, 48), 1: (0, 48), 2: (0, 48)}
 EARLY = {0: (48, 96), 1: (48, 96), 2: (48, 96)}
-LATE = {0: (144, 64), 2: (144, 80)}
+LATE = {0: (144, 64), 1: (144, 32), 2: (144, 48)}
 PARTS = (ATTN, EARLY, LATE)
 
 
@@ -154,10 +154,10 @@
 
 def layer_kernel(
     lens, gains, tok, cot, w_query, w_key, w_value, w_out, w_gate, w_up, w_down,
-    out_o, in_o, rows_o, down_o,
+    out_o, in_o, rows_o, down_o, attn_o,
     a0, a1, a2, w0, w1, w2, g0, g1, g2, h0, h1, h2,
     xa, xat, r0, rd0, s0, d0, s0b, d0b, ks, vs, qs, ps, att, hid, dhid, dqs, cosine, sine, bias, rdn,
-    v2s, cs, oacc, eacc, osum, esum, rdc, toks, out_s, in_s, lens_out, lens_in, *rest
+    v2s, cs, oacc, eacc, osum, esum, rdc, toks, out_s, in_s, lens_out, lens_in, sab, rab, *rest
 ):
     at = place()
     f = lax.axis_index("fsdp")
@@ -169,7 +169,7 @@
     t3, t2, t1 = rest[:3], rest[3:6], rest[6:9]
     sem0s, sem0r, semds, semdr, semxs, semxr, sems, semr, semls, semlr, semcs, semcr, semps, sempr = rest[9:23]
     bem0s, bem0r, bemds, bemdr, bems, bemr, bemls, bemlr, bemcs, bemcr = rest[23:33]
-    semms, semmr, semys, semyr, semzs, semzr, semws, semwr = rest[33:]
+    semms, semmr, semys, semyr, semzs, semzr, semws, semwr, semas, semar = rest[33:]
     attn_weights = (a0, a1, a2)
     weights = (w0, w1, w2)
     own_grads = (g0, g1, g2)
@@ -281,8 +281,11 @@
     def rest(i, part):
         return pl.ds(0, 48) if part == 0 else pl.ds(48, ROWS[i] - 48)
 
-    def block(i, fixed, core, rows):
-        where = select(NAMES, fixed)
+    def split(i):
+        return "z" if ORDERS[i][2] == "y" else "y"
+
+    def block(i, fixed, core, rows, half=None):
+        where = select(NAMES, fixed, half)
         if rows.start < 48:
             return attn_weights[i].at[where + (core,)]
         return weights[i].at[where + (pl.ds(rows.start - 48, rows.size),)]
@@ -314,6 +317,15 @@
         to = device(shifted(at, axis, k))
         return remote(mine, mine, send, recv, to), remote(other, other, send, recv, to)
 
+    def relay(i, part, way):
+        axis = ORDERS[i][2]
+        half, rows = (split(i), way), pl.ds(*PARTS[part][i])
+        mine = block(i, {axis: (at[axis] + (3, 1)[way]) % 4}, at["c"], rows, half)
+        other = block(i, {axis: (at[axis] + 2) % 4}, at["c"], rows, half)
+        send, recv = semls.at[i, part, (1, 3)[way]], semlr.at[i, part, (1, 3)[way]]
+        to = device(shifted(at, axis, (1, 3)[way]))
+        return remote(mine, mine, send, recv, to), remote(other, other, send, recv, to)
+
     def across(i, k):
         axis = ORDERS[i][2]
         where = {axis: (at[axis] + k) % 4}
@@ -332,21 +344,33 @@
                 ring(i, part, phase, k)[1].wait_recv()
 
     def start_last(part):
-        for k in (1, 3, 2):
+        for k in (1, 3) if part else (1, 3, 2):
             for i in PARTS[part]:
                 direct(i, part, k)[0].start()
 
+    def pass_last(part):
+        for way in range(2):
+            for i in PARTS[part]:
+                direct(i, part, (1, 3)[way])[1].wait_recv()
+                relay(i, part, way)[0].start()
+
     def arrive_last(part):
-        for k in (1, 3, 2):
-            for i in PARTS[part]:
-                direct(i, part, k)[1].wait_recv()
-                if part == 0:
+        for i in PARTS[part]:
+            if part:
+                for way in range(2):
+                    relay(i, part, way)[1].wait_recv()
+            else:
+                for k in (1, 3, 2):
+                    direct(i, part, k)[1].wait_recv()
                     across(i, (4 - k) % 4)[0].start()
 
     def sent(part):
         for i in PARTS[part]:
-            for k in (1, 2, 3):
+            for k in (1, 3) if part else (1, 2, 3):
                 direct(i, part, k)[0].wait_send()
+            if part:
+                for way in range(2):
+                    relay(i, part, way)[0].wait_send()
 
     for k in range(1, 16):
         first(k)[1].wait_recv()
@@ -359,7 +383,7 @@
     put(0, 48, piece[:, :128])
     put(0, 144, piece[:64, 256:])
     put(1, 48, piece[:, 128:256])
-    put(2, 192, piece[64:, 256:])
+    put(1, 144, piece[64:, 256:])
     down_copy(1 - xl).wait_recv()
     piece = nn(one_hot(48, 2, 24, 32, 0), rd0[...].reshape(64, 384)).astype(BF16)
     for b in range(3):
@@ -494,6 +518,7 @@
 
         lax.fori_loop(0, 2, attend_third, 0)
         if t == 0:
+            pass_last(1)
             start_last(2)
 
 
@@ -542,7 +567,7 @@
 
     def feed_early(y, carry):
         g_w = pair(*(w0[y, b, :, :, 0:96].reshape(768, 128) for b in range(2)))
-        u_w = pair(*(w1[y, b].reshape(768, 128) for b in range(2)))
+        u_w = pair(*(w1[y, b, :, :, 0:96].reshape(768, 128) for b in range(2)))
         xh, z = y // 2, (y % 2) * 2
         d_w = down_rows(xh, z, 48, 32)
         d_gate, d_up, g_d = gated(nn(v2, g_w), nn(v2, u_w), d_w)
@@ -559,7 +584,7 @@
 
     def feed_late(y, carry):
         def weight(b):
-            low_rows, high_rows = w0[y, b, :, :, 96:160], w2[y, b, :, :, 144:176]
+            low_rows, high_rows = w0[y, b, :, :, 96:160], w1[y, b, :, :, 96:128]
             return jnp.concatenate([low_rows, high_rows], axis=2).reshape(768, 128)
 
         w = pair(weight(0), weight(1))
@@ -579,7 +604,7 @@
         for b in range(2):
             rows = g[:, b * 128 : (b + 1) * 128].reshape(2, 4, 96, 128)
             h0[y, b, :, :, 144:208] = rows[:, :, :64]
-            h2[y, b, :, :, 192:224] = rows[:, :, 64:]
+            h1[y, b, :, :, 144:176] = rows[:, :, 64:]
         put_down(xh, z, 144, 16, g_d)
         return carry
 
@@ -605,9 +630,6 @@
             return carry
 
         lax.fori_loop(0, count(free), body, 0, unroll=4)
-
-    def split(i):
-        return "z" if ORDERS[i][2] == "y" else "y"
 
     def halfway(i, part, way):
         axis = ORDERS[i][2]
@@ -656,7 +678,9 @@
         def body(n, carry):
             index = full_index(NAMES, fixed, free, n) + (rows,)
             there = full_index(free, {}, free, n) + (rows,)
-            total = homes[i][index].astype(F32) + t3[i][(0,) + there].astype(F32) + t3[i][(2,) + there].astype(F32)
+            total = homes[i][index].astype(F32)
+            for k in (0, 2) if part else (0, 1, 2):
+                total = total + t3[i][(k,) + there].astype(F32)
             homes[i][index] = total.astype(BF16)
             return carry
 
@@ -714,6 +738,14 @@
             total = total + t1[i][k, rows].astype(F32)
         return total.astype(BF16)
 
+    def hop_last(i, k):
+        axis = ORDERS[i][2]
+        src = home(i, {axis: (at[axis] + k) % 4}, 0)
+        rows = pl.ds(*ATTN[i])
+        dst = t3[i].at[(k - 1,) + select(kept(NAMES, ORDERS[i][:2]), {}) + (rows,)]
+        send, recv = bemls.at[i, 0, k - 1], bemlr.at[i, 0, k - 1]
+        return remote(src, dst, send, recv, device(shifted(at, axis, k)))
+
     def half_start(part, items=FULL):
         for way in range(2):
             for i in items:
@@ -730,8 +762,12 @@
 
     def whole_on(part):
         for i in PARTS[part]:
-            for way in range(2):
-                whole(i, part, way).wait_recv()
+            if part:
+                for way in range(2):
+                    whole(i, part, way).wait_recv()
+            else:
+                for k in (1, 3, 2):
+                    hop_last(i, k).wait_recv()
             add_whole(i, part)
 
     for i in FULL:
@@ -741,10 +777,14 @@
                     for k in (1, 2, 3):
                         ring(i, part, phase, k)[0].wait_send()
     arrive_last(1)
-    lax.fori_loop(0, 4, feed_early, 0)
+    feed_early(0, 0)
+    pass_last(2)
+    for y in range(1, 4):
+        feed_early(y, 0)
     half_start(1)
     arrive_last(2)
-    lax.fori_loop(0, 4, feed_late, 0)
+    for y in range(4):
+        feed_late(y, 0)
     sum_o = remote(oacc.at[1 - at["c"]], osum, semps.at[2], sempr.at[2], sibling)
     sum_e = remote(eacc.at[1 - at["c"]], esum, semps.at[3], sempr.at[3], sibling)
     sum_e.start()
@@ -792,8 +832,8 @@
         for k in (2, 1, 3, 0):
             share(i, k).wait_recv()
             add_core(i, k)
-            if k == 2:
-                half_start(0, (i,))
+            if k:
+                hop_last(i, k).start()
 
     half_on(2)
     def third_back(h, carry):
@@ -811,13 +851,11 @@
     share_on(0)
     attend_back(1, 1)
     share_start(1)
-    half_on(0, (0,))
     attend_back(2, 0)
     share_on(1)
     attend_back(2, 1)
     share_start(2)
     whole_on(1)
-    half_on(0, (1,))
     share_on(2)
     whole_on(2)
     hop_start(1)
@@ -854,7 +892,6 @@
             grad_out(y).start()
 
         pl.when(y < at["y"])(add_across)
-    half_on(0, (2,))
     sum_o.wait()
     out_s[...] = (hid[...] + oacc[at["c"]] + osum[...]).astype(BF16)
 
@@ -879,10 +916,21 @@
         ],
         axis=0,
     )
-    mixed_units = jnp.concatenate([sum0[96:160], sum2[144:176]], axis=0)
+    mixed_units = jnp.concatenate([sum0[96:160], sum1[96:128]], axis=0)
     both = jnp.concatenate([sum0[0:96], sum1[0:96], mixed_units], axis=1)
     rows_mlp = nn(one_hot(96, 16, 6, 16, 0, True), both)
     d0b[...] = nn(one_hot(48, 2, 24, 32, 0, True), down).astype(BF16).reshape(2, 32, 384)
+    s0b[...] = rows_mlp.astype(BF16).reshape(2, 8, 16, 384)
+
+    def final(k):
+        return group(k, s0b, r0, bem0s, bem0r)
+
+    def final_down(slot):
+        return remote(d0b.at[1 - xl], rd0.at[slot], bemds, bemdr, beside)
+
+    for k in range(1, 16):
+        final(k)[0].start()
+    final_down(xl).start()
     hop_on(0)
 
     esum[...] += xa[here].astype(F32)
@@ -911,28 +959,32 @@
     pl.when(jnp.logical_not(stays))(lambda: in_move().start())
     pl.when(stays)(in_stay)
     attn = jnp.concatenate([last(i, 0) for i in range(3)], axis=1)
-    rows = rows_mlp + nn(one_hot(48, 16, 6, 16, at["c"] * 128 + 8, True), attn)
-    s0b[...] = rows.astype(BF16).reshape(2, 8, 16, 384)
-
-    def final(k):
-        return group(k, s0b, r0, bem0s, bem0r)
-
-    def final_down(slot):
-        return remote(d0b.at[1 - xl], rd0.at[slot], bemds, bemdr, beside)
-
-    for k in range(1, 16):
-        final(k)[0].start()
-    final_down(xl).start()
+    rows = nn(one_hot(48, 8, 6, 16, 0, True), attn)
+    sab[...] = rows.astype(BF16).reshape(8, 16, 384)
+
+    def final_attn(k):
+        to, frm = (s + k) % 8, (s - k + 8) % 8
+        out = remote(sab.at[to], rab.at[s], semas.at[k - 1], semar.at[k - 1], (f, to))
+        inn = remote(sab.at[to], rab.at[frm], semas.at[k - 1], semar.at[k - 1], (f, to))
+        return out, inn
+
+    for k in range(1, 8):
+        final_attn(k)[0].start()
+    rab[s] = sab[s]
     r0[at["c"] * 8 + s] = s0b[at["c"], s]
     rd0[xl] = d0b[xl]
     for k in range(1, 16):
         final(k)[1].wait_recv()
     final_down(1 - xl).wait_recv()
-
     rows_o[...] = r0[...]
     down_o[...] = rd0[...]
+    for k in range(1, 8):
+        final_attn(k)[1].wait_recv()
+    attn_o[...] = rab[...]
     for k in range(1, 16):
         final(k)[0].wait_send()
+    for k in range(1, 8):
+        final_attn(k)[0].wait_send()
     final_down(xl).wait_send()
     for y in range(3):
 
@@ -954,7 +1006,10 @@
         for k in range(4):
             across(i, k)[0].wait_send()
             share(i, k).wait_send()
-    for part in range(3):
+    for i in ATTN:
+        for k in (1, 2, 3):
+            hop_last(i, k).wait_send()
+    for part in (1, 2):
         for i in PARTS[part]:
             for way in range(2):
                 halfway(i, part, way).wait_send()
@@ -966,7 +1021,7 @@
                     hop(i, part, left, k).wait_send()
 
 
-def finish_kernel(gains, w_query, w_key, w_value, w_gate, w_up, rows_i, down_i, out_i, in_i,
+def finish_kernel(gains, w_query, w_key, w_value, w_gate, w_up, rows_i, down_i, attn_i, out_i, in_i,
                   out_o, in_o, ga1_o, gq_o, gk_o, gv_o, go_o, ga2_o, gg_o, gu_o, gd_o, s0):
     out_o[...] = out_i[...]
     in_o[...] = in_i[...]
@@ -984,13 +1039,12 @@
         return jnp.sum(jnp.where(lane == side, col, 0.0), axis=0, keepdims=True)
 
     gain_one, gain_two = gain_column(0), gain_column(1)
-    c = lax.axis_index("fsdp") % 2
     got = rows_i[...].reshape(2, 8, 16, 384)
     halves = [got[core, :, :8].reshape(64, 384) for core in range(2)]
     for which in range(2):
         natural = nn(halves[0], units(0, which == 1, True)) + nn(halves[1], units(1, which == 1, True))
         s0[which] = natural.reshape(8, 8, 384)
-    s0[2] = rows_i[pl.ds(c * 8, 8), 8:, :].astype(F32)
+    s0[2] = attn_i[:, 0:8, :].astype(F32)
     down = down_i[...].astype(F32)
     gain_sum_one = jnp.zeros((6, 1), F32)
     gain_sum_two = jnp.zeros((6, 1), F32)
@@ -1020,7 +1074,7 @@
 
 
 def layer(lens, gains, *arrays):
-    outs = [((128, 768), BF16), ((128, 768), F32), ((16, 16, 384), BF16), ((2, 32, 384), BF16)]
+    outs = [((128, 768), BF16), ((128, 768), F32), ((16, 16, 384), BF16), ((2, 32, 384), BF16), ((8, 16, 384), BF16)]
     sizes = tuple(SIZES[n] for n in NAMES)
     scratch = [(sizes + (2, 48, 128), BF16) for _ in ROWS] + [(sizes + (r - 48, 128), BF16) for r in ROWS]
     scratch += [(sizes + (2, 48, 128), BF16) for _ in ROWS]
@@ -1033,7 +1087,7 @@
         ((1024, 128), F32), ((1024, 128), F32), ((1024, 128), F32), ((4, 128, 768), BF16),
         ((2, 128, 768), BF16), ((2, 128, 768), BF16), ((2, 128, 768), F32), ((2, 128, 768), F32),
         ((128, 768), F32), ((128, 768), F32), ((4, 128, 768), BF16), ((128, 768), BF16), ((128, 768), BF16), ((128, 768), F32),
-        ((8, 128), F32), ((8, 128), F32),
+        ((8, 128), F32), ((8, 128), F32), ((8, 16, 384), BF16), ((8, 16, 384), BF16),
     ]
     for rings in (2, 1, 0):
         for i in range(3):
@@ -1044,7 +1098,7 @@
         DMA((3, 4, 3)), DMA((3, 4, 3)), DMA((3, 3, 4)), DMA((3, 3, 4)), DMA((3, 4)), DMA((3, 4)), DMA((4,)), DMA((4,)),
         DMA((15,)), DMA((15,)), DMA, DMA,
         DMA((3, 4, 3)), DMA((3, 4, 3)), DMA((3, 3, 4)), DMA((3, 3, 4)), DMA((3, 4)), DMA((3, 4)),
-        DMA((5,)), DMA((5,)), DMA((4,)), DMA((4,)), DMA((4,)), DMA((4,)), DMA((4,)), DMA((4,)),
+        DMA((5,)), DMA((5,)), DMA((4,)), DMA((4,)), DMA((4,)), DMA((4,)), DMA((4,)), DMA((4,)), DMA((7,)), DMA((7,)),
     ]
     return pl.pallas_call(
         layer_kernel,
@@ -1066,7 +1120,7 @@
     return pl.pallas_call(
         finish_kernel,
         out_shape=[jax.ShapeDtypeStruct(shape, kind) for shape, kind in outs],
-        in_specs=[SMEM_SPEC] + [VMEM_SPEC] * 9,
+        in_specs=[SMEM_SPEC] + [VMEM_SPEC] * 10,
         out_specs=[VMEM_SPEC] * len(outs),
         scratch_shapes=[pltpu.VMEM((3, 8, 8, 384), F32)],
         name="finish",
@@ -1075,10 +1129,10 @@
 
 def per_device(tokens, doc_lengths, attn_gain, w_query, w_key, w_value, w_out, mlp_gain, w_gate, w_up, w_down, cotangent):
     gains = jnp.stack([attn_gain, mlp_gain]).astype(F32)
-    layer_out, input_grad, rows, down = layer(
+    layer_out, input_grad, rows, down, rows_attn = layer(
         doc_lengths, gains, tokens[0], cotangent[0], w_query, w_key, w_value, w_out, w_gate, w_up, w_down
     )
-    out = finish(gains, w_query, w_key, w_value, w_gate, w_up, rows, down, layer_out, input_grad)
+    out = finish(gains, w_query, w_key, w_value, w_gate, w_up, rows, down, rows_attn, layer_out, input_grad)
     return (out[0][None], out[1][None], out[2][0]) + tuple(out[3:7]) + (out[7][0],) + tuple(out[8:])
 
 

time: 161 us -> 144 us (0.89)
  Pallas kernels: 159 us -> 142 us
    pallas_call x1, Pallas kernels: 157 us -> 139 us  [layer(): pl.pallas_call(layer_kernel, out_shape=[jax.ShapeDtypeStruct(shape, kind)...]
where the time goes in v5:
time: 144 us
  Pallas kernels  142 us (99%)
    pallas_call x1, Pallas kernels, layer(): pl.pallas_call(layer_kernel, out_shape=[jax.ShapeDtypeStruct(shape, kind)...  139 us

profile of v5, /device:TPU:1, one launch (start us, length us, event | category | flops | bytes accessed | tf_op | source)
XLA Modules:
  0.0 144.2 jit_solution(223960167446117671)
XLA Ops:
  0.6 0.0 copy-start
  0.7 0.0 copy-start.1
  0.7 0.6 copy-done
  1.3 0.0 copy-done.1
  1.3 0.6 maximum_convert_fusion.gains
  1.9 139.4 %layer.1 = (bf16[128,768]{1,0:T(8,128)(2,1)}, f32[128,768]{1,0:T(8,128)}, bf16[16,16,384]{2,1,0:T(8,128)(2,1)}, bf16[2,32,384]{2,1,0:T(8,128)(2,1)}, bf16[8,16,384]{2,1,0:T(8,128)(2,1)}) custom-call(s32[1,4]{1,0:T(1,128)} %lens.1, f32[2,6]{1,0:T(2,128)} %maximum_convert_fusion.gains, bf16[128,768]{1,0:T(8,128)(2,1)} %bitcast.8, bf16[128,768]{1,0:T(8,128)(2,1)} %bitcast.9, ...), custom_call_target="tpu_custom_call" | custom-call | tf_op jit(solution)/shard_map/layer/pallas_call | solution.py:1103
  141.4 2.7 %finish.1 = (bf16[128,768]{1,0:T(8,128)(2,1)}, f32[128,768]{1,0:T(8,128)}, f32[1,6]{1,0:T(1,128)}, f32[6,768]{1,0:T(8,128)}, f32[6,768]{1,0:T(8,128)}, /*index=5...) custom-call(f32[2,6]{1,0:T(2,128)} %maximum_convert_fusion.gains, ...), custom_call_target="tpu_custom_call" | custom-call | tf_op jit(solution)/shard_map/finish/pallas_call | solution.py:1120
Async XLA Ops:
  0.6 0.7 copy-start
  0.7 0.7 copy-start.1

commit v6 on v5

--- a/solution.py
+++ b/solution.py
@@ -20,11 +20,11 @@
 NAMES = ("y", "xl", "xh", "z")
 SIZES = {"y": 4, "xl": 2, "xh": 2, "z": 4, "c": 2}
 ORDERS = (("y", "z", "x"), ("z", "x", "y"), ("x", "y", "z"))
-ROWS = (208, 176, 192)
+ROWS = (208, 160, 208)
 FULL = (1, 0, 2)
 ATTN = {0: (0, 48), 1: (0, 48), 2: (0, 48)}
 EARLY = {0: (48, 96), 1: (48, 96), 2: (48, 96)}
-LATE = {0: (144, 64), 1: (144, 32), 2: (144, 48)}
+LATE = {0: (144, 64), 1: (144, 16), 2: (144, 64)}
 PARTS = (ATTN, EARLY, LATE)
 
 
@@ -102,6 +102,12 @@
     return ((i // 192 == core) & (j == jnp.where(r < 32, early, late))).astype(BF16)
 
 
+def as_column(row):
+    lane = lax.broadcasted_iota(jnp.int32, (6, 6), 1)
+    side = lax.broadcasted_iota(jnp.int32, (6, 6), 0)
+    return jnp.sum(jnp.where(lane == side, row.astype(F32), 0.0), axis=1, keepdims=True)
+
+
 def nn(a, b):
     return jnp.dot(a, b, preferred_element_type=F32)
 
@@ -153,7 +159,7 @@
 
 
 def layer_kernel(
-    lens, gains, tok, cot, w_query, w_key, w_value, w_out, w_gate, w_up, w_down,
+    lens, gain_a, gain_m, tok, cot, w_query, w_key, w_value, w_out, w_gate, w_up, w_down,
     out_o, in_o, rows_o, down_o, attn_o,
     a0, a1, a2, w0, w1, w2, g0, g1, g2, h0, h1, h2,
     xa, xat, r0, rd0, s0, d0, s0b, d0b, ks, vs, qs, ps, att, hid, dhid, dqs, cosine, sine, bias, rdn,
@@ -178,15 +184,7 @@
     xl = at["x"] % 2
     beside = (f, at["y"] * 2 + 1 - xl)
     bar, others = greeting(at)
-    row = lax.broadcasted_iota(jnp.int32, (6, 1), 0)
-
-    def gain_column(which):
-        col = jnp.zeros((6, 1), F32)
-        for r in range(6):
-            col = jnp.where(row == r, gains[which, r], col)
-        return col
-
-    gain_one, gain_two = gain_column(0), gain_column(1)
+    gain_one, gain_two = as_column(gain_a[...]), as_column(gain_m[...])
     for r in range(4):
         lens_out[r : r + 1] = jnp.full((1, 128), lens[0, r], jnp.int32).astype(F32)
     lens_out[4:8] = jnp.zeros((4, 128), F32)
@@ -257,10 +255,8 @@
     down_copy(xl).start()
 
     def move():
-        for n in (0, 2, 1):
+        for n in (0, 2):
             moves(n).start()
-        for n in range(3):
-            moves(n).wait()
 
     def stay():
         toks[...] = tok[...]
@@ -269,12 +265,6 @@
 
     pl.when(jnp.logical_not(stays))(move)
     pl.when(stays)(stay)
-    swap(cs, 0).start()
-    inputs = toks[...].astype(F32)
-    xa[here] = (inputs * norm_factor(inputs)).astype(BF16)
-    for y in range(1, 4):
-        pl.when(y > at["y"])(lambda y=y: token_out(y).start())
-    pl.when(at["c"] == 0)(lambda: token_across(at["y"])[0].start())
     r0[at["c"] * 8 + s] = s0b[at["c"], s]
     rd0[xl] = d0b[xl]
 
@@ -302,7 +292,8 @@
         axis = order[phase]
         fixed = {n: at[n] for n in ("x", "y", "z") if n not in order[:phase]}
         theirs = {**fixed, axis: (at[axis] - k + 4) % 4}
-        mine, other = block(i, fixed, at["c"], rest(i, part)), block(i, theirs, at["c"], rest(i, part))
+        rows = pl.ds(*PARTS[part][i])
+        mine, other = block(i, fixed, at["c"], rows), block(i, theirs, at["c"], rows)
         slot = 2 * part + phase
         send, recv = sems.at[i, slot, k - 1], semr.at[i, slot, k - 1]
         to = device(shifted(at, axis, k))
@@ -383,7 +374,8 @@
     put(0, 48, piece[:, :128])
     put(0, 144, piece[:64, 256:])
     put(1, 48, piece[:, 128:256])
-    put(1, 144, piece[64:, 256:])
+    put(1, 144, piece[64:80, 256:])
+    put(2, 192, piece[80:, 256:])
     down_copy(1 - xl).wait_recv()
     piece = nn(one_hot(48, 2, 24, 32, 0), rd0[...].reshape(64, 384)).astype(BF16)
     for b in range(3):
@@ -391,14 +383,31 @@
         put(2, 48 + 32 * b, piece[:32, lanes])
         put(2, 144 + 16 * b, piece[32:, lanes])
     start(1, 0)
+    start(2, 0)
+
+    def arrived():
+        for n in (0, 2):
+            moves(n).wait()
+        moves(1).start()
+
+    pl.when(jnp.logical_not(stays))(arrived)
+    inputs = toks[...].astype(F32)
+    xa[here] = (inputs * norm_factor(inputs)).astype(BF16)
+    for y in range(1, 4):
+        pl.when(y > at["y"])(lambda y=y: token_out(y).start())
+    pl.when(at["c"] == 0)(lambda: token_across(at["y"])[0].start())
     arrive(0, 0)
     start(0, 1)
+    arrive(1, 0)
+    start(1, 1)
     arrive(0, 1)
     start_last(0)
     for i in ATTN:
         across(i, 0)[0].start()
-    arrive(1, 0)
-    start(1, 1)
+    arrive(1, 1)
+    start_last(1)
+    arrive(2, 0)
+    start(2, 1)
 
     ends = [lens_in[0:1, :]]
     for r in (1, 2):
@@ -426,8 +435,7 @@
 
     lax.fori_loop(0, 8, table, 0)
 
-    arrive(1, 1)
-    start_last(1)
+
     for u in range(1, 8):
 
         def clear(u=u):
@@ -519,6 +527,8 @@
         lax.fori_loop(0, 2, attend_third, 0)
         if t == 0:
             pass_last(1)
+        if t == 1:
+            arrive(2, 1)
             start_last(2)
 
 
@@ -527,6 +537,8 @@
     factor_two = norm_factor(hidden)
     v2s[at["c"]] = (hidden * factor_two).astype(BF16)
     swap(v2s, 1).start()
+    pl.when(jnp.logical_not(stays))(lambda: moves(1).wait())
+    swap(cs, 0).start()
     oacc[...] = jnp.zeros_like(oacc)
     eacc[...] = jnp.zeros_like(eacc)
     swapped(cs, 0).wait()
@@ -584,8 +596,8 @@
 
     def feed_late(y, carry):
         def weight(b):
-            low_rows, high_rows = w0[y, b, :, :, 96:160], w1[y, b, :, :, 96:128]
-            return jnp.concatenate([low_rows, high_rows], axis=2).reshape(768, 128)
+            rows = (w0[y, b, :, :, 96:160], w1[y, b, :, :, 96:112], w2[y, b, :, :, 144:160])
+            return jnp.concatenate(rows, axis=2).reshape(768, 128)
 
         w = pair(weight(0), weight(1))
         xh, z = y // 2, (y % 2) * 2
@@ -604,7 +616,8 @@
         for b in range(2):
             rows = g[:, b * 128 : (b + 1) * 128].reshape(2, 4, 96, 128)
             h0[y, b, :, :, 144:208] = rows[:, :, :64]
-            h1[y, b, :, :, 144:176] = rows[:, :, 64:]
+            h1[y, b, :, :, 144:160] = rows[:, :, 64:80]
+            h2[y, b, :, :, 192:208] = rows[:, :, 80:]
         put_down(xh, z, 144, 16, g_d)
         return carry
 
@@ -771,11 +784,10 @@
             add_whole(i, part)
 
     for i in FULL:
-        for part in range(2):
-            if i in FULL:
-                for phase in range(2):
-                    for k in (1, 2, 3):
-                        ring(i, part, phase, k)[0].wait_send()
+        for part in range(3):
+            for phase in range(2):
+                for k in (1, 2, 3):
+                    ring(i, part, phase, k)[0].wait_send()
     arrive_last(1)
     feed_early(0, 0)
     pass_last(2)
@@ -840,7 +852,8 @@
         attend_back(0, h)
         return carry
 
-    lax.fori_loop(0, 2, third_back, 0)
+    attend_back(0, 0)
+    attend_back(0, 1)
 
     def share_start(i):
         for k in (2, 1, 3, 0):
@@ -916,7 +929,7 @@
         ],
         axis=0,
     )
-    mixed_units = jnp.concatenate([sum0[96:160], sum1[96:128]], axis=0)
+    mixed_units = jnp.concatenate([sum0[96:160], sum1[96:112], sum2[144:160]], axis=0)
     both = jnp.concatenate([sum0[0:96], sum1[0:96], mixed_units], axis=1)
     rows_mlp = nn(one_hot(96, 16, 6, 16, 0, True), both)
     d0b[...] = nn(one_hot(48, 2, 24, 32, 0, True), down).astype(BF16).reshape(2, 32, 384)
@@ -1021,24 +1034,16 @@
                     hop(i, part, left, k).wait_send()
 
 
-def finish_kernel(gains, w_query, w_key, w_value, w_gate, w_up, rows_i, down_i, attn_i, out_i, in_i,
+def finish_kernel(gain_a, gain_m, w_query, w_key, w_value, w_gate, w_up, rows_i, down_i, attn_i, out_i, in_i,
                   out_o, in_o, ga1_o, gq_o, gk_o, gv_o, go_o, ga2_o, gg_o, gu_o, gd_o, s0):
     out_o[...] = out_i[...]
     in_o[...] = in_i[...]
-    row = lax.broadcasted_iota(jnp.int32, (6, 1), 0)
-
-    def gain_column(which):
-        col = jnp.zeros((6, 1), F32)
-        for r in range(6):
-            col = jnp.where(row == r, gains[which, r], col)
-        return col
-
     def as_row(col):
         lane = lax.broadcasted_iota(jnp.int32, (6, 6), 1)
         side = lax.broadcasted_iota(jnp.int32, (6, 6), 0)
         return jnp.sum(jnp.where(lane == side, col, 0.0), axis=0, keepdims=True)
 
-    gain_one, gain_two = gain_column(0), gain_column(1)
+    gain_one, gain_two = as_column(gain_a[...]), as_column(gain_m[...])
     got = rows_i[...].reshape(2, 8, 16, 384)
     halves = [got[core, :, :8].reshape(64, 384) for core in range(2)]
     for which in range(2):
@@ -1073,7 +1078,7 @@
 DMA = pltpu.SemaphoreType.DMA
 
 
-def layer(lens, gains, *arrays):
+def layer(lens, *arrays):
     outs = [((128, 768), BF16), ((128, 768), F32), ((16, 16, 384), BF16), ((2, 32, 384), BF16), ((8, 16, 384), BF16)]
     sizes = tuple(SIZES[n] for n in NAMES)
     scratch = [(sizes + (2, 48, 128), BF16) for _ in ROWS] + [(sizes + (r - 48, 128), BF16) for r in ROWS]
@@ -1095,7 +1100,7 @@
             scratch.append(((3,) + left + (ROWS[i], 128), BF16))
     copies = [
         DMA((15,)), DMA((15,)), DMA, DMA, DMA((4,)), DMA((4,)),
-        DMA((3, 4, 3)), DMA((3, 4, 3)), DMA((3, 3, 4)), DMA((3, 3, 4)), DMA((3, 4)), DMA((3, 4)), DMA((4,)), DMA((4,)),
+        DMA((3, 6, 3)), DMA((3, 6, 3)), DMA((3, 3, 4)), DMA((3, 3, 4)), DMA((3, 4)), DMA((3, 4)), DMA((4,)), DMA((4,)),
         DMA((15,)), DMA((15,)), DMA, DMA,
         DMA((3, 4, 3)), DMA((3, 4, 3)), DMA((3, 3, 4)), DMA((3, 3, 4)), DMA((3, 4)), DMA((3, 4)),
         DMA((5,)), DMA((5,)), DMA((4,)), DMA((4,)), DMA((4,)), DMA((4,)), DMA((4,)), DMA((4,)), DMA((7,)), DMA((7,)),
@@ -1103,15 +1108,15 @@
     return pl.pallas_call(
         layer_kernel,
         out_shape=[jax.ShapeDtypeStruct(shape, kind) for shape, kind in outs],
-        in_specs=[SMEM_SPEC] * 2 + [VMEM_SPEC] * 9,
+        in_specs=[SMEM_SPEC] + [VMEM_SPEC] * 11,
         out_specs=[VMEM_SPEC] * len(outs),
         scratch_shapes=[pltpu.VMEM(shape, kind) for shape, kind in scratch] + copies,
         compiler_params=pltpu.CompilerParams(collective_id=0, has_side_effects=True, vmem_limit_bytes=VMEM_LIMIT),
         name="layer",
-    )(lens, gains, *arrays)
-
-
-def finish(gains, *arrays):
+    )(lens, *arrays)
+
+
+def finish(*arrays):
     outs = [
         ((128, 768), BF16), ((128, 768), F32), ((1, 6), F32),
         ((6, 768), F32), ((6, 768), F32), ((6, 768), F32), ((6, 768), F32),
@@ -1120,19 +1125,19 @@
     return pl.pallas_call(
         finish_kernel,
         out_shape=[jax.ShapeDtypeStruct(shape, kind) for shape, kind in outs],
-        in_specs=[SMEM_SPEC] + [VMEM_SPEC] * 10,
+        in_specs=[VMEM_SPEC] * 12,
         out_specs=[VMEM_SPEC] * len(outs),
         scratch_shapes=[pltpu.VMEM((3, 8, 8, 384), F32)],
         name="finish",
-    )(gains, *arrays)
+    )(*arrays)
 
 
 def per_device(tokens, doc_lengths, attn_gain, w_query, w_key, w_value, w_out, mlp_gain, w_gate, w_up, w_down, cotangent):
-    gains = jnp.stack([attn_gain, mlp_gain]).astype(F32)
+    gains = (attn_gain.reshape(1, 6), mlp_gain.reshape(1, 6))
     layer_out, input_grad, rows, down, rows_attn = layer(
-        doc_lengths, gains, tokens[0], cotangent[0], w_query, w_key, w_value, w_out, w_gate, w_up, w_down
+        doc_lengths, *gains, tokens[0], cotangent[0], w_query, w_key, w_value, w_out, w_gate, w_up, w_down
     )
-    out = finish(gains, w_query, w_key, w_value, w_gate, w_up, rows, down, rows_attn, layer_out, input_grad)
+    out = finish(*gains, w_query, w_key, w_value, w_gate, w_up, rows, down, rows_attn, layer_out, input_grad)
     return (out[0][None], out[1][None], out[2][0]) + tuple(out[3:7]) + (out[7][0],) + tuple(out[8:])
 
 

time: 144 us -> 138 us (0.958)
  Pallas kernels: 142 us -> 137 us
    pallas_call x1, Pallas kernels: 139 us -> 134 us  [layer(): pl.pallas_call(layer_kernel, out_shape=[jax.ShapeDtypeStruct(shape, kind)...]
where the time goes in v6:
time: 138 us; the launch traced here: 137 us
  Pallas kernels  137 us (99%)
    pallas_call x1, Pallas kernels, layer(): pl.pallas_call(layer_kernel, out_shape=[jax.ShapeDtypeStruct(shape, kind)...  134 us

profile of v6, /device:TPU:1, one launch (start us, length us, event | category | flops | bytes accessed | tf_op | source)
XLA Modules:
  0.0 137.3 jit_solution(17114141498044151343)
XLA Ops:
  0.6 133.8 %layer.1 = (bf16[128,768]{1,0:T(8,128)(2,1)}, f32[128,768]{1,0:T(8,128)}, bf16[16,16,384]{2,1,0:T(8,128)(2,1)}, bf16[2,32,384]{2,1,0:T(8,128)(2,1)}, bf16[8,16,384]{2,1,0:T(8,128)(2,1)}) custom-call(s32[1,4]{1,0:T(1,128)} %lens.1, bf16[1,6]{1,0:T(2,128)(2,1)} %bitcast.10, bf16[1,6]{1,0:T(2,128)(2,1)} %bitcast.12, bf16[128,768]{1,0:T(8,128)(2,1)} %bitcast.8, ...), custom_call_target="tpu_custom_call" | custom-call | tf_op jit(solution)/shard_map/layer/pallas_call | solution.py:1108
  134.4 2.7 %finish.1 = (bf16[128,768]{1,0:T(8,128)(2,1)}, f32[128,768]{1,0:T(8,128)}, f32[1,6]{1,0:T(1,128)}, f32[6,768]{1,0:T(8,128)}, f32[6,768]{1,0:T(8,128)}, /*index=5...) custom-call(bf16[1,6]{1,0:T(2,128)(2,1)} %bitcast.11, ...), custom_call_target="tpu_custom_call" | custom-call | tf_op jit(solution)/shard_map/finish/pallas_call | solution.py:1125

commit v7 on v6

--- a/solution.py
+++ b/solution.py
@@ -20,11 +20,11 @@
 NAMES = ("y", "xl", "xh", "z")
 SIZES = {"y": 4, "xl": 2, "xh": 2, "z": 4, "c": 2}
 ORDERS = (("y", "z", "x"), ("z", "x", "y"), ("x", "y", "z"))
-ROWS = (208, 160, 208)
+ROWS = (192, 192, 192)
 FULL = (1, 0, 2)
 ATTN = {0: (0, 48), 1: (0, 48), 2: (0, 48)}
 EARLY = {0: (48, 96), 1: (48, 96), 2: (48, 96)}
-LATE = {0: (144, 64), 1: (144, 16), 2: (144, 64)}
+LATE = {0: (144, 48), 1: (144, 48), 2: (144, 48)}
 PARTS = (ATTN, EARLY, LATE)
 
 
@@ -372,10 +372,9 @@
     start(0, 0)
     piece = nn(one_hot(96, 16, 6, 16, 0), flat).astype(BF16)
     put(0, 48, piece[:, :128])
-    put(0, 144, piece[:64, 256:])
+    put(0, 144, piece[:48, 256:])
     put(1, 48, piece[:, 128:256])
-    put(1, 144, piece[64:80, 256:])
-    put(2, 192, piece[80:, 256:])
+    put(1, 144, piece[48:96, 256:])
     down_copy(1 - xl).wait_recv()
     piece = nn(one_hot(48, 2, 24, 32, 0), rd0[...].reshape(64, 384)).astype(BF16)
     for b in range(3):
@@ -596,7 +595,7 @@
 
     def feed_late(y, carry):
         def weight(b):
-            rows = (w0[y, b, :, :, 96:160], w1[y, b, :, :, 96:112], w2[y, b, :, :, 144:160])
+            rows = (w0[y, b, :, :, 96:144], w1[y, b, :, :, 96:144])
             return jnp.concatenate(rows, axis=2).reshape(768, 128)
 
         w = pair(weight(0), weight(1))
@@ -615,9 +614,8 @@
         g = nn(v2t, d_both).astype(BF16)
         for b in range(2):
             rows = g[:, b * 128 : (b + 1) * 128].reshape(2, 4, 96, 128)
-            h0[y, b, :, :, 144:208] = rows[:, :, :64]
-            h1[y, b, :, :, 144:160] = rows[:, :, 64:80]
-            h2[y, b, :, :, 192:208] = rows[:, :, 80:]
+            h0[y, b, :, :, 144:192] = rows[:, :, :48]
+            h1[y, b, :, :, 144:192] = rows[:, :, 48:96]
         put_down(xh, z, 144, 16, g_d)
         return carry
 
@@ -929,7 +927,7 @@
         ],
         axis=0,
     )
-    mixed_units = jnp.concatenate([sum0[96:160], sum1[96:112], sum2[144:160]], axis=0)
+    mixed_units = jnp.concatenate([sum0[96:144], sum1[96:144]], axis=0)
     both = jnp.concatenate([sum0[0:96], sum1[0:96], mixed_units], axis=1)
     rows_mlp = nn(one_hot(96, 16, 6, 16, 0, True), both)
     d0b[...] = nn(one_hot(48, 2, 24, 32, 0, True), down).astype(BF16).reshape(2, 32, 384)

time: 138 us -> 135 us (0.978)
  Pallas kernels: 137 us -> 133 us
    pallas_call x1, Pallas kernels: 134 us -> 130 us  [layer(): pl.pallas_call(layer_kernel, out_shape=[jax.ShapeDtypeStruct(shape, kind)...]
where the time goes in v7:
time: 135 us; the launch traced here: 134 us
  Pallas kernels  133 us (99%)
    pallas_call x1, Pallas kernels, layer(): pl.pallas_call(layer_kernel, out_shape=[jax.ShapeDtypeStruct(shape, kind)...  130 us
    pallas_call x1, Pallas kernels, finish(): pl.pallas_call(finish_kernel, out_shape=[jax.ShapeDtypeStruct(shape, kind...  2.74 us

profile of v7, /device:TPU:1, one launch (start us, length us, event | category | flops | bytes accessed | tf_op | source)
XLA Modules:
  0.0 133.5 jit_solution(13002704202985509785)
XLA Ops:
  0.6 130.0 %layer.1 = (bf16[128,768]{1,0:T(8,128)(2,1)}, f32[128,768]{1,0:T(8,128)}, bf16[16,16,384]{2,1,0:T(8,128)(2,1)}, bf16[2,32,384]{2,1,0:T(8,128)(2,1)}, bf16[8,16,384]{2,1,0:T(8,128)(2,1)}) custom-call(s32[1,4]{1,0:T(1,128)} %lens.1, bf16[1,6]{1,0:T(2,128)(2,1)} %bitcast.10, bf16[1,6]{1,0:T(2,128)(2,1)} %bitcast.12, bf16[128,768]{1,0:T(8,128)(2,1)} %bitcast.8, ...), custom_call_target="tpu_custom_call" | custom-call | tf_op jit(solution)/shard_map/layer/pallas_call | solution.py:1106
  130.6 2.7 %finish.1 = (bf16[128,768]{1,0:T(8,128)(2,1)}, f32[128,768]{1,0:T(8,128)}, f32[1,6]{1,0:T(1,128)}, f32[6,768]{1,0:T(8,128)}, f32[6,768]{1,0:T(8,128)}, /*index=5...) custom-call(bf16[1,6]{1,0:T(2,128)(2,1)} %bitcast.11, ...), custom_call_target="tpu_custom_call" | custom-call | tf_op jit(solution)/shard_map/finish/pallas_call | solution.py:1123
